TPU v7x, 32 devices: a whole 2x2x4 slice. The times are simulated.
32 devices in a mesh: fsdp: 4 (over x, core), ctx: 2 (over y), tp: 4 (over z).
Axes of the slice: x: 2, y: 2, z: 4, core: 2. Of those that a mesh axis runs over, the one named last changes fastest.
Arguments:
- tokens: bfloat16 [8192, 1024], P(('fsdp', 'ctx')), may hold values from -6 to 6
- cotangent: bfloat16 [8192, 1024], P(('fsdp', 'ctx')), may hold values from -6 to 6
- routes: int32 [8192, 2], P(('fsdp', 'ctx')), may hold values from 0 to 7, all different within a row; in each aligned block of 1024 rows (0 to 1023, 1024 to 2047, ...) at most 320 rows name the same one
- buckets: int32 [4095], replicated, may hold values from 0 to 31
- attention_in: float32 [3, 1024, 1024], P(None, ('fsdp', 'ctx'), 'tp'), may hold values from -0.1875 to 0.1875
- attention_out: float32 [1024, 1024], P('tp', ('fsdp', 'ctx')), may hold values from -3.5 to 3.5
- router: float32 [1024, 8], P(('fsdp', 'ctx')), may hold values from -0.125 to 0.125
- gains: float32 [2, 1024], P(None, ('fsdp', 'ctx')), may hold values from 0.5 to 1.5
- bias_table: float32 [32, 16], P(('fsdp', 'ctx'), 'tp'), may hold values from -6 to 6
- expert_in: float32 [8, 1024, 2, 2816], P(('fsdp', 'ctx'), None, None, 'tp'), may hold values from -0.1875 to 0.1875
- expert_out: float32 [8, 2816, 1024], P(('fsdp', 'ctx'), 'tp'), may hold values from -0.21875 to 0.21875
- attention_in_left: float32 [2, 3, 4096, 128], P(None, None, ('fsdp', 'ctx', 'tp')), as said below
- attention_in_right: float32 [2, 3, 8192, 256], P(None, None, ('fsdp', 'ctx', 'tp')), as said below
- attention_out_left: float32 [2, 8192, 256], P(None, ('fsdp', 'ctx', 'tp')), as said below
- attention_out_right: float32 [2, 4096, 128], P(None, ('fsdp', 'ctx', 'tp')), as said below
- expert_in_left: float32 [2, 32768, 1024], P(None, ('fsdp', 'ctx', 'tp')), as said below
- expert_in_right: float32 [2, 45056, 1408], P(None, ('fsdp', 'ctx', 'tp')), as said below
- expert_out_left: float32 [2, 22528, 704], P(None, ('fsdp', 'ctx', 'tp')), as said below
- expert_out_right: float32 [2, 32768, 1024], P(None, ('fsdp', 'ctx', 'tp')), as said below
- router_moment: float32 [1024, 8], P(('fsdp', 'ctx')), may hold values from 262144 to 1048576
- gains_moment: float32 [2, 1024], P(None, ('fsdp', 'ctx')), may hold values from 16384 to 65536
- table_moment: float32 [32, 16], P(('fsdp', 'ctx'), 'tp'), may hold values from 5461 to 21844
Outputs:
- output: bfloat16 [8192, 1024], P(('fsdp', 'ctx'))
- tokens_grad: float32 [8192, 1024], P(('fsdp', 'ctx'))
- attention_in_grad: float32 [3, 1024, 1024], P(None, ('fsdp', 'ctx'), 'tp')
- attention_in_new: float32 [3, 1024, 1024], P(None, ('fsdp', 'ctx'), 'tp')
- attention_in_left_new: float32 [3, 4096, 128], P(None, ('fsdp', 'ctx', 'tp'))
- attention_in_right_new: float32 [3, 8192, 256], P(None, ('fsdp', 'ctx', 'tp'))
- attention_out_grad: float32 [1024, 1024], P('tp', ('fsdp', 'ctx'))
- attention_out_new: float32 [1024, 1024], P('tp', ('fsdp', 'ctx'))
- attention_out_left_new: float32 [8192, 256], P(('fsdp', 'ctx', 'tp'))
- attention_out_right_new: float32 [4096, 128], P(('fsdp', 'ctx', 'tp'))
- expert_in_grad: float32 [8, 1024, 2, 2816], P(('fsdp', 'ctx'), None, None, 'tp')
- expert_in_new: float32 [8, 1024, 2, 2816], P(('fsdp', 'ctx'), None, None, 'tp')
- expert_in_left_new: float32 [32768, 1024], P(('fsdp', 'ctx', 'tp'))
- expert_in_right_new: float32 [45056, 1408], P(('fsdp', 'ctx', 'tp'))
- expert_out_grad: float32 [8, 2816, 1024], P(('fsdp', 'ctx'), 'tp')
- expert_out_new: float32 [8, 2816, 1024], P(('fsdp', 'ctx'), 'tp')
- expert_out_left_new: float32 [22528, 704], P(('fsdp', 'ctx', 'tp'))
- expert_out_right_new: float32 [32768, 1024], P(('fsdp', 'ctx', 'tp'))
- router_grad: float32 [1024, 8], P(('fsdp', 'ctx'))
- router_moment_new: float32 [1024, 8], P(('fsdp', 'ctx'))
- router_new: float32 [1024, 8], P(('fsdp', 'ctx'))
- gains_grad: float32 [2, 1024], P(None, ('fsdp', 'ctx'))
- gains_moment_new: float32 [2, 1024], P(None, ('fsdp', 'ctx'))
- gains_new: float32 [2, 1024], P(None, ('fsdp', 'ctx'))
- table_grad: float32 [32, 16], P(('fsdp', 'ctx'), 'tp')
- table_moment_new: float32 [32, 16], P(('fsdp', 'ctx'), 'tp')
- table_new: float32 [32, 16], P(('fsdp', 'ctx'), 'tp')
Inputs may be any that keep to these rules, and one draw needn't show every extreme that they name: `routes`: in the rows of one device the two experts of a row differ, no expert is named by more than 320 rows, a bound that some block reaches. `attention_in_left`: index 0 of the first dimension holds each block's symmetric statistic with a positive diagonal, index 1 its given symmetric inverse root. `attention_in_right`: as for attention_in_left. `attention_out_left`: as for attention_in_left. `attention_out_right`: as for attention_in_left. `expert_in_left`: as for attention_in_left. `expert_in_right`: as for attention_in_left. `expert_out_left`: as for attention_in_left. `expert_out_right`: as for attention_in_left.
All inputs are finite; a program needn't handle non-finite values.
Results may differ from a plain program's by a relative error of at most 0.034.
Values may be sent and summed in bfloat16 or wider, within the bound.
A program may use at most 832 MiB of HBM per device.

v0:
```python
import jax
import jax.numpy as jnp
from jax import lax
from jax.sharding import PartitionSpec as P

DH = 64
TOPK = 2


highest = lax.Precision.HIGHEST
norm_epsilon = 1e-06
step_epsilon = 1e-06
moment_epsilon = 1e-08
clip_level = 4.0
decay = 0.5
matrix_rate = 0.3
gain_rate = 0.25
router_rate = 0.01
table_rate = 0.3


def normalize(values, gain):
    return values * lax.rsqrt(jnp.mean(values * values, -1, keepdims=True) + norm_epsilon) * gain


def gated_gelu(both):
    return jax.nn.gelu(both[..., 0, :], approximate=True) * both[..., 1, :]


def precondition(grad, master, left, right):
    new_left = decay * left[0] + (1.0 - decay) * jnp.dot(grad, grad.T, precision=highest)
    new_right = decay * right[0] + (1.0 - decay) * jnp.dot(grad.T, grad, precision=highest)
    direction = jnp.dot(jnp.dot(left[1], grad, precision=highest), right[1], precision=highest)
    size = jnp.sqrt(jnp.mean(master * master) + step_epsilon)
    step = (
        matrix_rate * size * direction * lax.rsqrt(jnp.mean(direction * direction) + step_epsilon)
    )
    return (new_left, new_right, master - step)


def adapt(grad, moment, master, rate):
    new_moment = decay * moment + (1.0 - decay) * grad * grad
    return (new_moment, master - rate * grad * lax.rsqrt(new_moment + moment_epsilon))


def bias_block(table_rows, position, block, key_count):
    heads = table_rows.shape[0]
    width = key_count + block
    segment = lax.dynamic_slice_in_dim(table_rows, position, width, 1)
    tiled = jnp.broadcast_to(segment[:, None, :], (heads, block, width)).reshape(
        heads, block * width
    )
    tiled = tiled[:, : block * (width - 1)].reshape(heads, block, width - 1)
    return tiled[:, :, block - 1 : block - 1 + key_count]


def diagonal_sums(grid, block, key_count):
    heads = grid.shape[0]
    padded = jnp.pad(grid, ((0, 0), (0, 0), (block, 0))).reshape(heads, block * (key_count + block))
    padded = jnp.pad(padded, ((0, 0), (0, block))).reshape(heads, block, key_count + block + 1)
    return jnp.sum(padded, 1)[:, 1 : key_count + block]


def crossing(values):
    return lax.all_to_all(values, ("fsdp", "ctx"), split_axis=0, concat_axis=0, tiled=True)


def row_sum(values):
    return lax.psum(values, "tp")


def head_sum(values):
    return lax.psum(values, "tp")


def on_device(
    tokens,
    cotangent,
    routes,
    buckets,
    attention_in,
    attention_out,
    router,
    gains,
    bias_table,
    expert_in,
    expert_out,
    attention_in_left,
    attention_in_right,
    attention_out_left,
    attention_out_right,
    expert_in_left,
    expert_in_right,
    expert_out_left,
    expert_out_right,
    router_moment,
    gains_moment,
    table_moment,
):
    rows = tokens.shape[0]
    width = tokens.shape[1]
    length = rows * lax.axis_size("ctx")
    head_cols = attention_in.shape[2]
    local_heads = head_cols // DH
    experts = router.shape[1]
    capacity = rows * TOPK * 5 // (4 * experts)
    block = min(512, rows)
    blocks = rows // block
    scale = DH ** (-0.5)
    offset = lax.axis_index("ctx") * rows
    entry_full, exit_full, router_full, gains_full, table_full = (
        lax.all_gather(attention_in.astype(jnp.bfloat16), ("fsdp", "ctx"), axis=1, tiled=True),
        lax.all_gather(attention_out.astype(jnp.bfloat16), ("fsdp", "ctx"), axis=1, tiled=True),
        lax.all_gather(router.astype(jnp.bfloat16), ("fsdp", "ctx"), axis=0, tiled=True),
        lax.all_gather(gains.astype(jnp.bfloat16), ("fsdp", "ctx"), axis=1, tiled=True),
        lax.all_gather(bias_table.astype(jnp.bfloat16), ("fsdp", "ctx"), axis=0, tiled=True),
    )
    gain_first = gains_full[0].astype(jnp.float32)
    gain_second = gains_full[1].astype(jnp.float32)
    expand_in = expert_in[0].astype(jnp.bfloat16)
    expand_out = expert_out[0].astype(jnp.bfloat16)
    inputs = tokens.astype(jnp.float32)
    first = normalize(inputs, gain_first).astype(jnp.bfloat16)
    projected = jnp.einsum(
        "sd,kde->kse", first, entry_full, preferred_element_type=jnp.float32
    ).astype(jnp.bfloat16)
    query = projected[0]
    pairs = lax.all_gather(projected[1:], "ctx", axis=1, tiled=True)
    key_heads = pairs[0].reshape(length, local_heads, DH)
    value_heads = pairs[1].reshape(length, local_heads, DH)
    hits = (buckets[:, None] == jnp.arange(table_full.shape[0], dtype=jnp.int32)[None, :]).astype(
        jnp.float32
    )
    table_rows = jnp.dot(hits, table_full.astype(jnp.float32), precision=highest).T
    table_rows = jnp.concatenate([table_rows, jnp.zeros((local_heads, 1), jnp.float32)], 1)
    table_width = table_rows.shape[1]

    def position_of(start):
        return length - block - start

    query_blocks = query.reshape(blocks, block, local_heads, DH)
    starts = offset + jnp.arange(blocks, dtype=jnp.int32) * block

    def forward_block(items):
        block_query, start = items
        logit = (
            jnp.einsum("qhd,khd->hqk", block_query, key_heads, preferred_element_type=jnp.float32)
            * scale
        )
        scores = logit + bias_block(table_rows, position_of(start), block, length)
        top = jnp.max(scores, -1, keepdims=True)
        powers = jnp.exp(scores - top)
        total = jnp.sum(powers, -1, keepdims=True)
        shares = (powers / total).astype(jnp.bfloat16)
        mixed_block = jnp.einsum(
            "hqk,khd->qhd", shares, value_heads, preferred_element_type=jnp.float32
        )
        return (mixed_block, top[..., 0] + jnp.log(total[..., 0]), jnp.max(logit, axis=(1, 2)))

    mixed, log_total, peaks = lax.map(forward_block, (query_blocks, starts))
    mixed = mixed.reshape(rows, head_cols).astype(jnp.bfloat16)
    peaks = lax.pmax(jnp.max(peaks, 0), ("fsdp", "ctx"))
    partial_value = jnp.dot(mixed, exit_full, preferred_element_type=jnp.float32)
    middle = inputs + head_sum(partial_value)
    second = normalize(middle, gain_second).astype(jnp.bfloat16)
    logits = jnp.dot(second, router_full, preferred_element_type=jnp.float32)
    picked = jnp.take_along_axis(logits, routes, 1)
    top = jnp.max(picked, -1, keepdims=True)
    powers = jnp.exp(picked - top)
    weights_gate = powers / jnp.sum(powers, -1, keepdims=True)
    chosen = routes.reshape(-1)
    route_hits = (chosen[:, None] == jnp.arange(experts, dtype=jnp.int32)[None, :]).astype(
        jnp.int32
    )
    slots = jnp.sum(route_hits * (jnp.cumsum(route_hits, 0) - 1), 1)
    slot_rows = chosen * capacity + slots
    buffer = (
        jnp.zeros((experts * capacity, width), jnp.bfloat16)
        .at[slot_rows]
        .set(jnp.repeat(second, TOPK, axis=0))
        .reshape(experts, capacity, width)
    )
    arrived = crossing(buffer)
    mixed_up = jnp.einsum("scd,dgf->scgf", arrived, expand_in, preferred_element_type=jnp.float32)
    hidden = gated_gelu(mixed_up).astype(jnp.bfloat16)
    expert_part = jnp.einsum("scf,fd->scd", hidden, expand_out, preferred_element_type=jnp.float32)
    returned = crossing(row_sum(expert_part).astype(jnp.bfloat16))
    outputs_rows = (
        returned.reshape(experts * capacity, width)[slot_rows]
        .reshape(rows, TOPK, width)
        .astype(jnp.float32)
    )
    result = middle + jnp.sum(weights_gate[..., None] * outputs_rows, 1)
    grad_result = cotangent.astype(jnp.float32)
    grad_gate = jnp.sum(grad_result[:, None, :] * outputs_rows, -1)
    grad_rows = (
        (weights_gate[..., None] * grad_result[:, None, :])
        .astype(jnp.bfloat16)
        .reshape(rows * TOPK, width)
    )
    grad_buffer = (
        jnp.zeros((experts * capacity, width), jnp.bfloat16)
        .at[slot_rows]
        .set(grad_rows)
        .reshape(experts, capacity, width)
    )
    grad_arrived = crossing(grad_buffer)
    grad_hidden = jnp.einsum(
        "scd,fd->scf", grad_arrived, expand_out, preferred_element_type=jnp.float32
    )
    grad_expand_out = jnp.einsum(
        "scf,scd->fd", hidden, grad_arrived, preferred_element_type=jnp.float32
    )
    unused, pull = jax.vjp(gated_gelu, mixed_up)
    grad_mixed_up = pull(grad_hidden)[0].astype(jnp.bfloat16)
    grad_expand_in = jnp.einsum(
        "scd,scgf->dgf", arrived, grad_mixed_up, preferred_element_type=jnp.float32
    )
    grad_part = jnp.einsum(
        "scgf,dgf->scd", grad_mixed_up, expand_in, preferred_element_type=jnp.float32
    )
    grad_back = crossing(row_sum(grad_part).astype(jnp.bfloat16))
    grad_second = jnp.sum(
        grad_back.reshape(experts * capacity, width)[slot_rows]
        .reshape(rows, TOPK, width)
        .astype(jnp.float32),
        1,
    )
    grad_picked = weights_gate * (grad_gate - jnp.sum(weights_gate * grad_gate, -1, keepdims=True))
    route_match = (
        routes[:, :, None] == jnp.arange(experts, dtype=jnp.int32)[None, None, :]
    ).astype(jnp.float32)
    grad_logits = jnp.sum(grad_picked[..., None] * route_match, 1).astype(jnp.bfloat16)
    grad_second = grad_second + jnp.einsum(
        "se,de->sd", grad_logits, router_full, preferred_element_type=jnp.float32
    )
    grad_router = jnp.einsum("sd,se->de", second, grad_logits, preferred_element_type=jnp.float32)
    unused, pull = jax.vjp(normalize, middle, gain_second)
    grad_middle_norm, grad_gain_second = pull(grad_second)
    grad_middle = grad_result + grad_middle_norm
    grad_attention = grad_middle.astype(jnp.bfloat16)
    grad_mixed = jnp.einsum(
        "sd,ed->se", grad_attention, exit_full, preferred_element_type=jnp.float32
    ).astype(jnp.bfloat16)
    grad_exit = jnp.einsum("se,sd->ed", mixed, grad_attention, preferred_element_type=jnp.float32)
    grad_blocks = grad_mixed.reshape(blocks, block, local_heads, DH)

    def backward_block(carry, items):
        key_grad, value_grad, table_line = carry
        block_query, block_grad, start, log_block = items
        position = position_of(start)
        logit = (
            jnp.einsum("qhd,khd->hqk", block_query, key_heads, preferred_element_type=jnp.float32)
            * scale
        )
        shares = jnp.exp(
            logit + bias_block(table_rows, position, block, length) - log_block[..., None]
        )
        grad_shares = jnp.einsum(
            "qhd,khd->hqk", block_grad, value_heads, preferred_element_type=jnp.float32
        )
        grad_scores = (
            shares * (grad_shares - jnp.sum(shares * grad_shares, -1, keepdims=True))
        ).astype(jnp.bfloat16)
        value_grad = value_grad + jnp.einsum(
            "hqk,qhd->khd",
            shares.astype(jnp.bfloat16),
            block_grad,
            preferred_element_type=jnp.float32,
        )
        key_grad = (
            key_grad
            + jnp.einsum(
                "hqk,qhd->khd", grad_scores, block_query, preferred_element_type=jnp.float32
            )
            * scale
        )
        grad_query = (
            jnp.einsum("hqk,khd->qhd", grad_scores, key_heads, preferred_element_type=jnp.float32)
            * scale
        )
        sums = diagonal_sums(grad_scores.astype(jnp.float32), block, length)
        window = lax.dynamic_slice_in_dim(table_line, position, length + block - 1, 1)
        table_line = lax.dynamic_update_slice_in_dim(table_line, window + sums, position, 1)
        return ((key_grad, value_grad, table_line), grad_query)

    start_carry = (
        jnp.zeros((length, local_heads, DH), jnp.float32),
        jnp.zeros((length, local_heads, DH), jnp.float32),
        jnp.zeros((local_heads, table_width), jnp.float32),
    )
    (key_grad, value_grad, table_line), grad_query = lax.scan(
        backward_block, start_carry, (query_blocks, grad_blocks, starts, log_total)
    )
    pair_terms = jnp.stack([key_grad, value_grad]).reshape(2, length, head_cols)
    pair_grad = lax.psum_scatter(pair_terms, "ctx", scatter_dimension=1, tiled=True)
    grad_projected = jnp.concatenate([grad_query.reshape(1, rows, head_cols), pair_grad], 0).astype(
        jnp.bfloat16
    )
    table_grad = jnp.dot(hits.T, table_line[:, : table_width - 1].T, precision=highest)
    grad_entry = jnp.einsum(
        "sd,kse->kde", first, grad_projected, preferred_element_type=jnp.float32
    )
    grad_first_part = jnp.einsum(
        "kse,kde->sd", grad_projected, entry_full, preferred_element_type=jnp.float32
    )
    grad_first = head_sum(grad_first_part)
    unused, pull = jax.vjp(normalize, inputs, gain_first)
    grad_inputs, grad_gain_first = pull(grad_first)
    grad_tokens = grad_middle + grad_inputs
    owned_in, owned_out, owned_router, owned_gains, owned_table = (
        lax.psum_scatter(grad_entry, ("fsdp", "ctx"), scatter_dimension=1, tiled=True),
        lax.psum_scatter(grad_exit, ("fsdp", "ctx"), scatter_dimension=1, tiled=True),
        lax.psum_scatter(grad_router, ("fsdp", "ctx"), scatter_dimension=0, tiled=True),
        lax.psum_scatter(
            jnp.stack([grad_gain_first, grad_gain_second]),
            ("fsdp", "ctx"),
            scatter_dimension=1,
            tiled=True,
        ),
        lax.psum_scatter(table_grad, ("fsdp", "ctx"), scatter_dimension=0, tiled=True),
    )
    in_left, in_right, in_new = jax.vmap(precondition)(
        owned_in,
        attention_in,
        jnp.swapaxes(attention_in_left, 0, 1),
        jnp.swapaxes(attention_in_right, 0, 1),
    )
    column = jnp.sqrt(jnp.repeat(clip_level / jnp.maximum(peaks, clip_level), DH))
    in_new = in_new * jnp.stack([column, column, jnp.ones_like(column)])[:, None, :]
    out_left, out_right, out_new = precondition(
        owned_out, attention_out, attention_out_left, attention_out_right
    )
    expand_left, expand_right, expand_new = precondition(
        grad_expand_in.reshape(width, -1),
        expert_in.reshape(width, -1),
        expert_in_left,
        expert_in_right,
    )
    shrink_left, shrink_right, shrink_new = precondition(
        grad_expand_out, expert_out[0], expert_out_left, expert_out_right
    )
    router_moment_new, router_new = adapt(owned_router, router_moment, router, router_rate)
    gains_moment_new, gains_new = adapt(owned_gains, gains_moment, gains, gain_rate)
    table_moment_new, table_new = adapt(owned_table, table_moment, bias_table, table_rate)
    return (
        result.astype(jnp.bfloat16),
        grad_tokens,
        owned_in,
        in_new,
        in_left,
        in_right,
        owned_out,
        out_new,
        out_left,
        out_right,
        grad_expand_in[None],
        expand_new.reshape(expert_in.shape),
        expand_left,
        expand_right,
        grad_expand_out[None],
        shrink_new[None],
        shrink_left,
        shrink_right,
        owned_router,
        router_moment_new,
        router_new,
        owned_gains,
        gains_moment_new,
        gains_new,
        owned_table,
        table_moment_new,
        table_new,
    )


def solution(mesh):
    placed = (
        P(("fsdp", "ctx"), None),
        P(("fsdp", "ctx"), None),
        P(("fsdp", "ctx"), None),
        P(),
        P(None, ("fsdp", "ctx"), "tp"),
        P("tp", ("fsdp", "ctx")),
        P(("fsdp", "ctx"), None),
        P(None, ("fsdp", "ctx")),
        P(("fsdp", "ctx"), "tp"),
        P(("fsdp", "ctx"), None, None, "tp"),
        P(("fsdp", "ctx"), "tp", None),
        P(None, None, ("fsdp", "ctx", "tp"), None),
        P(None, None, ("fsdp", "ctx", "tp"), None),
        P(None, ("fsdp", "ctx", "tp"), None),
        P(None, ("fsdp", "ctx", "tp"), None),
        P(None, ("fsdp", "ctx", "tp"), None),
        P(None, ("fsdp", "ctx", "tp"), None),
        P(None, ("fsdp", "ctx", "tp"), None),
        P(None, ("fsdp", "ctx", "tp"), None),
        P(("fsdp", "ctx"), None),
        P(None, ("fsdp", "ctx")),
        P(("fsdp", "ctx"), "tp"),
    )
    return jax.shard_map(
        on_device,
        mesh=mesh,
        in_specs=placed,
        out_specs=(
            P(("fsdp", "ctx"), None),
            P(("fsdp", "ctx"), None),
            P(None, ("fsdp", "ctx"), "tp"),
            P(None, ("fsdp", "ctx"), "tp"),
            P(None, ("fsdp", "ctx", "tp"), None),
            P(None, ("fsdp", "ctx", "tp"), None),
            P("tp", ("fsdp", "ctx")),
            P("tp", ("fsdp", "ctx")),
            P(("fsdp", "ctx", "tp"), None),
            P(("fsdp", "ctx", "tp"), None),
            P(("fsdp", "ctx"), None, None, "tp"),
            P(("fsdp", "ctx"), None, None, "tp"),
            P(("fsdp", "ctx", "tp"), None),
            P(("fsdp", "ctx", "tp"), None),
            P(("fsdp", "ctx"), "tp", None),
            P(("fsdp", "ctx"), "tp", None),
            P(("fsdp", "ctx", "tp"), None),
            P(("fsdp", "ctx", "tp"), None),
            P(("fsdp", "ctx"), None),
            P(("fsdp", "ctx"), None),
            P(("fsdp", "ctx"), None),
            P(None, ("fsdp", "ctx")),
            P(None, ("fsdp", "ctx")),
            P(None, ("fsdp", "ctx")),
            P(("fsdp", "ctx"), "tp"),
            P(("fsdp", "ctx"), "tp"),
            P(("fsdp", "ctx"), "tp"),
        ),
        check_vma=False,
    )
```

profile of v0, /device:TPU:0, one launch (start us, length us, event | category | flops | bytes accessed | tf_op | source)
XLA Modules:
  0.0 2814.0 jit_solution(12611620345506766938)
XLA Ops:
  88.3 359.4 %while.35 = (s32[]{:T(128)}, bf16[2,512,4,64]{1,3,2,0:T(8,128)(2,1)}, f32[2,4,512]{2,1,0:T(4,128)}, f32[2,4]{1,0:T(2,128)S(1)}, bf16[2,512,4,64]{1,3,2,0:T(8,128...) while((s32[]{:T(128)}, ...), condition=%wide.region_5.6_spmd, body=%wide.region_1.5_spmd.sunk | while | flops 1128265728 | bytes 359670080 | solution.py:160
  133.7 59.0 %reshape.470 = f32[5240832]{0:T(1024)} reshape(f32[4,1310208]{1,0:T(4,128)} %slice.266) | data formatting | bytes 41926656 | tf_op jit(solution)/shard_map/while
  192.7 29.8 %reshape.471 = f32[4,512,2559]{2,1,0:T(8,128)} reshape(f32[5240832]{0:T(1024)} %reshape.470) | data formatting | bytes 41926656 | tf_op jit(solution)/shard_map/while/body/eval_jaxpr/reshape | solution.py:53
  309.0 59.1 %reshape.470 = f32[5240832]{0:T(1024)} reshape(f32[4,1310208]{1,0:T(4,128)} %slice.266) | data formatting | bytes 41926656 | tf_op jit(solution)/shard_map/while
  368.1 30.0 %reshape.471 = f32[4,512,2559]{2,1,0:T(8,128)} reshape(f32[5240832]{0:T(1024)} %reshape.470) | data formatting | bytes 41926656 | tf_op jit(solution)/shard_map/while/body/eval_jaxpr/reshape | solution.py:53
  458.8 151.9 %all-reduce.11.cloned.1.call-done = f32[1024,1024]{1,0:T(8,128)} async-done(((f32[1024,1024]{1,0:T(8,128)}), f32[1024,1024]{1,0:T(8,128)}) %all-reduce.11.cloned.1.call-update) | async-done | bytes 4194320 | tf_op jit(solution)/shard_map/psum | solution.py:73
  664.3 51.2 %all_gather.23 = bf16[1024,8]{0,1:T(8,128)(2,1)S(1)} all-gather(bf16[128,8]{0,1:T(8,128)(2,1)S(1)} %convert_element_type.154), channel_id=1, replica_groups=mesh['fsdp'=4,'ctx'=2,'tp'=4] {'fsdp','ctx'}, dimensions={0}, use_global_device_ids=true | all-gather | bytes 18432 | tf_op jit(solution)/shard_map/all_gather | solution.py:114
  776.2 34.0 %all-to-all-done.2 = bf16[8,320,1024]{2,1,0:T(8,128)(2,1)} async-done(((bf16[8,320,1024]{2,1,0:T(8,128)(2,1)}), bf16[8,320,1024]{2,1,0:T(8,128)(2,1)}, u32[]{:S(2)}, u32[]{:S(2)}) %all-to-all-start.2) | async-done | bytes 5242912 | tf_op jit(solution)/shard_map/all_to_all | solution.py:65
  845.1 696.9 %all-reduce.14 = (bf16[8,320,1024]{2,1,0:T(8,128)(2,1)}, bf16[8,320,1024]{2,1,0:T(8,128)(2,1)}) all-reduce(f32[8,320,1024]{2,1,0:T(8,128)} %fusion.85, f32[8,320,1024]{2,1,0:T(8,128)} %convolution_bitcast_fusion.1), channel_id=1, replica_groups=mesh['fsdp'=4,'ctx'=2,'tp'=4] {'tp'}, use_global_device_ids=true, to_apply=%region_14.15 | all-reduce | flops 5242880 | bytes 31457280 | tf_op jit(solution)/shard_map/psum | solution.py:69
  1542.0 66.8 %all_to_all.20 = bf16[8,320,1024]{2,1,0:T(8,128)(2,1)} all-to-all(bf16[8,320,1024]{2,1,0:T(8,128)(2,1)} %get-tuple-element.679), channel_id=1, replica_groups=mesh['fsdp'=4,'ctx'=2,'tp'=4] {'fsdp','ctx'}, dimensions={0} | all-to-all | bytes 10485760 | tf_op jit(solution)/shard_map/all_to_all | solution.py:65
  1630.4 42.6 %all-to-all-done.3 = bf16[8,320,1024]{2,1,0:T(8,128)(2,1)} async-done(((bf16[8,320,1024]{2,1,0:T(8,128)(2,1)}), bf16[8,320,1024]{2,1,0:T(8,128)(2,1)}, u32[]{:S(2)}, u32[]{:S(2)}) %all-to-all-start.3) | async-done | bytes 5242912 | tf_op jit(solution)/shard_map/all_to_all | solution.py:65
  1754.5 639.7 %while.36 = (s32[]{:T(128)}, f32[2048,4,64]{0,2,1:T(8,128)}, f32[2048,4,64]{0,2,1:T(8,128)}, f32[4,4096]{1,0:T(4,128)}, bf16[2,512,4,64]{1,3,2,0:T(8,128)(2,1)},...) while((s32[]{:T(128)}, f32[2048,4,64]{0,2,1:T(8,128)}, ...), condition=%wide.region_26.27_spmd.clone, body=%wide.region_23.26_spmd.clone.sunk | while | flops 2735343616 | bytes 626409728 | solution.py:292
  1807.4 59.3 %reshape.473 = f32[5240832]{0:T(1024)} reshape(f32[4,1310208]{1,0:T(4,128)} %slice.268) | data formatting | bytes 41926656 | tf_op jit(solution)/shard_map/while
  1866.7 29.7 %reshape.474 = f32[4,512,2559]{2,1,0:T(8,128)} reshape(f32[5240832]{0:T(1024)} %reshape.473) | data formatting | bytes 41926656 | tf_op jit(solution)/shard_map/while/body/eval_jaxpr/reshape | solution.py:53
  1969.5 58.8 %reshape.475 = f32[5244928]{0:T(1024)} reshape(f32[4,1311232]{1,0:T(4,128)} %pad_convert_fusion.2) | data formatting | bytes 41959424 | tf_op jit(solution)/shard_map/while
  2028.3 31.7 %reshape.476 = f32[4,512,2561]{2,1,0:T(8,128)} reshape(f32[5244928]{0:T(1024)} %reshape.475) | data formatting | bytes 41959424 | tf_op jit(solution)/shard_map/while/body/eval_jaxpr/reshape | solution.py:60
  2122.5 59.4 %reshape.473 = f32[5240832]{0:T(1024)} reshape(f32[4,1310208]{1,0:T(4,128)} %slice.268) | data formatting | bytes 41926656 | tf_op jit(solution)/shard_map/while
  2181.8 29.9 %reshape.474 = f32[4,512,2559]{2,1,0:T(8,128)} reshape(f32[5240832]{0:T(1024)} %reshape.473) | data formatting | bytes 41926656 | tf_op jit(solution)/shard_map/while/body/eval_jaxpr/reshape | solution.py:53
  2289.1 58.9 %reshape.475 = f32[5244928]{0:T(1024)} reshape(f32[4,1311232]{1,0:T(4,128)} %pad_convert_fusion.2) | data formatting | bytes 41959424 | tf_op jit(solution)/shard_map/while
  2347.9 31.9 %reshape.476 = f32[4,512,2561]{2,1,0:T(8,128)} reshape(f32[5244928]{0:T(1024)} %reshape.475) | data formatting | bytes 41959424 | tf_op jit(solution)/shard_map/while/body/eval_jaxpr/reshape | solution.py:60
  2478.8 36.6 %multiply_reduce_fusion.4 = (f32[]{:T(128)}, f32[1024,1408]{1,0:T(8,128)}) fusion(f32[1408,1024]{1,0:T(8,128)} %fusion.78, f32[2,1408,1408]{2,1,0:T(8,128)} %param.42), kind=kOutput, calls=%fused_computation.101 | convolution fusion | flops 24363401216 | bytes 19464196 | tf_op jit(solution)/shard_map/dot_general | solution.py:33
  2598.5 36.4 %all-reduce.13.cloned.1.call-done = f32[1024,1024]{1,0:T(8,128)} async-done(((f32[1024,1024]{1,0:T(8,128)}), f32[1024,1024]{1,0:T(8,128)}) %all-reduce.13.cloned.1.call-update) | async-done | bytes 4194320 | tf_op jit(solution)/shard_map/psum | solution.py:73
  2667.6 33.9 %fusion.36 = f32[1408,1408]{1,0:T(8,128)} fusion(f32[1024,1408]{0,1:T(8,128)} %bitcast.423, f32[2,1408,1408]{2,1,0:T(8,128)} %param.42), kind=kOutput, calls=%fused_computation.60 | convolution fusion | flops 24364482560 | bytes 27394048 | tf_op jit(solution)/shard_map/dot_general | solution.py:32
  2748.1 48.6 %reduce-scatter.10.cloned.1.call-done = f32[3,128,256]{1,2,0:T(8,128)} async-done(((f32[3,1024,256]{1,2,0:T(8,128)}), f32[3,128,256]{1,2,0:T(8,128)}) %reduce-scatter.10.cloned.1.call-update) | async-done | bytes 393232 | tf_op jit(solution)/shard_map/reduce_scatter | solution.py:312
  (423 shorter events, 1037.6 us)
Async XLA Ops:
  7.2 31.7 %all-gather.4.cloned.1.call-start = ((), (), s32[]{:S(2)}) async-start(), calls=%async_computation.9 | async-start | bytes 1769472 | tf_op jit(solution)/shard_map/all_gather | solution.py:112
  9.6 73.0 %all-gather.6.cloned.1.call-start = ((), (), s32[]{:S(2)}) async-start(), calls=%async_computation.10 | async-start | bytes 3145728 | tf_op jit(solution)/shard_map/all_gather | solution.py:128
  44.0 566.7 %all-reduce.11.cloned.1.call-start = ((), (), s32[]{:S(2)}) async-start(), calls=%async_computation.11 | async-start | bytes 8388608 | tf_op jit(solution)/shard_map/psum | solution.py:73
  447.7 168.2 %copy-start.77 = (f32[2,4]{1,0:T(2,128)}, f32[2,4]{1,0:T(2,128)S(1)}, u32[]{:S(2)}) copy-start(f32[2,4]{1,0:T(2,128)S(1)} %get-tuple-element.300) | copy-start | bytes 100
  454.4 156.2 %copy-start.16 = (bf16[1024,1024]{1,0:T(8,128)(2,1)S(1)}, bf16[1024,1024]{1,0:T(8,128)(2,1)}, u32[]{:S(2)}) copy-start(bf16[1024,1024]{1,0:T(8,128)(2,1)} %param.26) | copy-start | bytes 6291460
  458.7 168.1 %copy-start.65 = (s32[2048,1]{0,1:T(1,128)}, s32[2048,1]{0,1:T(1,128)S(1)}, u32[]{:S(2)}) copy-start(s32[2048,1]{0,1:T(1,128)S(1)} %compare_select_fusion) | copy-start | bytes 24580
  458.7 156.7 %copy-start.55 = (f32[1,1024]{1,0:T(1,128)S(1)}, f32[1,1024]{1,0:T(1,128)}, u32[]{:S(2)}) copy-start(f32[1,1024]{1,0:T(1,128)} %get-tuple-element.706) | copy-start | bytes 12292
  615.9 99.7 %copy-start.14 = (bf16[1024,1024]{1,0:T(8,128)(2,1)}, bf16[1024,1024]{1,0:T(8,128)(2,1)S(1)}, u32[]{:S(2)}) copy-start(bf16[1024,1024]{1,0:T(8,128)(2,1)S(1)} %multiply_convert_fusion.3) | copy-start | bytes 6291460
  640.5 105.0 %all-to-all-start = ((bf16[8,320,1024]{2,1,0:T(8,128)(2,1)}), bf16[8,320,1024]{2,1,0:T(8,128)(2,1)}, u32[]{:S(2)}, u32[]{:S(2)}) async-start(bf16[8,320,1024]{2,1,0:T(8,128)(2,1)} %bitcast.393), calls=%async_computation | async-start | bytes 10485760 | tf_op jit(solution)/shard_map/all_to_all | solution.py:65
  745.5 64.7 %all-to-all-start.2 = ((bf16[8,320,1024]{2,1,0:T(8,128)(2,1)}), bf16[8,320,1024]{2,1,0:T(8,128)(2,1)}, u32[]{:S(2)}, u32[]{:S(2)}) async-start(bf16[8,320,1024]{2,1,0:T(8,128)(2,1)} %bitcast.394), calls=%async_computation.2 | async-start | bytes 10485760 | tf_op jit(solution)/shard_map/all_to_all | solution.py:65
  1608.8 64.3 %all-to-all-start.3 = ((bf16[8,320,1024]{2,1,0:T(8,128)(2,1)}), bf16[8,320,1024]{2,1,0:T(8,128)(2,1)}, u32[]{:S(2)}, u32[]{:S(2)}) async-start(bf16[8,320,1024]{2,1,0:T(8,128)(2,1)} %get-tuple-element.680), calls=%async_computation.3 | async-start | bytes 10485760 | tf_op jit(solution)/shard_map/all_to_all | solution.py:65
  1613.6 858.5 %reduce-scatter.8.cloned.1.call-start = ((), (), s32[]{:S(2)}) async-start(), calls=%async_computation.12 | async-start | bytes 6291456 | tf_op jit(solution)/shard_map/reduce_scatter | solution.py:296
  2403.7 231.2 %all-reduce.13.cloned.1.call-start = ((), (), s32[]{:S(2)}) async-start(), calls=%async_computation.13 | async-start | bytes 8388608 | tf_op jit(solution)/shard_map/psum | solution.py:73
  2478.7 248.3 %reduce-scatter.14.cloned.1.call-start = ((), (), s32[]{:S(2)}) async-start(), calls=%async_computation.16 | async-start | bytes 36864 | tf_op jit(solution)/shard_map/reduce_scatter | solution.py:314
  2478.8 71.5 %slice-start = ((s8[5767168]{0:T(1024)(128)(4,1)}), s8[1572864]{0:T(1024)(128)(4,1)S(1)}, s32[]{:S(2)}) async-start(s8[5767168]{0:T(1024)(128)(4,1)} %bitcast.391), calls=%async_computation.18 | async-start | bytes 3145728
  2554.8 173.5 %reduce-scatter.12.cloned.1.call-start = ((), (), s32[]{:S(2)}) async-start(), calls=%async_computation.15 | async-start | bytes 1179648 | tf_op jit(solution)/shard_map/reduce_scatter | solution.py:313
  2558.8 187.8 %reduce-scatter.16.cloned.1.call-start = ((), (), s32[]{:S(2)}) async-start(), calls=%async_computation.17 | async-start | bytes 589824
  2572.4 62.5 %copy-start.17 = (bf16[1024,1024]{1,0:T(8,128)(2,1)S(1)}, bf16[1024,1024]{1,0:T(8,128)(2,1)}, u32[]{:S(2)}) copy-start(bf16[1024,1024]{1,0:T(8,128)(2,1)} %param.26) | copy-start | bytes 6291460
  2572.4 62.5 %copy-start.62 = (f32[1024]{0:T(1024)S(1)}, f32[1024]{0:T(1024)}, u32[]{:S(2)}) copy-start(f32[1024]{0:T(1024)} %copy-done.61) | copy-start | bytes 12292
  2639.6 157.1 %reduce-scatter.10.cloned.1.call-start = ((), (), s32[]{:S(2)}) async-start(), calls=%async_computation.14 | async-start | bytes 3538944 | tf_op jit(solution)/shard_map/reduce_scatter | solution.py:312
  2667.6 63.7 %copy-start.41 = (f32[256,128]{1,0:T(8,128)S(1)}, f32[256,128]{1,0:T(8,128)}, u32[]{:S(2)}) copy-start(f32[256,128]{1,0:T(8,128)} %param.31) | copy-start | bytes 393220
  2667.6 68.4 %copy-start.58 = (f32[1024]{0:T(1024)S(1)}, f32[1024]{0:T(1024)}, u32[]{:S(2)}) copy-start(f32[1024]{0:T(1024)} %copy-done.57) | copy-start | bytes 12292
  2736.1 64.0 %copy-start.32 = (f32[3,128,256]{2,1,0:T(8,128)S(1)}, f32[3,128,256]{2,1,0:T(8,128)}, u32[]{:S(2)}) copy-start(f32[3,128,256]{2,1,0:T(8,128)} %param.30) | copy-start | bytes 1179652
  2741.6 64.0 %copy-start.31 = (f32[2,3,256,256]{3,2,1,0:T(8,128)S(1)}, f32[2,3,256,256]{3,2,1,0:T(8,128)}, u32[]{:S(2)}) copy-start(f32[2,3,256,256]{3,2,1,0:T(8,128)} %param.38) | copy-start | bytes 4718596
  (85 other events, 1319.7 us)
Sparse Core Ops, SparseCore 0:
  10.5 28.3 all-gather.3
  44.1 36.6 all-gather.5
  454.6 155.9 all-reduce.10
  2403.8 56.0 reduce-scatter.7
  2478.8 156.0 all-reduce.12
  2639.2 30.2 reduce-scatter.13
  2673.2 36.1 reduce-scatter.11
  2712.4 34.1 reduce-scatter.15
  2750.4 46.2 reduce-scatter.9
where the time goes:
time: 2820 us; the launch traced here: 2810 us
  local copies, waits for them, and re-layouts  924 us (33%)
  blocking collectives  902 us (32%)
  matrix products  413 us (15%)
  waiting for transfers between devices  331 us (12%)
  other arithmetic  189 us (7%)
    psum x1, blocking collectives, row_sum(): return lax.psum(values, 'tp')  697 us
    while x50, local copies, waits for them, and re-layouts  538 us
    psum x2, waiting for transfers between devices, head_sum(): return lax.psum(values, 'tp')  188 us
    reshape x4, local copies, waits for them, and re-layouts, bias_block(): tiled = tiled[:, :block * (width - 1)].reshape(heads, block, width - 1)  119 us
    all_to_all x3, waiting for transfers between devices, crossing(): lax.all_to_all(values, ('fsdp', 'ctx'), split_axis=0, concat_axis=0, tile...  76.6 us
    all_to_all x1, blocking collectives, crossing(): lax.all_to_all(values, ('fsdp', 'ctx'), split_axis=0, concat_axis=0, tile...  66.8 us
    reshape x2, local copies, waits for them, and re-layouts, diagonal_sums(): jnp.pad(padded, ((0, 0), (0, block)))  63.7 us
  transfers between devices with their start and end apart: 12, of which 7 were waited for; matrix products, arithmetic and copies ran while one was open for 12% of the time, Pallas kernels for 0%

commit v1 on v0

v1 whole, which is shorter than its diff:
```python
import functools

import jax
import jax.numpy as jnp
from jax import lax
from jax.experimental import pallas as pl
from jax.experimental.pallas import tpu as pltpu

from jax.sharding import PartitionSpec as P

DH = 64
LANES = 128
MIB = 1024 * 1024


TOPK = 2

highest = lax.Precision.HIGHEST
norm_epsilon = 1e-06
step_epsilon = 1e-06
moment_epsilon = 1e-08
clip_level = 4.0
decay = 0.5
matrix_rate = 0.3
gain_rate = 0.25
router_rate = 0.01
table_rate = 0.3


def dot_nt(left, right):
    return lax.dot_general(left, right, (((1,), (1,)), ((), ())), preferred_element_type=jnp.float32)


def dot_nn(left, right):
    return lax.dot_general(left, right, (((1,), (0,)), ((), ())), preferred_element_type=jnp.float32)


def dot_tn(left, right):
    return lax.dot_general(left, right, (((0,), (0,)), ((), ())), preferred_element_type=jnp.float32)


def half_mask(shape, half):
    lane = lax.broadcasted_iota(jnp.int32, shape, 1)
    return (lane // DH) == half


def attend_kernel(length, rows, tile, q_ref, k_ref, v_ref, line_ref, mixed_ref, log_ref, peak_ref, strip, wide):
    step = pl.program_id(1)
    span = line_ref.shape[2]

    @pl.when(step == 0)
    def _():
        for half in range(2):
            line = jnp.broadcast_to(line_ref[0, half : half + 1, :], (LANES, span))
            strip[half] = pltpu.roll(line, span - (LANES - 1), 1, stride=1, stride_axis=0)
        wide[:, :LANES] = v_ref[...]
        wide[:, LANES:] = jnp.ones((length, LANES), jnp.bfloat16)
        peak_ref[...] = jnp.full(peak_ref.shape, -jnp.inf, jnp.float32)

    query = q_ref[...]
    groups = tile // LANES
    last = rows // LANES - 1
    mixed = jnp.zeros((tile, LANES), jnp.float32)
    for half in range(2):
        mine = half_mask((tile, LANES), half)
        own = jnp.where(mine, query, jnp.zeros_like(query))
        logit = dot_nt(own, k_ref[...])
        top = jnp.max(logit, 1, keepdims=True)
        bias = []
        for group in range(groups):
            start = pl.multiple_of((last - (step * groups + group)) * LANES, LANES)
            bias.append(strip[half, :, pl.ds(start, length)])
        bias = jnp.concatenate(bias, 0) if groups > 1 else bias[0]
        powers = jnp.exp(logit + bias - top)
        both = dot_nn(powers.astype(jnp.bfloat16), wide[...])
        total = both[:, LANES:]
        mixed = jnp.where(mine, both[:, :LANES] / total, mixed)
        log_total = top + jnp.log(total)
        log_ref[0, half : half + 1, :] = log_total.T[0:1, :]
        best = jnp.max(jnp.broadcast_to(top, (tile, LANES)), 0, keepdims=True)
        peak_ref[0, half : half + 1, :] = jnp.maximum(peak_ref[0, half : half + 1, :], best)
    mixed_ref[...] = mixed.astype(jnp.bfloat16)


def attend(query, keys, values, lines):
    rows, cols = query.shape
    length = keys.shape[0]
    pairs = cols // LANES
    tile = 256 if length <= 4096 else 128
    span = lines.shape[2]
    return pl.pallas_call(
        functools.partial(attend_kernel, length, rows, tile),
        grid=(pairs, rows // tile),
        in_specs=[
            pl.BlockSpec((tile, LANES), lambda p, t: (t, p)),
            pl.BlockSpec((length, LANES), lambda p, t: (0, p)),
            pl.BlockSpec((length, LANES), lambda p, t: (0, p)),
            pl.BlockSpec((1, 2, span), lambda p, t: (p, 0, 0)),
        ],
        out_specs=[
            pl.BlockSpec((tile, LANES), lambda p, t: (t, p)),
            pl.BlockSpec((1, 2, tile), lambda p, t: (p, 0, t)),
            pl.BlockSpec((1, 2, LANES), lambda p, t: (p, 0, 0)),
        ],
        out_shape=[
            jax.ShapeDtypeStruct((rows, cols), jnp.bfloat16),
            jax.ShapeDtypeStruct((pairs, 2, rows), jnp.float32),
            jax.ShapeDtypeStruct((pairs, 2, LANES), jnp.float32),
        ],
        scratch_shapes=[
            pltpu.VMEM((2, LANES, span), jnp.float32),
            pltpu.VMEM((length, 2 * LANES), jnp.bfloat16),
        ],
        compiler_params=pltpu.CompilerParams(vmem_limit_bytes=56 * MIB),
        cost_estimate=pl.CostEstimate(flops=16 * rows * length * cols, bytes_accessed=8 * length * cols, transcendentals=rows * length * cols // DH),
    )(query, keys, values, lines)


def attend_back_kernel(length, rows, tile, chunk, q_ref, k_ref, v_ref, g_ref, m_ref, log_ref, line_ref, dq_ref, dk_ref, dv_ref, sums_ref, strip, gather):
    step = pl.program_id(1)
    steps = pl.num_programs(1)
    span = line_ref.shape[2]
    last = length // LANES - 1

    @pl.when(step == 0)
    def _():
        for half in range(2):
            line = jnp.broadcast_to(line_ref[0, half : half + 1, :], (LANES, span))
            strip[half] = pltpu.roll(line, span - LANES, 1, stride=1, stride_axis=0)
        gather[...] = jnp.zeros_like(gather)
        dk_ref[...] = jnp.zeros_like(dk_ref)
        dv_ref[...] = jnp.zeros_like(dv_ref)

    query = q_ref[...]
    grad = g_ref[...]
    product = grad.astype(jnp.float32) * m_ref[...].astype(jnp.float32)
    owns, grads, deltas, logs = [], [], [], []
    for half in range(2):
        mine = half_mask((tile, LANES), half)
        owns.append(jnp.where(mine, query, jnp.zeros_like(query)))
        grads.append(jnp.where(mine, grad, jnp.zeros_like(grad)))
        picks = half_mask((8, LANES), half).astype(jnp.float32)
        deltas.append(
            lax.dot_general(picks, product, (((1,), (1,)), ((), ())), precision=lax.Precision.HIGHEST, preferred_element_type=jnp.float32)[0:1, :]
        )
        logs.append(log_ref[0, half : half + 1, :])

    def one_chunk(number, carry):
        outs = []
        base = pl.multiple_of(number * chunk, chunk)
        keys = k_ref[pl.ds(base, chunk), :]
        values = v_ref[pl.ds(base, chunk), :]
        new_key = dk_ref[pl.ds(base, chunk), :]
        new_value = dv_ref[pl.ds(base, chunk), :]
        for half in range(2):
            logit = dot_nt(keys, owns[half])
            places = []
            bias = []
            for group in range(chunk // LANES):
                row_group = number * (chunk // LANES) + group
                start = pl.multiple_of((last - row_group) * LANES + step * tile, LANES)
                places.append(start)
                bias.append(strip[half, :, pl.ds(start, tile)])
            bias = jnp.concatenate(bias, 0) if len(bias) > 1 else bias[0]
            shares = jnp.exp(logit + bias - logs[half])
            grad_shares = dot_nt(values, grads[half])
            scores = shares * (grad_shares - deltas[half])
            low_shares = shares.astype(jnp.bfloat16)
            low_scores = scores.astype(jnp.bfloat16)
            new_value = new_value + dot_nn(low_shares, grads[half])
            new_key = new_key + dot_nn(low_scores, owns[half])
            outs.append(carry[half] + dot_tn(low_scores, keys))
            for group, start in enumerate(places):
                gather[half, :, pl.ds(start, tile)] += scores[group * LANES : (group + 1) * LANES]
        dk_ref[pl.ds(base, chunk), :] = new_key
        dv_ref[pl.ds(base, chunk), :] = new_value
        return tuple(outs)

    zero = jnp.zeros((tile, LANES), jnp.float32)
    first, second = lax.fori_loop(0, length // chunk, one_chunk, (zero, zero))
    both = jnp.where(half_mask((tile, LANES), 0), first, second)
    dq_ref[...] = (both * (DH**-0.5)).astype(dq_ref.dtype)

    @pl.when(step == steps - 1)
    def _():
        for half in range(2):
            values = gather[half]
            size = LANES // 2
            while size >= 1:
                values = values[:size] + pltpu.roll(values[size : 2 * size], span - size, 1)
                size //= 2
            sums_ref[0, half : half + 1, :] = pltpu.roll(jnp.broadcast_to(values, (8, span)), LANES, 1)[0:1]


def attend_back(query, keys, values, grad, mixed, logs, lines):
    rows, cols = query.shape
    length = keys.shape[0]
    pairs = cols // LANES
    tile = 256
    chunk = 512
    span = lines.shape[2]
    return pl.pallas_call(
        functools.partial(attend_back_kernel, length, rows, tile, chunk),
        grid=(pairs, rows // tile),
        in_specs=[
            pl.BlockSpec((tile, LANES), lambda p, t: (t, p)),
            pl.BlockSpec((length, LANES), lambda p, t: (0, p)),
            pl.BlockSpec((length, LANES), lambda p, t: (0, p)),
            pl.BlockSpec((tile, LANES), lambda p, t: (t, p)),
            pl.BlockSpec((tile, LANES), lambda p, t: (t, p)),
            pl.BlockSpec((1, 2, tile), lambda p, t: (p, 0, t)),
            pl.BlockSpec((1, 2, span), lambda p, t: (p, 0, 0)),
        ],
        out_specs=[
            pl.BlockSpec((tile, LANES), lambda p, t: (t, p)),
            pl.BlockSpec((length, LANES), lambda p, t: (0, p)),
            pl.BlockSpec((length, LANES), lambda p, t: (0, p)),
            pl.BlockSpec((1, 2, span), lambda p, t: (p, 0, 0)),
        ],
        out_shape=[
            jax.ShapeDtypeStruct((rows, cols), jnp.bfloat16),
            jax.ShapeDtypeStruct((length, cols), jnp.float32),
            jax.ShapeDtypeStruct((length, cols), jnp.float32),
            jax.ShapeDtypeStruct((pairs, 2, span), jnp.float32),
        ],
        scratch_shapes=[
            pltpu.VMEM((2, LANES, span), jnp.float32),
            pltpu.VMEM((2, LANES, span), jnp.float32),
        ],
        compiler_params=pltpu.CompilerParams(vmem_limit_bytes=60 * MIB),
        cost_estimate=pl.CostEstimate(flops=40 * rows * length * cols, bytes_accessed=24 * length * cols, transcendentals=rows * length * cols // DH),
    )(query, keys, values, grad, mixed, logs, lines)


def normalize(values, gain):
    return values * lax.rsqrt(jnp.mean(values * values, -1, keepdims=True) + norm_epsilon) * gain


def gated_gelu(both):
    return jax.nn.gelu(both[..., 0, :], approximate=True) * both[..., 1, :]


def precondition(grad, master, left, right):
    low = grad.astype(jnp.bfloat16)
    new_left = decay * left[0] + (1.0 - decay) * dot_nt(low, low)
    new_right = decay * right[0] + (1.0 - decay) * dot_tn(low, low)
    turned = dot_nn(left[1].astype(jnp.bfloat16), low).astype(jnp.bfloat16)
    direction = dot_nn(turned, right[1].astype(jnp.bfloat16))
    size = jnp.sqrt(jnp.mean(master * master) + step_epsilon)
    step = (
        matrix_rate * size * direction * lax.rsqrt(jnp.mean(direction * direction) + step_epsilon)
    )
    return (new_left, new_right, master - step)


def adapt(grad, moment, master, rate):
    new_moment = decay * moment + (1.0 - decay) * grad * grad
    return (new_moment, master - rate * grad * lax.rsqrt(new_moment + moment_epsilon))


def barrier(*values):
    return lax.optimization_barrier(values)


def crossing(values):
    return lax.all_to_all(values, ("fsdp", "ctx"), split_axis=0, concat_axis=0, tiled=True)


def on_device(
    tokens,
    cotangent,
    routes,
    buckets,
    attention_in,
    attention_out,
    router,
    gains,
    bias_table,
    expert_in,
    expert_out,
    attention_in_left,
    attention_in_right,
    attention_out_left,
    attention_out_right,
    expert_in_left,
    expert_in_right,
    expert_out_left,
    expert_out_right,
    router_moment,
    gains_moment,
    table_moment,
):
    low = jnp.bfloat16
    rows = tokens.shape[0]
    width = tokens.shape[1]
    shards = lax.axis_size("fsdp") * lax.axis_size("ctx")
    n_ctx = lax.axis_size("ctx")
    n_tp = lax.axis_size("tp")
    here = lax.axis_index("fsdp") * n_ctx + lax.axis_index("ctx")
    tp_here = lax.axis_index("tp")
    length = rows * n_ctx
    depth = attention_in.shape[1]
    head_cols = attention_in.shape[2]
    local_heads = head_cols // DH
    head_pairs = head_cols // LANES
    table_size = bias_table.shape[0]
    experts = router.shape[1]
    capacity = rows * TOPK * 5 // (4 * experts)
    slots_all = experts * capacity
    span = length + rows

    sizes = (depth * experts, 2 * depth, table_size * local_heads)
    small = jnp.concatenate(
        [router.astype(low).reshape(-1), gains.astype(low).reshape(-1), bias_table.astype(low).reshape(-1)]
    )
    small = jnp.pad(small, (0, -small.shape[0] % (16 * head_cols))).reshape(-1, head_cols)
    gathered = lax.all_gather(
        jnp.concatenate([attention_in.astype(low).reshape(3 * depth, head_cols), small], 0),
        ("fsdp", "ctx"),
        axis=0,
        tiled=False,
    )
    entry_full = (
        gathered[:, : 3 * depth]
        .reshape(shards, 3, depth, head_cols)
        .transpose(1, 0, 2, 3)
        .reshape(3, width, head_cols)
    )
    small = gathered[:, 3 * depth :].reshape(shards, -1)
    router_full = small[:, : sizes[0]].reshape(width, experts)
    gains_full = (
        small[:, sizes[0] : sizes[0] + sizes[1]]
        .reshape(shards, 2, depth)
        .transpose(1, 0, 2)
        .reshape(2, width)
    )
    table_full = small[:, sizes[0] + sizes[1] : sum(sizes)].reshape(shards * table_size, local_heads)
    gain_first = gains_full[0].astype(jnp.float32)
    gain_second = gains_full[1].astype(jnp.float32)
    expand_in = expert_in[0].astype(low)
    expand_out = expert_out[0].astype(low)

    chosen = routes.reshape(-1)
    route_hits = (chosen[:, None] == jnp.arange(experts, dtype=jnp.int32)[None, :]).astype(
        jnp.int32
    )
    slots = jnp.sum(route_hits * (jnp.cumsum(route_hits, 0) - 1), 1)
    slot_rows = (chosen * capacity + slots).reshape(rows, TOPK)
    place = jnp.arange(slots_all, dtype=jnp.int32)
    first_hit = place[:, None] == slot_rows[None, :, 0]
    second_hit = place[:, None] == slot_rows[None, :, 1]
    picks = (first_hit | second_hit).astype(low)
    other = jnp.sum(
        jnp.where(first_hit, routes[None, :, 1], 0) + jnp.where(second_hit, routes[None, :, 0], 0),
        1,
    )
    grad_buffer = dot_nn(picks, cotangent).astype(low).reshape(experts, capacity, width)
    other_arrived = crossing(other.reshape(experts, capacity)).reshape(-1)
    grad_arrived = crossing(grad_buffer).reshape(slots_all, width)

    inputs = tokens.astype(jnp.float32)
    first = normalize(inputs, gain_first).astype(low)
    first, unused = barrier(first, grad_buffer)
    projected = jnp.einsum(
        "sd,kde->kse", first, entry_full, preferred_element_type=jnp.float32
    )
    query = (projected[0].astype(low) * (DH**-0.5)).astype(low)
    key_value = projected[1:].astype(low)
    low_end = length - rows - lax.axis_index("ctx") * rows
    near = lax.dynamic_slice_in_dim(jnp.pad(buckets, (0, 1)), low_end, span, 0)
    hits = (near[:, None] == jnp.arange(table_full.shape[0], dtype=jnp.int32)[None, :]).astype(low)
    lines = lax.dot_general(
        table_full, hits, (((0,), (1,)), ((), ())), preferred_element_type=jnp.float32
    ).reshape(head_pairs, 1, 2, span)
    back_lines = lines[..., ::-1]
    exit_own = lax.all_gather(attention_out.astype(low), ("fsdp", "ctx"), axis=1, tiled=True)
    exits = [exit_own]
    for shift in range(1, n_tp):
        exits.append(
            lax.ppermute(exit_own, "tp", [(i, (i + shift) % n_tp) for i in range(n_tp)])
        )
    turned = jnp.concatenate(exits[::-1] + exits[::-1], 0)
    exit_all = lax.dynamic_slice_in_dim(
        turned, (n_tp - 1 - tp_here) * head_cols, n_tp * head_cols, 0
    ).reshape(n_tp, head_pairs, LANES, width)
    queries, pairs, mixed_parts, logs, peak_parts = [], [], [], [], []
    value = jnp.zeros((), jnp.float32)
    for pair in range(head_pairs):
        columns = slice(pair * LANES, (pair + 1) * LANES)
        queries.append(query[:, columns])
        pairs.append(lax.all_gather(key_value[:, :, columns], "ctx", axis=1, tiled=True))
    for pair in range(head_pairs):
        mixed_part, log_part, peak_part = attend(
            queries[pair], pairs[pair][0], pairs[pair][1], lines[pair]
        )
        mixed_parts.append(mixed_part)
        logs.append(log_part)
        peak_parts.append(peak_part[0, :, 0])
        mixed_all = lax.all_gather(mixed_part, "tp", axis=1, tiled=True)
        value = value + dot_nn(mixed_all, exit_all[:, pair].reshape(n_tp * LANES, width))
    mixed = jnp.concatenate(mixed_parts, 1)
    middle = inputs + value
    second = normalize(middle, gain_second).astype(low)

    buffer = dot_nn(picks, second).astype(low).reshape(experts, capacity, width)
    buffer, grad_arrived, other_arrived = barrier(buffer, grad_arrived, other_arrived)
    arrived = crossing(buffer).reshape(slots_all, width)
    plain_grad = dot_nt(grad_arrived, expand_out)
    arrived, plain_grad = barrier(arrived, plain_grad)
    logits = dot_nn(arrived, router_full)
    names = jnp.arange(experts, dtype=jnp.int32)[None, :]
    contrast = (names == here).astype(jnp.float32) - (names == other_arrived[:, None]).astype(
        jnp.float32
    )
    gate = jax.nn.sigmoid(jnp.sum(logits * contrast, 1, keepdims=True))
    mixed_up = jnp.einsum("sd,dgf->sgf", arrived, expand_in, preferred_element_type=jnp.float32)
    hidden, pull = jax.vjp(gated_gelu, mixed_up)
    gated_hidden = (gate * hidden).astype(low)
    grad_gate = jnp.sum(plain_grad * hidden, 1, keepdims=True)
    grad_choice = (gate * (1.0 - gate) * grad_gate * contrast).astype(low)
    grad_mixed_up = pull(gate * plain_grad)[0].astype(low)
    sent_grads = (
        jnp.einsum("sgf,dgf->sd", grad_mixed_up, expand_in, preferred_element_type=jnp.float32)
        + dot_nt(grad_choice, router_full)
    ).astype(low)
    back_grads = crossing(sent_grads.reshape(experts, capacity, width)).reshape(slots_all, width)

    sent_rows = dot_nn(gated_hidden, expand_out).astype(low)
    grad_router = dot_tn(arrived, grad_choice)
    grad_expand_out = dot_tn(gated_hidden, grad_arrived)
    shrink_left, shrink_right, shrink_new = precondition(
        grad_expand_out, expert_out[0], expert_out_left, expert_out_right
    )
    grad_expand_in = jnp.einsum(
        "sd,sgf->dgf", arrived, grad_mixed_up, preferred_element_type=jnp.float32
    )
    back_grads, sent_rows, grad_router, grad_expand_out, grad_expand_in, shrink_left, shrink_right, shrink_new = barrier(
        back_grads, sent_rows, grad_router, grad_expand_out, grad_expand_in, shrink_left, shrink_right, shrink_new
    )
    grad_second = lax.psum(dot_tn(picks, back_grads).astype(low), "tp").astype(jnp.float32)

    back_rows = crossing(sent_rows.reshape(experts, capacity, width)).reshape(slots_all, width)
    expand_left, expand_right, expand_new = precondition(
        grad_expand_in.reshape(width, -1),
        expert_in.reshape(width, -1),
        expert_in_left,
        expert_in_right,
    )
    result_part = dot_tn(picks, back_rows).astype(low)
    grad_second, expand_left, expand_right, expand_new, result_part = barrier(
        grad_second, expand_left, expand_right, expand_new, result_part
    )
    result = (middle + lax.psum(result_part, "tp").astype(jnp.float32)).astype(low)

    unused, pull = jax.vjp(normalize, middle, gain_second)
    grad_middle_norm, grad_gain_second = pull(grad_second)
    grad_middle = cotangent.astype(jnp.float32) + grad_middle_norm
    grad_attention = grad_middle.astype(low)
    grad_mixed = dot_nt(grad_attention, exit_own).astype(low)
    grad_queries, key_value_grads, sums = [], [], []
    for pair in range(head_pairs):
        columns = slice(pair * LANES, (pair + 1) * LANES)
        grad_query, key_grad, value_grad, line_sums = attend_back(
            queries[pair],
            pairs[pair][0],
            pairs[pair][1],
            grad_mixed[:, columns],
            mixed_parts[pair],
            logs[pair],
            back_lines[pair],
        )
        grad_queries.append(grad_query)
        sums.append(line_sums)
        terms = jnp.concatenate([key_grad, value_grad], 1).astype(low)
        swapped = lax.all_to_all(
            terms.reshape(n_ctx, rows, 2 * LANES), "ctx", split_axis=0, concat_axis=0, tiled=True
        )
        key_value_grads.append(jnp.sum(swapped.astype(jnp.float32), 0).astype(low))
    grad_projected = jnp.stack(
        [
            jnp.concatenate(grad_queries, 1),
            jnp.concatenate([terms[:, :LANES] for terms in key_value_grads], 1),
            jnp.concatenate([terms[:, LANES:] for terms in key_value_grads], 1),
        ]
    )
    grad_exit = dot_tn(mixed, grad_attention).astype(low)
    grad_first_part = jnp.einsum(
        "kse,kde->sd", grad_projected, entry_full, preferred_element_type=jnp.float32
    )
    grad_first_part, result = barrier(grad_first_part.astype(low), result)
    grad_first = lax.psum(grad_first_part, "tp").astype(jnp.float32)
    grad_entry = jnp.einsum(
        "sd,kse->dke", first, grad_projected, preferred_element_type=jnp.float32
    ).astype(low)
    entry_terms = lax.all_to_all(
        grad_entry.reshape(shards, depth, 3 * head_cols),
        ("fsdp", "ctx"),
        split_axis=0,
        concat_axis=0,
        tiled=True,
    )
    owned_in = (
        jnp.sum(entry_terms.astype(jnp.float32), 0).reshape(depth, 3, head_cols).transpose(1, 0, 2)
    )
    exit_terms = lax.all_to_all(
        grad_exit.reshape(head_cols, shards, depth).transpose(1, 0, 2),
        ("fsdp", "ctx"),
        split_axis=0,
        concat_axis=0,
        tiled=True,
    )
    owned_out = jnp.sum(exit_terms.astype(jnp.float32), 0)
    unused, pull = jax.vjp(normalize, inputs, gain_first)
    grad_inputs, grad_gain_first = pull(grad_first)
    grad_tokens = grad_middle + grad_inputs

    table_grad = lax.dot_general(
        hits.astype(jnp.float32),
        jnp.concatenate(sums, 0).reshape(local_heads, span)[:, ::-1],
        (((0,), (1,)), ((), ())),
        precision=highest,
        preferred_element_type=jnp.float32,
    )
    own_tp = (jnp.arange(n_tp) == tp_here).astype(jnp.float32)
    own_shard = (jnp.arange(shards) == here).astype(jnp.float32)
    gain_sums = jnp.stack([grad_gain_first, grad_gain_second]) * own_tp[0]
    peak_own = jnp.concatenate(peak_parts)
    pieces = [
        grad_router,
        gain_sums,
        own_tp[:, None, None] * table_grad[None],
        own_shard[:, None, None] * own_tp[None, :, None] * peak_own[None, None, :],
    ]
    packed = jnp.concatenate([piece.reshape(-1) for piece in pieces])
    total = packed.shape[0]
    packed = lax.psum(
        jnp.pad(packed, (0, -total % 1024)).reshape(-1, LANES), ("fsdp", "ctx", "tp")
    ).reshape(-1)
    spots = [0]
    for piece in pieces:
        spots.append(spots[-1] + piece.size)
    router_sum = packed[spots[0] : spots[1]].reshape(shards, depth, experts)
    owned_router = lax.dynamic_index_in_dim(router_sum, here, 0, keepdims=False)
    gain_sum = packed[spots[1] : spots[2]].reshape(2, width)
    owned_gains = lax.dynamic_slice_in_dim(gain_sum, here * depth, depth, 1)
    table_sum = packed[spots[2] : spots[3]].reshape(n_tp, shards, table_size, local_heads)
    owned_table = jnp.einsum("t,s,tsbh->bh", own_tp, own_shard, table_sum, precision=highest)
    peak_sum = packed[spots[3] : spots[4]].reshape(shards, n_tp, local_heads)
    peaks = jnp.max(jnp.einsum("t,sth->sh", own_tp, peak_sum, precision=highest), 0)
    in_left, in_right, in_new = jax.vmap(precondition)(
        owned_in,
        attention_in,
        jnp.swapaxes(attention_in_left, 0, 1),
        jnp.swapaxes(attention_in_right, 0, 1),
    )
    column = jnp.sqrt(jnp.repeat(clip_level / jnp.maximum(peaks, clip_level), DH))
    in_new = in_new * jnp.stack([column, column, jnp.ones_like(column)])[:, None, :]
    out_left, out_right, out_new = precondition(
        owned_out, attention_out, attention_out_left, attention_out_right
    )
    router_moment_new, router_new = adapt(owned_router, router_moment, router, router_rate)
    gains_moment_new, gains_new = adapt(owned_gains, gains_moment, gains, gain_rate)
    table_moment_new, table_new = adapt(owned_table, table_moment, bias_table, table_rate)
    return (
        result,
        grad_tokens,
        owned_in,
        in_new,
        in_left,
        in_right,
        owned_out,
        out_new,
        out_left,
        out_right,
        grad_expand_in[None],
        expand_new.reshape(expert_in.shape),
        expand_left,
        expand_right,
        grad_expand_out[None],
        shrink_new[None],
        shrink_left,
        shrink_right,
        owned_router,
        router_moment_new,
        router_new,
        owned_gains,
        gains_moment_new,
        gains_new,
        owned_table,
        table_moment_new,
        table_new,
    )


def solution(mesh):
    placed = (
        P(("fsdp", "ctx"), None),
        P(("fsdp", "ctx"), None),
        P(("fsdp", "ctx"), None),
        P(),
        P(None, ("fsdp", "ctx"), "tp"),
        P("tp", ("fsdp", "ctx")),
        P(("fsdp", "ctx"), None),
        P(None, ("fsdp", "ctx")),
        P(("fsdp", "ctx"), "tp"),
        P(("fsdp", "ctx"), None, None, "tp"),
        P(("fsdp", "ctx"), "tp", None),
        P(None, None, ("fsdp", "ctx", "tp"), None),
        P(None, None, ("fsdp", "ctx", "tp"), None),
        P(None, ("fsdp", "ctx", "tp"), None),
        P(None, ("fsdp", "ctx", "tp"), None),
        P(None, ("fsdp", "ctx", "tp"), None),
        P(None, ("fsdp", "ctx", "tp"), None),
        P(None, ("fsdp", "ctx", "tp"), None),
        P(None, ("fsdp", "ctx", "tp"), None),
        P(("fsdp", "ctx"), None),
        P(None, ("fsdp", "ctx")),
        P(("fsdp", "ctx"), "tp"),
    )
    return jax.shard_map(
        on_device,
        mesh=mesh,
        in_specs=placed,
        out_specs=(
            P(("fsdp", "ctx"), None),
            P(("fsdp", "ctx"), None),
            P(None, ("fsdp", "ctx"), "tp"),
            P(None, ("fsdp", "ctx"), "tp"),
            P(None, ("fsdp", "ctx", "tp"), None),
            P(None, ("fsdp", "ctx", "tp"), None),
            P("tp", ("fsdp", "ctx")),
            P("tp", ("fsdp", "ctx")),
            P(("fsdp", "ctx", "tp"), None),
            P(("fsdp", "ctx", "tp"), None),
            P(("fsdp", "ctx"), None, None, "tp"),
            P(("fsdp", "ctx"), None, None, "tp"),
            P(("fsdp", "ctx", "tp"), None),
            P(("fsdp", "ctx", "tp"), None),
            P(("fsdp", "ctx"), "tp", None),
            P(("fsdp", "ctx"), "tp", None),
            P(("fsdp", "ctx", "tp"), None),
            P(("fsdp", "ctx", "tp"), None),
            P(("fsdp", "ctx"), None),
            P(("fsdp", "ctx"), None),
            P(("fsdp", "ctx"), None),
            P(None, ("fsdp", "ctx")),
            P(None, ("fsdp", "ctx")),
            P(None, ("fsdp", "ctx")),
            P(("fsdp", "ctx"), "tp"),
            P(("fsdp", "ctx"), "tp"),
            P(("fsdp", "ctx"), "tp"),
        ),
        check_vma=False,
    )
```

time: 2820 us -> 900 us (0.32)
  blocking collectives: 902 us -> 59.2 us
  local copies, waits for them, and re-layouts: 924 us -> 100 us
  matrix products: 413 us -> 210 us
  other arithmetic: 189 us -> 92.8 us
  Pallas kernels: 0 us -> 69 us
  waiting for transfers between devices: 331 us -> 294 us
  starting transfers between devices: 15.1 us -> 44.4 us
    psum x1, blocking collectives: 697 us -> 39.5 us  [on_device(): lax.psum(jnp.pad(packed, (0, -total % 1024)).reshape(-1, LANES), ('fsdp',...]
    while x51 -> x0, local copies, waits for them, and re-layouts: 539 us -> none
    dot_general x45 -> x33, matrix products: 405 us -> 201 us  [the longest x10 64.6 us: dot_nn(): lax.dot_general(left, right, (((1,), (0,)), ((), ())), preferred_element_...]
    reshape x10 -> x15, local copies, waits for them, and re-layouts: 193 us -> 7.58 us  [the longest x1 3.69 us: on_device(): entry_full = gathered[:, :3 * depth].reshape(shards, 3, depth, head_cols)...]
    all_gather x4 -> x1, blocking collectives: 99.9 us -> 19.7 us  [on_device(): lax.all_gather(attention_out.astype(low), ('fsdp', 'ctx'), axis=1, tiled=...]
    pallas_call x0 -> x4, Pallas kernels: none -> 69 us  [the longest x2 44.2 us: attend_back(): pl.pallas_call(functools.partial(attend_back_kernel, length, rows, tile,...]
    all_to_all x1 -> x0, blocking collectives: 66.8 us -> none  [crossing(): lax.all_to_all(values, ('fsdp', 'ctx'), split_axis=0, concat_axis=0, tile...]
    reduce_scatter x4 -> x0, waiting for transfers between devices: 48.6 us -> none  [the longest x1 48.6 us: on_device(): lax.psum_scatter(grad_entry, ('fsdp', 'ctx'), scatter_dimension=1, tiled=...]
  transfers between devices with their start and end apart: 12 -> 20, of which waited for: 7 -> 11; matrix products, arithmetic and copies ran while one was open for 12% -> 30% of each run, Pallas kernels for 0% -> 5%
where the time goes in v1:
time: 900 us; the launch traced here: 890 us
  waiting for transfers between devices  294 us (33%)
  matrix products  210 us (23%)
  local copies, waits for them, and re-layouts  100 us (11%)
  other arithmetic  92.8 us (10%)
  Pallas kernels  69 us (8%)
  blocking collectives  59.2 us (7%)
  starting transfers between devices  44.4 us (5%)
  between operations  19.8 us (2%)
    psum x1, waiting for transfers between devices, on_device(): lax.psum(dot_tn(picks, back_grads).astype(low), 'tp').astype(jnp.float32)  65.8 us
    dot_general x10, matrix products, dot_nn(): lax.dot_general(left, right, (((1,), (0,)), ((), ())), preferred_element_...  64.6 us
    psum x1, waiting for transfers between devices, on_device(): grad_first = lax.psum(grad_first_part, 'tp').astype(jnp.float32)  63.9 us
    dot_general x9, matrix products, dot_tn(): lax.dot_general(left, right, (((0,), (0,)), ((), ())), preferred_element_...  55.1 us
    psum x1, waiting for transfers between devices, on_device(): lax.psum(result_part, 'tp').astype(jnp.float32)  52.2 us
    all_to_all x5, waiting for transfers between devices, crossing(): lax.all_to_all(values, ('fsdp', 'ctx'), split_axis=0, concat_axis=0, tile...  49.2 us
    pallas_call x2, Pallas kernels, attend_back(): pl.pallas_call(functools.partial(attend_back_kernel, length, rows, tile,...  44.2 us
    psum x1, blocking collectives, on_device(): lax.psum(jnp.pad(packed, (0, -total % 1024)).reshape(-1, LANES), ('fsdp',...  39.5 us
  transfers between devices with their start and end apart: 20, of which 11 were waited for; matrix products, arithmetic and copies ran while one was open for 30% of the time, Pallas kernels for 5%

profile of v1, /device:TPU:0, one launch (start us, length us, event | category | flops | bytes accessed | tf_op | source)
XLA Modules:
  0.0 889.9 jit_solution(1758315259510100667)
XLA Ops:
  8.9 19.7 %all_gather.25 = bf16[256,1024]{1,0:T(8,128)(2,1)S(1)} all-gather(bf16[256,128]{1,0:T(8,128)(2,1)S(1)} %get-tuple-element.294), channel_id=1, replica_groups=mesh['fsdp'=4,'ctx'=2,'tp'=4] {'fsdp','ctx'}, dimensions={1}, use_global_device_ids=true | all-gather | bytes 589824 | tf_op jit(solution)/shard_map/all_gather | solution.py:376
  46.3 9.0 %convolution_convert_fusion.2 = bf16[2560,1024]{1,0:T(8,128)(2,1)} fusion(bf16[1024,1024]{1,0:T(8,128)(2,1)} %param.23, s32[1024]{0:T(1024)S(1)} %bitcast.376, s32[1024]{0:T(1024)S(1)} %bitcast.371), kind=kOutput, calls=%fused_computation.51 | convolution fusion | flops 5379194880 | bytes 7348224 | tf_op jit(solution)/shard_map/dot_general | solution.py:35
  85.9 16.5 %all-gather.7.cloned.1.call-done = bf16[2,2048,128]{2,1,0:T(8,128)(2,1)} async-done(((bf16[2,1024,128]{2,1,0:T(8,128)(2,1)}), bf16[2,2048,128]{2,1,0:T(8,128)(2,1)}) %all-gather.7.cloned.1.call-update) | async-done | bytes 1048592 | tf_op jit(solution)/shard_map/all_gather | solution.py:391
  104.6 12.4 %shard_map.421 = (bf16[1024,128]{1,0:T(8,128)(2,1)}, f32[1,2,1024]{2,1,0:T(2,128)}, f32[1,2,128]{2,1,0:T(2,128)}) custom-call(bf16[1024,128]{1,0:T(8,128)(2,1)} %get-tuple-element.289.q_ref, bf16[2048,128]{1,0:T(8,128)(2,1)} %get-tuple-element.280.k_ref, bf16[2048,128]{1,0:T(8,128)(2,1)} %get-tuple-element.279.v_ref, f32[1,2,3072]{2,1,0:T(2,128)} %get-tuple-element.296.line_ref), custom_call_target="tpu_custom_call" | custom-call | flops 4294967296 | bytes 2097152 | tf_op jit(solution)/shard_map/pallas_call | solution.py:91
  137.9 12.4 %shard_map.422 = (bf16[1024,128]{1,0:T(8,128)(2,1)}, f32[1,2,1024]{2,1,0:T(2,128)}, f32[1,2,128]{2,1,0:T(2,128)}) custom-call(bf16[1024,128]{1,0:T(8,128)(2,1)} %get-tuple-element.290.q_ref, bf16[2048,128]{1,0:T(8,128)(2,1)} %get-tuple-element.282.k_ref, bf16[2048,128]{1,0:T(8,128)(2,1)} %get-tuple-element.281.v_ref, f32[1,2,3072]{2,1,0:T(2,128)} %get-tuple-element.297.line_ref), custom_call_target="tpu_custom_call" | custom-call | flops 4294967296 | bytes 2097152 | tf_op jit(solution)/shard_map/pallas_call | solution.py:91
  166.2 22.6 %all-gather.13.cloned.1.call-done = bf16[1024,512]{1,0:T(8,128)(2,1)} async-done(((bf16[1024,128]{1,0:T(8,128)(2,1)}), bf16[1024,512]{1,0:T(8,128)(2,1)}) %all-gather.13.cloned.1.call-update) | async-done | bytes 1048592 | tf_op jit(solution)/shard_map/all_gather | solution.py:399
  222.1 8.5 fusion.198
  230.6 37.0 %all-to-all-done.2 = bf16[8,320,1024]{2,1,0:T(8,128)(2,1)} async-done(((bf16[8,320,1024]{2,1,0:T(8,128)(2,1)}), bf16[8,320,1024]{2,1,0:T(8,128)(2,1)}, u32[]{:S(2)}, u32[]{:S(2)}) %all-to-all-start.2) | async-done | bytes 5242912 | tf_op jit(solution)/shard_map/all_to_all | solution.py:266
  267.6 14.7 %fusion.24 = f32[2560,2,704]{0,2,1:T(8,128)} fusion(bf16[2560,1024]{1,0:T(8,128)(2,1)} %bitcast.31, f32[1,1024,2,704]{1,3,2,0:T(8,128)} %param.31), kind=kOutput, calls=%fused_computation.56 | convolution fusion | flops 7383416832 | bytes 25427968 | tf_op jit(solution)/shard_map/sd,dgf->sgf/dot_general | solution.py:416
  286.5 13.2 %fusion.45 = f32[704,1024]{1,0:T(8,128)} fusion(bf16[2560,1024]{1,0:T(8,128)(2,1)} %bitcast.28, f32[2560]{0:T(1024)S(1)} %add_divide_fusion, f32[2560,2,704]{0,2,1:T(8,128)} %fusion.24), kind=kOutput, calls=%fused_computation.83 | convolution fusion | flops 3710812160 | bytes 22554624 | tf_op jit(solution)/shard_map/dot_general | solution.py:39
  299.7 11.6 %multiply_bitcast_fusion = (f32[2560,1,704]{0,2,1:T(8,128)S(1)}, f32[2560,1,704]{0,2,1:T(8,128)}, f32[2560]{0:T(1024)S(1)}) fusion(f32[2560,704]{0,1:T(8,128)S(1)} %bitcast.334, f32[2560]{0:T(1024)S(1)} %add_divide_fusion, f32[2560,2,704]{0,2,1:T(8,128)} %fusion.24), kind=kLoop, calls=%fused_computation.43 | loop fusion | flops 46855680 | bytes 36065280 | tf_op jit(solution)/shard_map/transpose(jvp())/broadcast_in_dim | solution.py:240
  311.3 15.9 %fusion.49 = f32[2560,1024,1]{1,0,2:T(8,128)} fusion(f32[1,1024,2,704]{1,3,2,0:T(8,128)S(1)} %bitcast.322, f32[2560,1,704]{0,2,1:T(8,128)} %get-tuple-element.271, f32[2560,1,704]{0,2,1:T(8,128)S(1)} %get-tuple-element.270), kind=kOutput, calls=%fused_computation.88 | convolution fusion | flops 7390625792 | bytes 30670848 | tf_op jit(solution)/shard_map/sgf,dgf->sd/dot_general | solution.py:423
  339.8 8.7 multiply_reduce_fusion.6
  376.5 13.6 %fusion.22 = f32[1024,2,704]{0,2,1:T(8,128)} fusion(bf16[2560,1024]{1,0:T(8,128)(2,1)} %bitcast.31, f32[2560,1,704]{0,2,1:T(8,128)} %get-tuple-element.271, f32[2560,1,704]{0,2,1:T(8,128)S(1)} %bitcast.332), kind=kOutput, calls=%fused_computation.54 | convolution fusion | flops 7389184000 | bytes 25427968 | tf_op jit(solution)/shard_map/sd,sgf->dgf/dot_general | solution.py:434
  390.1 9.2 %all-to-all-done.3 = bf16[8,320,1024]{2,1,0:T(8,128)(2,1)} async-done(((bf16[8,320,1024]{2,1,0:T(8,128)(2,1)}), bf16[8,320,1024]{2,1,0:T(8,128)(2,1)}, u32[]{:S(2)}, u32[]{:S(2)}) %all-to-all-start.3) | async-done | bytes 5242912 | tf_op jit(solution)/shard_map/all_to_all | solution.py:266
  402.4 15.7 %multiply_reduce_fusion.1 = (f32[]{:T(128)}, f32[1024,1408]{1,0:T(8,128)}) fusion(f32[2,1408,1408]{2,1,0:T(8,128)} %param.38, bf16[1024,1408]{0,1:T(8,128)(2,1)S(1)} %bitcast.345, f32[2,1024,1024]{2,1,0:T(8,128)} %param.37), kind=kOutput, calls=%fused_computation.47 | convolution fusion | flops 7017201664 | bytes 14712836 | tf_op jit(solution)/shard_map/dot_general | solution.py:35
  423.6 9.8 %fusion.65 = bf16[1024,1024]{0,1:T(8,128)(2,1)} fusion(bf16[2560,1024]{1,0:T(8,128)(2,1)} %bitcast.41, s32[1024]{0:T(1024)S(1)} %bitcast.379, s32[1024]{0:T(1024)S(1)} %bitcast.374), kind=kOutput, calls=%fused_computation.108 | convolution fusion | flops 5377622016 | bytes 7348224 | tf_op jit(solution)/shard_map/dot_general | solution.py:39
  454.7 65.8 %all-reduce.9.cloned.1.call-done = bf16[1024,1024]{0,1:T(8,128)(2,1)} async-done(((bf16[1024,1024]{0,1:T(8,128)(2,1)}), bf16[1024,1024]{0,1:T(8,128)(2,1)}) %all-reduce.9.cloned.1.call-update) | async-done | bytes 2097168 | tf_op jit(solution)/shard_map/psum | solution.py:440
  524.5 9.7 %fusion.68 = bf16[1024,1024]{0,1:T(8,128)(2,1)} fusion(bf16[2560,1024]{1,0:T(8,128)(2,1)} %bitcast.56, s32[1024]{0:T(1024)S(1)} %bitcast.380, s32[1024]{0:T(1024)S(1)} %bitcast.375), kind=kOutput, calls=%fused_computation.109 | convolution fusion | flops 5377622016 | bytes 7348224 | tf_op jit(solution)/shard_map/dot_general | solution.py:39
  568.0 52.2 %all-reduce.11.cloned.1.call-done = bf16[1024,1024]{0,1:T(8,128)(2,1)} async-done(((bf16[1024,1024]{0,1:T(8,128)(2,1)}), bf16[1024,1024]{0,1:T(8,128)(2,1)}) %all-reduce.11.cloned.1.call-update) | async-done | bytes 2097168 | tf_op jit(solution)/shard_map/psum | solution.py:453
  629.5 22.3 %shard_map.423 = (bf16[1024,128]{1,0:T(8,128)(2,1)}, f32[2048,128]{1,0:T(8,128)}, f32[2048,128]{1,0:T(8,128)}, f32[1,2,3072]{2,1,0:T(2,128)}) custom-call(bf16[1024,128]{1,0:T(8,128)(2,1)} %get-tuple-element.289.q_ref, bf16[2048,128]{1,0:T(8,128)(2,1)} %get-tuple-element.280.k_ref, bf16[2048,128]{1,0:T(8,128)(2,1)} %get-tuple-element.279.v_ref, ...), custom_call_target="tpu_custom_call" | custom-call | flops 10737418240 | bytes 6291456 | tf_op jit(solution)/shard_map/pallas_call | solution.py:202
  659.1 22.0 %shard_map.424 = (bf16[1024,128]{1,0:T(8,128)(2,1)}, f32[2048,128]{1,0:T(8,128)}, f32[2048,128]{1,0:T(8,128)}, f32[1,2,3072]{2,1,0:T(2,128)}) custom-call(bf16[1024,128]{1,0:T(8,128)(2,1)} %get-tuple-element.290.q_ref, bf16[2048,128]{1,0:T(8,128)(2,1)} %get-tuple-element.282.k_ref, bf16[2048,128]{1,0:T(8,128)(2,1)} %get-tuple-element.281.v_ref, ...), custom_call_target="tpu_custom_call" | custom-call | flops 10737418240 | bytes 6291456 | tf_op jit(solution)/shard_map/pallas_call | solution.py:202
  760.6 63.9 %all-reduce.13.cloned.1.call-done = bf16[1024,1024]{0,1:T(8,128)(2,1)} async-done(((bf16[1024,1024]{0,1:T(8,128)(2,1)}), bf16[1024,1024]{0,1:T(8,128)(2,1)}) %all-reduce.13.cloned.1.call-update) | async-done | bytes 2097168 | tf_op jit(solution)/shard_map/psum | solution.py:491
  827.9 39.5 %psum.31 = f32[88,128]{1,0:T(8,128)S(1)} all-reduce(f32[88,128]{1,0:T(8,128)S(1)} %fusion.121), channel_id=1, replica_groups=mesh['fsdp'=4,'ctx'=2,'tp'=4] {'fsdp','ctx','tp'}, use_global_device_ids=true, to_apply=%region_24.25 | all-reduce | flops 11264 | bytes 90112 | tf_op jit(solution)/shard_map/psum | solution.py:536
  (374 shorter events, 344.5 us)
Async XLA Ops:
  7.2 55.6 %all-gather.15.cloned.1.call-start = ((), (), s32[]{:S(2)}) async-start(), calls=%async_computation.16 | async-start | bytes 1843200 | tf_op jit(solution)/shard_map/all_gather | solution.py:317
  28.5 129.0 %copy-start.5 = (bf16[256,1024]{1,0:T(8,128)(2,1)}, bf16[256,1024]{1,0:T(8,128)(2,1)S(1)}, u32[]{:S(2)}) copy-start(bf16[256,1024]{1,0:T(8,128)(2,1)S(1)} %all_gather.25) | copy-start | bytes 1572868
  28.5 104.4 %collective-permute-start = (bf16[256,1024]{1,0:T(8,128)(2,1)S(1)}, bf16[256,1024]{1,0:T(8,128)(2,1)S(1)}, u32[]{:S(2)}, u32[]{:S(2)}) collective-permute-start(bf16[256,1024]{1,0:T(8,128)(2,1)S(1)} %all_gather.25), channel_id=1, source_target_pairs={{0,3},{1,0},{2,1},{3,2},{4,7},{5,4},{6,5},{7,6},{8,11},{9,8},{10,9... | collective-permute-start | bytes 1572872 | tf_op jit(solution)/shard_map/ppermute | solution.py:380
  32.1 101.6 %collective-permute-start.1 = (bf16[256,1024]{1,0:T(8,128)(2,1)S(1)}, bf16[256,1024]{1,0:T(8,128)(2,1)}, u32[]{:S(2)}, u32[]{:S(2)}) collective-permute-start(bf16[256,1024]{1,0:T(8,128)(2,1)S(1)} %all_gather.25), channel_id=1, source_target_pairs={{0,2},{1,3},{2,0},{3,1},{4,6},{5,7},{6,4},{7,5},{8,10},{9,11},{10,... | collective-permute-start | bytes 1572872 | tf_op jit(solution)/shard_map/ppermute | solution.py:380
  37.0 65.4 %all-gather.7.cloned.1.call-start = ((), (), s32[]{:S(2)}) async-start(), calls=%async_computation.9 | async-start | bytes 1572864 | tf_op jit(solution)/shard_map/all_gather | solution.py:391
  45.0 143.7 %copy-start = (bf16[1024,1024]{0,1:T(8,128)(2,1)}, bf16[1024,1024]{0,1:T(8,128)(2,1)S(1)}, u32[]{:S(2)}) copy-start(bf16[1024,1024]{0,1:T(8,128)(2,1)S(1)} %copy.177) | copy-start | bytes 6291460
  46.3 146.7 %copy-start.51 = (s32[1024,1]{0,1:T(1,128)}, s32[1024,1]{0,1:T(1,128)S(1)}, u32[]{:S(2)}) copy-start(s32[1024,1]{0,1:T(1,128)S(1)} %get-tuple-element.301) | copy-start | bytes 12292
  46.3 146.7 %copy-start.53 = (s32[1024,1]{0,1:T(1,128)}, s32[1024,1]{0,1:T(1,128)S(1)}, u32[]{:S(2)}) copy-start(s32[1024,1]{0,1:T(1,128)S(1)} %get-tuple-element.302) | copy-start | bytes 12292
  80.9 54.7 %all-gather.11.cloned.1.call-start = ((), (), s32[]{:S(2)}) async-start(), calls=%async_computation.11 | async-start | bytes 1572864 | tf_op jit(solution)/shard_map/all_gather | solution.py:391
  83.8 77.5 %all-gather.9.cloned.1.call-start = ((), (), s32[]{:S(2)}) async-start(), calls=%async_computation.10 | async-start | bytes 1310720 | tf_op jit(solution)/shard_map/all_gather | solution.py:399
  119.9 8.0 all-to-all-start.1
  123.2 27.0 %collective-permute-start.2 = (bf16[256,1024]{1,0:T(8,128)(2,1)S(1)}, bf16[256,1024]{1,0:T(8,128)(2,1)}, u32[]{:S(2)}, u32[]{:S(2)}) collective-permute-start(bf16[256,1024]{1,0:T(8,128)(2,1)S(1)} %all_gather.25), channel_id=1, source_target_pairs={{0,1},{1,2},{2,3},{3,0},{4,5},{5,6},{6,7},{7,4},{8,9},{9,10},{10,1... | collective-permute-start | bytes 1572872 | tf_op jit(solution)/shard_map/ppermute | solution.py:380
  127.8 75.0 %all-to-all-start = ((bf16[8,320,1024]{2,1,0:T(8,128)(2,1)}), bf16[8,320,1024]{2,1,0:T(8,128)(2,1)}, u32[]{:S(2)}, u32[]{:S(2)}) async-start(bf16[8,320,1024]{2,1,0:T(8,128)(2,1)} %bitcast.340), calls=%async_computation | async-start | bytes 10485760 | tf_op jit(solution)/shard_map/all_to_all | solution.py:266
  132.5 56.2 %all-gather.13.cloned.1.call-start = ((), (), s32[]{:S(2)}) async-start(), calls=%async_computation.12 | async-start | bytes 1310720 | tf_op jit(solution)/shard_map/all_gather | solution.py:399
  202.9 64.7 %all-to-all-start.2 = ((bf16[8,320,1024]{2,1,0:T(8,128)(2,1)}), bf16[8,320,1024]{2,1,0:T(8,128)(2,1)}, u32[]{:S(2)}, u32[]{:S(2)}) async-start(bf16[8,320,1024]{2,1,0:T(8,128)(2,1)} %bitcast.342), calls=%async_computation.2 | async-start | bytes 10485760 | tf_op jit(solution)/shard_map/all_to_all | solution.py:266
  335.1 64.1 %all-to-all-start.3 = ((bf16[8,320,1024]{2,1,0:T(8,128)(2,1)}), bf16[8,320,1024]{2,1,0:T(8,128)(2,1)}, u32[]{:S(2)}, u32[]{:S(2)}) async-start(bf16[8,320,1024]{2,1,0:T(8,128)(2,1)} %bitcast.323), calls=%async_computation.3 | async-start | bytes 10485760 | tf_op jit(solution)/shard_map/all_to_all | solution.py:266
  418.8 105.7 %all-to-all-start.4 = ((bf16[8,320,1024]{2,1,0:T(8,128)(2,1)}), bf16[8,320,1024]{2,1,0:T(8,128)(2,1)}, u32[]{:S(2)}, u32[]{:S(2)}) async-start(bf16[8,320,1024]{2,1,0:T(8,128)(2,1)} %bitcast.341), calls=%async_computation.4 | async-start | bytes 10485760 | tf_op jit(solution)/shard_map/all_to_all | solution.py:266
  423.5 97.0 %all-reduce.9.cloned.1.call-start = ((), (), s32[]{:S(2)}) async-start(), calls=%async_computation.13 | async-start | bytes 4194304 | tf_op jit(solution)/shard_map/psum | solution.py:440
  433.4 186.8 %all-reduce.11.cloned.1.call-start = ((), (), s32[]{:S(2)}) async-start(), calls=%async_computation.14 | async-start | bytes 4194304 | tf_op jit(solution)/shard_map/psum | solution.py:453
  655.5 36.9 %all-to-all-start.5 = ((bf16[2,1024,256]{2,1,0:T(8,128)(2,1)}), bf16[2,1024,256]{2,1,0:T(8,128)(2,1)S(1)}, u32[]{:S(2)}, u32[]{:S(2)}) async-start(bf16[2,1024,256]{2,1,0:T(8,128)(2,1)} %pad_maximum_fusion.1), calls=%async_computation.5 | async-start | bytes 2097152 | tf_op jit(solution)/shard_map/all_to_all | solution.py:475
  692.4 18.4 %all-to-all-start.6 = ((bf16[2,1024,256]{2,1,0:T(8,128)(2,1)}), bf16[2,1024,256]{2,1,0:T(8,128)(2,1)}, u32[]{:S(2)}, u32[]{:S(2)}) async-start(bf16[2,1024,256]{2,1,0:T(8,128)(2,1)} %pad_maximum_fusion.2), calls=%async_computation.6 | async-start | bytes 2097152 | tf_op jit(solution)/shard_map/all_to_all | solution.py:475
  710.8 17.6 %all-to-all-start.8 = ((bf16[8,256,128]{2,1,0:T(8,128)(2,1)}), bf16[8,256,128]{2,1,0:T(8,128)(2,1)S(1)}, u32[]{:S(2)}, u32[]{:S(2)}) async-start(bf16[8,256,128]{2,1,0:T(8,128)(2,1)} %bitcast.347), calls=%async_computation.8 | async-start | bytes 1048576 | tf_op jit(solution)/shard_map/all_to_all | solution.py:505
  728.4 24.5 %all-to-all-start.7 = ((bf16[8,128,768]{1,2,0:T(8,128)(2,1)}), bf16[8,128,768]{1,2,0:T(8,128)(2,1)}, u32[]{:S(2)}, u32[]{:S(2)}) async-start(bf16[8,128,768]{1,2,0:T(8,128)(2,1)} %copy.190), calls=%async_computation.7 | async-start | bytes 3145728 | tf_op jit(solution)/shard_map/all_to_all | solution.py:495
  732.7 91.8 %all-reduce.13.cloned.1.call-start = ((), (), s32[]{:S(2)}) async-start(), calls=%async_computation.15 | async-start | bytes 4194304 | tf_op jit(solution)/shard_map/psum | solution.py:491
  (75 other events, 1440.3 us)
Sparse Core Ops, SparseCore 0:
  37.2 25.6 all-gather.14
  81.0 21.2 all-gather.6
  104.5 21.2 all-gather.10
  127.8 29.2 all-gather.8
  158.5 30.1 all-gather.12
  433.5 86.9 all-reduce.8
  534.4 85.7 all-reduce.10
  738.4 86.1 all-reduce.12

commit v2 on v1

--- a/solution.py
+++ b/solution.py
@@ -116,20 +116,284 @@
     )(query, keys, values, lines)
 
 
-def attend_back_kernel(length, rows, tile, chunk, q_ref, k_ref, v_ref, g_ref, m_ref, log_ref, line_ref, dq_ref, dk_ref, dv_ref, sums_ref, strip, gather):
+def remote(source, target, send, receive, where):
+    return pltpu.make_async_remote_copy(
+        src_ref=source,
+        dst_ref=target,
+        send_sem=send,
+        recv_sem=receive,
+        device_id=where,
+        device_id_type=pl.DeviceIdType.MESH,
+    )
+
+
+class LineSum:
+    lag = 3
+
+    def __init__(self, axis, count, size, pairs, own, left, right, stage, total, sems):
+        self.axis, self.count, self.size, self.pairs = axis, count, size, pairs
+        self.own, self.left, self.right, self.stage, self.total = own, left, right, stage, total
+        self.part_send, self.left_got, self.right_got, self.total_got, self.down_send, self.up_send = (
+            sems.at[0], sems.at[1], sems.at[2], sems.at[3], sems.at[4], sems.at[5],
+        )
+        self.owners = ((count - 1) // 2, count // 2)
+        self.reach = [max(owner, count - 1 - owner) for owner in self.owners]
+        self.steps = pairs + self.lag * 2 * max(self.reach)
+
+    @staticmethod
+    def scratch(rows, width, size):
+        return [pltpu.VMEM((rows, width), jnp.bfloat16)] * 4 + [
+            pltpu.SemaphoreType.DMA((6, rows // size))
+        ]
+
+    def signal_neighbours(self, barrier):
+        me = lax.axis_index(self.axis)
+        for offset, there in ((-1, me > 0), (1, me < self.count - 1)):
+
+            @pl.when(there)
+            def _():
+                pl.semaphore_signal(
+                    barrier,
+                    inc=1,
+                    device_id={self.axis: me + offset},
+                    device_id_type=pl.DeviceIdType.MESH,
+                )
+
+    def neighbours(self):
+        me = lax.axis_index(self.axis)
+        return jnp.where(me > 0, 1, 0) + jnp.where(me < self.count - 1, 1, 0)
+
+    def place(self, side, pair):
+        chunk = side * self.pairs + pair
+        return chunk, pl.ds(pl.multiple_of(chunk * self.size, self.size), self.size)
+
+    def part_up(self, chunk, rows):
+        me = lax.axis_index(self.axis)
+        return remote(
+            self.stage.at[rows], self.left.at[rows], self.part_send.at[chunk], self.left_got.at[chunk], {self.axis: me + 1}
+        )
+
+    def part_down(self, chunk, rows):
+        me = lax.axis_index(self.axis)
+        return remote(
+            self.stage.at[rows], self.right.at[rows], self.part_send.at[chunk], self.right_got.at[chunk], {self.axis: me - 1}
+        )
+
+    def total_up(self, chunk, rows):
+        me = lax.axis_index(self.axis)
+        return remote(
+            self.total.at[rows], self.total.at[rows], self.up_send.at[chunk], self.total_got.at[chunk], {self.axis: me + 1}
+        )
+
+    def total_down(self, chunk, rows):
+        me = lax.axis_index(self.axis)
+        return remote(
+            self.total.at[rows], self.total.at[rows], self.down_send.at[chunk], self.total_got.at[chunk], {self.axis: me - 1}
+        )
+
+    def arrived(self, target, rows, got):
+        me = lax.axis_index(self.axis)
+        peer = jnp.where(me < self.count - 1, me + 1, me - 1)
+        remote(target.at[rows], target.at[rows], got, got, {self.axis: peer}).wait_recv()
+
+    def step(self, number):
+        me = lax.axis_index(self.axis)
+        last = self.count - 1
+        wide = jnp.float32
+        for side, owner in enumerate(self.owners):
+            reach = self.reach[side]
+            from_end = jnp.where(me < owner, me, jnp.where(me > owner, last - me, reach))
+            pair = number - self.lag * from_end
+            chunk, rows = self.place(side, pair)
+            inside = (pair >= 0) & (pair < self.pairs)
+
+            @pl.when(inside & (me == 0) & (me < owner))
+            def _():
+                self.stage[rows, :] = self.own[rows, :]
+                self.part_up(chunk, rows).start()
+
+            @pl.when(inside & (me > 0) & (me < owner))
+            def _():
+                self.arrived(self.left, rows, self.left_got.at[chunk])
+                self.stage[rows, :] = (self.own[rows, :].astype(wide) + self.left[rows, :].astype(wide)).astype(jnp.bfloat16)
+                self.part_up(chunk, rows).start()
+
+            @pl.when(inside & (me == last) & (me > owner))
+            def _():
+                self.stage[rows, :] = self.own[rows, :]
+                self.part_down(chunk, rows).start()
+
+            @pl.when(inside & (me < last) & (me > owner))
+            def _():
+                self.arrived(self.right, rows, self.right_got.at[chunk])
+                self.stage[rows, :] = (self.own[rows, :].astype(wide) + self.right[rows, :].astype(wide)).astype(jnp.bfloat16)
+                self.part_down(chunk, rows).start()
+
+            @pl.when(inside & (me == owner))
+            def _():
+                value = self.own[rows, :].astype(wide)
+                if owner > 0:
+                    self.arrived(self.left, rows, self.left_got.at[chunk])
+                    value = value + self.left[rows, :].astype(wide)
+                if owner < last:
+                    self.arrived(self.right, rows, self.right_got.at[chunk])
+                    value = value + self.right[rows, :].astype(wide)
+                self.total[rows, :] = value.astype(jnp.bfloat16)
+                if owner > 0:
+                    self.total_down(chunk, rows).start()
+                if owner < last:
+                    self.total_up(chunk, rows).start()
+
+            away = jnp.where(me < owner, owner - me, me - owner)
+            pair = number - self.lag * (reach + away)
+            chunk, rows = self.place(side, pair)
+            inside = (pair >= 0) & (pair < self.pairs) & (me != owner)
+
+            @pl.when(inside)
+            def _():
+                self.arrived(self.total, rows, self.total_got.at[chunk])
+
+            @pl.when(inside & (me < owner) & (me > 0))
+            def _():
+                self.total_down(chunk, rows).start()
+
+            @pl.when(inside & (me > owner) & (me < last))
+            def _():
+                self.total_up(chunk, rows).start()
+
+    def finish(self):
+        me = lax.axis_index(self.axis)
+        last = self.count - 1
+        for side, owner in enumerate(self.owners):
+
+            def one(pair, carry):
+                chunk, rows = self.place(side, pair)
+
+                @pl.when(me < owner)
+                def _():
+                    self.part_up(chunk, rows).wait_send()
+
+                @pl.when(me > owner)
+                def _():
+                    self.part_down(chunk, rows).wait_send()
+
+                @pl.when((me <= owner) & (me > 0))
+                def _():
+                    self.total_down(chunk, rows).wait_send()
+
+                @pl.when((me >= owner) & (me < last))
+                def _():
+                    self.total_up(chunk, rows).wait_send()
+
+                return carry
+
+            lax.fori_loop(0, self.pairs, one, 0)
+
+
+SUM_ROWS = 16
+
+
+def combine_sum_kernel(count, slots_ref, back_ref, out_ref, own, left, right, stage, total, sems):
+    rows, width = own.shape
+    places = back_ref.shape[0]
+    line = LineSum("tp", count, SUM_ROWS, rows // SUM_ROWS // 2, own, left, right, stage, total, sems)
+    barrier = pltpu.get_barrier_semaphore()
+    line.signal_neighbours(barrier)
+    size, depth = 256, 512
+
+    def one(number, carry):
+        spot = pl.ds(pl.multiple_of(number * size, size), size)
+        slots = slots_ref[spot, :]
+        value = jnp.zeros((size, width), jnp.float32)
+        for start in range(0, places, depth):
+            lane = lax.broadcasted_iota(jnp.int32, (size, depth), 1) + start
+            hit = (lane == slots[:, 0:1]) | (lane == slots[:, 1:2])
+            value = value + dot_nn(
+                jnp.where(hit, 1.0, 0.0).astype(jnp.bfloat16), back_ref[start : start + depth, :]
+            )
+        own[spot, :] = value.astype(jnp.bfloat16)
+        return carry
+
+    lax.fori_loop(0, rows // size, one, 0)
+    pl.semaphore_wait(barrier, line.neighbours())
+
+    def step(number, carry):
+        line.step(number)
+        return carry
+
+    lax.fori_loop(0, line.steps, step, 0)
+    out_ref[...] = total[...]
+    line.finish()
+
+
+def combine_sum(slots, back, rows):
+    width = back.shape[1]
+    vmem = pl.BlockSpec(memory_space=pltpu.VMEM)
+    return pl.pallas_call(
+        functools.partial(combine_sum_kernel, lax.axis_size("tp")),
+        out_shape=jax.ShapeDtypeStruct((rows, width), jnp.bfloat16),
+        in_specs=[vmem, vmem],
+        out_specs=vmem,
+        scratch_shapes=[pltpu.VMEM((rows, width), jnp.bfloat16)] + LineSum.scratch(rows, width, SUM_ROWS),
+        compiler_params=pltpu.CompilerParams(
+            collective_id=0, has_side_effects=True, vmem_limit_bytes=48 * MIB
+        ),
+        cost_estimate=pl.CostEstimate(
+            flops=2 * rows * back.shape[0] * width, bytes_accessed=200 * rows * width, transcendentals=0
+        ),
+    )(slots, back)
+
+
+def attend_back_kernel(length, rows, tile, chunk, n_pairs_all, n_ctx, n_tp, q_ref, k_ref, v_ref, g_ref, m_ref, log_ref, line_ref, part_ref, dq_ref, dkv_ref, sums_ref, total_ref, strip, gather, dk_ref, dv_ref, mine_ref, got_ref, swap_send, swap_got, left, right, stage, total, sems):
+    pair = pl.program_id(0)
     step = pl.program_id(1)
-    steps = pl.num_programs(1)
+    n_pairs = n_pairs_all
+    steps = rows // tile
     span = line_ref.shape[2]
     last = length // LANES - 1
+    here = lax.axis_index("ctx")
+    turn = pair * steps + step
+    line_sum = LineSum("tp", n_tp, SUM_ROWS, part_ref.shape[0] // SUM_ROWS // 2, part_ref, left, right, stage, total, sems)
+    barrier = pltpu.get_barrier_semaphore()
+
+    def swap(slot, peer):
+        return remote(
+            mine_ref.at[peer], got_ref.at[slot, here], swap_send.at[slot, peer], swap_got.at[slot, here], {"ctx": peer}
+        )
+
+    def arrival(slot, peer):
+        return remote(
+            mine_ref.at[peer], got_ref.at[slot, peer], swap_send.at[slot, peer], swap_got.at[slot, peer], {"ctx": peer}
+        )
+
+    @pl.when(turn == 0)
+    def _():
+        line_sum.signal_neighbours(barrier)
+        for peer in range(n_ctx):
+
+            @pl.when(peer != here)
+            def _():
+                pl.semaphore_signal(
+                    barrier, inc=1, device_id={"ctx": peer}, device_id_type=pl.DeviceIdType.MESH
+                )
+
+        pl.semaphore_wait(barrier, line_sum.neighbours() + (n_ctx - 1))
 
     @pl.when(step == 0)
     def _():
         for half in range(2):
             line = jnp.broadcast_to(line_ref[0, half : half + 1, :], (LANES, span))
-            strip[half] = pltpu.roll(line, span - LANES, 1, stride=1, stride_axis=0)
+            strip[half] = pltpu.roll(line, span - LANES, 1, stride=1, stride_axis=0).astype(strip.dtype)
         gather[...] = jnp.zeros_like(gather)
         dk_ref[...] = jnp.zeros_like(dk_ref)
         dv_ref[...] = jnp.zeros_like(dv_ref)
+
+    chunks = length // chunk
+    turns = n_pairs_all * steps * chunks
+
+    def sum_step(number, carry):
+        line_sum.step(number)
+        return carry
 
     query = q_ref[...]
     grad = g_ref[...]
@@ -147,6 +411,8 @@
 
     def one_chunk(number, carry):
         outs = []
+        now = turn * chunks + number
+        lax.fori_loop(now * line_sum.steps // turns, (now + 1) * line_sum.steps // turns, sum_step, 0)
         base = pl.multiple_of(number * chunk, chunk)
         keys = k_ref[pl.ds(base, chunk), :]
         values = v_ref[pl.ds(base, chunk), :]
@@ -160,7 +426,7 @@
                 row_group = number * (chunk // LANES) + group
                 start = pl.multiple_of((last - row_group) * LANES + step * tile, LANES)
                 places.append(start)
-                bias.append(strip[half, :, pl.ds(start, tile)])
+                bias.append(strip[half, :, pl.ds(start, tile)].astype(jnp.float32))
             bias = jnp.concatenate(bias, 0) if len(bias) > 1 else bias[0]
             shares = jnp.exp(logit + bias - logs[half])
             grad_shares = dot_nt(values, grads[half])
@@ -183,6 +449,21 @@
 
     @pl.when(step == steps - 1)
     def _():
+        for peer in range(n_ctx):
+            spot = slice(peer * rows, (peer + 1) * rows)
+
+            @pl.when((peer != here) & (pair > 0))
+            def _():
+                swap(pair - 1, peer).wait_send()
+
+            mine_ref[peer, :, :LANES] = dk_ref[spot, :].astype(jnp.bfloat16)
+            mine_ref[peer, :, LANES:] = dv_ref[spot, :].astype(jnp.bfloat16)
+
+            @pl.when(peer != here)
+            def _():
+                swap(pair, peer).start()
+
+        got_ref[pair, here] = mine_ref[here]
         for half in range(2):
             values = gather[half]
             size = LANES // 2
@@ -191,45 +472,309 @@
                 size //= 2
             sums_ref[0, half : half + 1, :] = pltpu.roll(jnp.broadcast_to(values, (8, span)), LANES, 1)[0:1]
 
-
-def attend_back(query, keys, values, grad, mixed, logs, lines):
+    @pl.when((step == steps - 1) & (pair == n_pairs - 1))
+    def _():
+        total_ref[...] = total[...]
+        for slot in range(2):
+            for peer in range(n_ctx):
+
+                @pl.when(peer != here)
+                def _():
+                    arrival(slot, peer).wait_recv()
+
+            value = got_ref[slot, 0].astype(jnp.float32)
+            for peer in range(1, n_ctx):
+                value = value + got_ref[slot, peer].astype(jnp.float32)
+            dkv_ref[slot] = value.astype(jnp.bfloat16)
+        for peer in range(n_ctx):
+
+            @pl.when(peer != here)
+            def _():
+                swap(1, peer).wait_send()
+
+        line_sum.finish()
+
+
+def attend_back(query, key_value, grad, mixed, logs, lines, part):
     rows, cols = query.shape
-    length = keys.shape[0]
+    length = key_value.shape[2]
     pairs = cols // LANES
+    depth = 2 if length <= 4096 else 1
+    n_ctx = lax.axis_size("ctx")
     tile = 256
     chunk = 512
     span = lines.shape[2]
+    width = part.shape[1]
     return pl.pallas_call(
-        functools.partial(attend_back_kernel, length, rows, tile, chunk),
+        functools.partial(attend_back_kernel, length, rows, tile, chunk, pairs, n_ctx, lax.axis_size("tp")),
         grid=(pairs, rows // tile),
         in_specs=[
             pl.BlockSpec((tile, LANES), lambda p, t: (t, p)),
-            pl.BlockSpec((length, LANES), lambda p, t: (0, p)),
-            pl.BlockSpec((length, LANES), lambda p, t: (0, p)),
+            pl.BlockSpec((None, None, length, LANES), lambda p, t: (p, 0, 0, 0), pipeline_mode=pl.Buffered(depth)),
+            pl.BlockSpec((None, None, length, LANES), lambda p, t: (p, 1, 0, 0), pipeline_mode=pl.Buffered(depth)),
             pl.BlockSpec((tile, LANES), lambda p, t: (t, p)),
             pl.BlockSpec((tile, LANES), lambda p, t: (t, p)),
             pl.BlockSpec((1, 2, tile), lambda p, t: (p, 0, t)),
             pl.BlockSpec((1, 2, span), lambda p, t: (p, 0, 0)),
+            pl.BlockSpec(memory_space=pltpu.VMEM),
         ],
         out_specs=[
             pl.BlockSpec((tile, LANES), lambda p, t: (t, p)),
-            pl.BlockSpec((length, LANES), lambda p, t: (0, p)),
-            pl.BlockSpec((length, LANES), lambda p, t: (0, p)),
+            pl.BlockSpec(memory_space=pltpu.VMEM),
             pl.BlockSpec((1, 2, span), lambda p, t: (p, 0, 0)),
+            pl.BlockSpec(memory_space=pltpu.VMEM),
         ],
         out_shape=[
             jax.ShapeDtypeStruct((rows, cols), jnp.bfloat16),
-            jax.ShapeDtypeStruct((length, cols), jnp.float32),
-            jax.ShapeDtypeStruct((length, cols), jnp.float32),
+            jax.ShapeDtypeStruct((pairs, rows, 2 * LANES), jnp.bfloat16),
             jax.ShapeDtypeStruct((pairs, 2, span), jnp.float32),
+            jax.ShapeDtypeStruct((rows, width), jnp.bfloat16),
         ],
         scratch_shapes=[
+            pltpu.VMEM((2, LANES, span), jnp.float32 if length <= 4096 else jnp.bfloat16),
             pltpu.VMEM((2, LANES, span), jnp.float32),
-            pltpu.VMEM((2, LANES, span), jnp.float32),
+            pltpu.VMEM((length, LANES), jnp.float32),
+            pltpu.VMEM((length, LANES), jnp.float32),
+            pltpu.VMEM((n_ctx, rows, 2 * LANES), jnp.bfloat16),
+            pltpu.VMEM((pairs, n_ctx, rows, 2 * LANES), jnp.bfloat16),
+            pltpu.SemaphoreType.DMA((pairs, n_ctx)),
+            pltpu.SemaphoreType.DMA((pairs, n_ctx)),
+        ]
+        + LineSum.scratch(rows, width, SUM_ROWS),
+        compiler_params=pltpu.CompilerParams(
+            collective_id=1, has_side_effects=True, vmem_limit_bytes=60 * MIB
+        ),
+        cost_estimate=pl.CostEstimate(flops=40 * rows * length * cols, bytes_accessed=24 * length * cols, transcendentals=rows * length * cols // DH),
+    )(query, key_value, key_value, grad, mixed, logs, lines, part)
+
+
+def greet(barrier, me, peers):
+    for number, where in peers:
+
+        @pl.when(number != me)
+        def _():
+            pl.semaphore_signal(
+                barrier, inc=1, device_id=where, device_id_type=pl.DeviceIdType.MESH
+            )
+
+
+def tail_kernel(
+    n_fsdp,
+    n_ctx,
+    n_tp,
+    blocks,
+    sum_rows,
+    part_ref,
+    small_ref,
+    grad_ref,
+    scale_ref,
+    s_right,
+    p_right,
+    s_left,
+    p_left,
+    w_ref,
+    new_right,
+    new_left,
+    new_w,
+    total_ref,
+    small_out,
+    turned,
+    direction,
+    squares,
+    plane_got,
+    line_got,
+    line_own,
+    plane_send,
+    plane_sem,
+    tp_send,
+    tp_sem,
+    left,
+    right,
+    stage,
+    total,
+    sems,
+):
+    turn = pl.program_id(0)
+    turns = pl.num_programs(0)
+    rights, lefts = blocks
+    line = LineSum("tp", n_tp, SUM_ROWS, part_ref.shape[0] // SUM_ROWS // 2, part_ref, left, right, stage, total, sems)
+    here = lax.axis_index("fsdp") * n_ctx + lax.axis_index("ctx")
+    tp_here = lax.axis_index("tp")
+    shards = n_fsdp * n_ctx
+    plane = [(f * n_ctx + c, {"fsdp": f, "ctx": c}) for f in range(n_fsdp) for c in range(n_ctx)]
+    column = [(t, {"tp": t}) for t in range(n_tp)]
+    other = jnp.where(here == 0, 1, 0)
+    other_where = {"fsdp": other // n_ctx, "ctx": other % n_ctx}
+    other_tp = {"tp": jnp.where(tp_here == 0, 1, 0)}
+    middle = rights + 2
+
+    def plane_copy(number, where):
+        return remote(small_ref.at[number], plane_got.at[here], plane_send.at[number], plane_sem.at[here], where)
+
+    def tp_copy(number, where):
+        return remote(line_own, line_got.at[tp_here], tp_send.at[number], tp_sem.at[tp_here], where)
+
+    @pl.when(turn == 0)
+    def _():
+        barrier = pltpu.get_barrier_semaphore()
+        greet(barrier, here, plane)
+        greet(barrier, tp_here, column)
+        squares[...] = jnp.zeros_like(squares)
+        pl.semaphore_wait(barrier, shards - 1 + n_tp - 1)
+        for number, where in plane:
+
+            @pl.when(number != here)
+            def _():
+                plane_copy(number, where).start()
+
+        plane_got[here] = small_ref[here]
+
+    @pl.when(turn == middle)
+    def _():
+        for number, where in plane:
+
+            @pl.when(number != here)
+            def _():
+                remote(plane_got.at[number], plane_got.at[number], plane_sem.at[number], plane_sem.at[number], other_where).wait_recv()
+
+        added = plane_got[0]
+        largest = plane_got[0]
+        for number in range(1, shards):
+            added = added + plane_got[number]
+            largest = jnp.maximum(largest, plane_got[number])
+        row = lax.broadcasted_iota(jnp.int32, added.shape, 0)
+        line_own[...] = jnp.where(row == sum_rows + 1, largest, added)
+        for number, where in column:
+
+            @pl.when(number != tp_here)
+            def _():
+                tp_copy(number, where).start()
+
+        line_got[tp_here] = line_own[...]
+
+    def one(number, carry):
+        line.step(number)
+        return carry
+
+    lax.fori_loop(turn * line.steps // turns, (turn + 1) * line.steps // turns, one, 0)
+
+    @pl.when(turn < rights)
+    def _():
+        spot = pl.ds(pl.multiple_of(turn * LANES, LANES), LANES)
+        grad = grad_ref[...]
+        new_right[...] = decay * s_right[...] + (1.0 - decay) * dot_nt(grad_ref[spot, :], grad)
+        turned[spot, :] = dot_nn(p_right[...].astype(jnp.bfloat16), grad).astype(jnp.bfloat16)
+
+    @pl.when((turn >= rights) & (turn < rights + lefts))
+    def _():
+        spot = pl.ds(pl.multiple_of((turn - rights) * LANES, LANES), LANES)
+        new_left[...] = decay * s_left[...] + (1.0 - decay) * dot_tn(grad_ref[:, spot], grad_ref[...])
+        value = dot_nn(turned[...], p_left[...].astype(jnp.bfloat16))
+        squares[...] = squares[...] + jnp.sum(value * value, 0, keepdims=True)
+        direction[:, spot] = value.astype(jnp.bfloat16)
+
+    @pl.when(turn >= rights + lefts)
+    def _():
+        spot = pl.ds(pl.multiple_of((turn - rights - lefts) * LANES, LANES), LANES)
+        mean = jnp.sum(squares[0:1, :], 1, keepdims=True) / (grad_ref.shape[0] * grad_ref.shape[1])
+        factor = scale_ref[0:1, 0:1] * lax.rsqrt(mean + step_epsilon)
+        new_w[...] = w_ref[...] - factor * direction[spot, :].astype(jnp.float32)
+
+    @pl.when(turn == turns - 1)
+    def _():
+        total_ref[...] = total[...]
+        for number, where in column:
+
+            @pl.when(number != tp_here)
+            def _():
+                remote(line_got.at[number], line_got.at[number], tp_sem.at[number], tp_sem.at[number], other_tp).wait_recv()
+
+        added = line_got[0]
+        for number in range(1, n_tp):
+            added = added + line_got[number]
+        row = lax.broadcasted_iota(jnp.int32, added.shape, 0)
+        small_out[...] = jnp.where(row < sum_rows, added, line_own[...])
+        for number, where in plane:
+
+            @pl.when(number != here)
+            def _():
+                plane_copy(number, where).wait_send()
+
+        for number, where in column:
+
+            @pl.when(number != tp_here)
+            def _():
+                tp_copy(number, where).wait_send()
+
+        line.finish()
+
+
+def tail(part, small, sum_rows, grad, scale, left, right, weight):
+    rows, width = part.shape
+    deep, wide = grad.shape
+    n_fsdp, n_ctx, n_tp = lax.axis_size("fsdp"), lax.axis_size("ctx"), lax.axis_size("tp")
+    rights, lefts = deep // LANES, wide // LANES
+    turns = 2 * rights + lefts
+    small_rows = small.shape[1]
+    vmem = pl.BlockSpec(memory_space=pltpu.VMEM)
+
+    def at_right(turn):
+        return jnp.minimum(turn, rights - 1)
+
+    def at_left(turn):
+        return jnp.clip(turn - rights, 0, lefts - 1)
+
+    def at_weight(turn):
+        return jnp.clip(turn - rights - lefts, 0, rights - 1)
+
+    return pl.pallas_call(
+        functools.partial(tail_kernel, n_fsdp, n_ctx, n_tp, (rights, lefts), sum_rows),
+        grid=(turns,),
+        in_specs=[
+            vmem,
+            vmem,
+            vmem,
+            vmem,
+            pl.BlockSpec((None, LANES, deep), lambda t: (0, at_right(t), 0)),
+            pl.BlockSpec((None, LANES, deep), lambda t: (1, at_right(t), 0)),
+            pl.BlockSpec((None, LANES, wide), lambda t: (0, at_left(t), 0)),
+            pl.BlockSpec((None, wide, LANES), lambda t: (1, 0, at_left(t))),
+            pl.BlockSpec((LANES, wide), lambda t: (at_weight(t), 0)),
         ],
-        compiler_params=pltpu.CompilerParams(vmem_limit_bytes=60 * MIB),
-        cost_estimate=pl.CostEstimate(flops=40 * rows * length * cols, bytes_accessed=24 * length * cols, transcendentals=rows * length * cols // DH),
-    )(query, keys, values, grad, mixed, logs, lines)
+        out_specs=[
+            pl.BlockSpec((LANES, deep), lambda t: (at_right(t), 0)),
+            pl.BlockSpec((LANES, wide), lambda t: (at_left(t), 0)),
+            pl.BlockSpec((LANES, wide), lambda t: (at_weight(t), 0)),
+            vmem,
+            vmem,
+        ],
+        out_shape=[
+            jax.ShapeDtypeStruct((deep, deep), jnp.float32),
+            jax.ShapeDtypeStruct((wide, wide), jnp.float32),
+            jax.ShapeDtypeStruct((deep, wide), jnp.float32),
+            jax.ShapeDtypeStruct((rows, width), jnp.bfloat16),
+            jax.ShapeDtypeStruct((small_rows, LANES), jnp.float32),
+        ],
+        scratch_shapes=[
+            pltpu.VMEM((deep, wide), jnp.bfloat16),
+            pltpu.VMEM((deep, wide), jnp.bfloat16),
+            pltpu.VMEM((1, LANES), jnp.float32),
+            pltpu.VMEM((n_fsdp * n_ctx, small_rows, LANES), jnp.float32),
+            pltpu.VMEM((n_tp, small_rows, LANES), jnp.float32),
+            pltpu.VMEM((small_rows, LANES), jnp.float32),
+            pltpu.SemaphoreType.DMA((n_fsdp * n_ctx,)),
+            pltpu.SemaphoreType.DMA((n_fsdp * n_ctx,)),
+            pltpu.SemaphoreType.DMA((n_tp,)),
+            pltpu.SemaphoreType.DMA((n_tp,)),
+        ]
+        + LineSum.scratch(rows, width, SUM_ROWS),
+        compiler_params=pltpu.CompilerParams(
+            collective_id=2, has_side_effects=True, vmem_limit_bytes=56 * MIB
+        ),
+        cost_estimate=pl.CostEstimate(
+            flops=8 * deep * wide * (deep + wide), bytes_accessed=240 * rows * width, transcendentals=0
+        ),
+    )(part, small, grad, scale, right, right, left, left, weight)
 
 
 def normalize(values, gain):
@@ -372,7 +917,10 @@
     lines = lax.dot_general(
         table_full, hits, (((0,), (1,)), ((), ())), preferred_element_type=jnp.float32
     ).reshape(head_pairs, 1, 2, span)
-    back_lines = lines[..., ::-1]
+    hits_back = (near[::-1][:, None] == jnp.arange(table_full.shape[0], dtype=jnp.int32)[None, :]).astype(low)
+    back_lines = lax.dot_general(
+        table_full, hits_back, (((0,), (1,)), ((), ())), preferred_element_type=jnp.float32
+    ).reshape(head_pairs, 2, span)
     exit_own = lax.all_gather(attention_out.astype(low), ("fsdp", "ctx"), axis=1, tiled=True)
     exits = [exit_own]
     for shift in range(1, n_tp):
@@ -432,121 +980,99 @@
         grad_expand_out, expert_out[0], expert_out_left, expert_out_right
     )
     grad_expand_in = jnp.einsum(
-        "sd,sgf->dgf", arrived, grad_mixed_up, preferred_element_type=jnp.float32
+        "sgf,sd->gfd", grad_mixed_up, arrived, preferred_element_type=jnp.float32
     )
     back_grads, sent_rows, grad_router, grad_expand_out, grad_expand_in, shrink_left, shrink_right, shrink_new = barrier(
         back_grads, sent_rows, grad_router, grad_expand_out, grad_expand_in, shrink_left, shrink_right, shrink_new
     )
-    grad_second = lax.psum(dot_tn(picks, back_grads).astype(low), "tp").astype(jnp.float32)
+    grad_second = combine_sum(slot_rows, back_grads, rows)
 
     back_rows = crossing(sent_rows.reshape(experts, capacity, width)).reshape(slots_all, width)
-    expand_left, expand_right, expand_new = precondition(
-        grad_expand_in.reshape(width, -1),
-        expert_in.reshape(width, -1),
-        expert_in_left,
-        expert_in_right,
-    )
+    grad_second, back_rows = barrier(grad_second, back_rows)
     result_part = dot_tn(picks, back_rows).astype(low)
-    grad_second, expand_left, expand_right, expand_new, result_part = barrier(
-        grad_second, expand_left, expand_right, expand_new, result_part
-    )
-    result = (middle + lax.psum(result_part, "tp").astype(jnp.float32)).astype(low)
 
     unused, pull = jax.vjp(normalize, middle, gain_second)
-    grad_middle_norm, grad_gain_second = pull(grad_second)
+    grad_middle_norm, grad_gain_second = pull(grad_second.astype(jnp.float32))
     grad_middle = cotangent.astype(jnp.float32) + grad_middle_norm
     grad_attention = grad_middle.astype(low)
     grad_mixed = dot_nt(grad_attention, exit_own).astype(low)
-    grad_queries, key_value_grads, sums = [], [], []
-    for pair in range(head_pairs):
-        columns = slice(pair * LANES, (pair + 1) * LANES)
-        grad_query, key_grad, value_grad, line_sums = attend_back(
-            queries[pair],
-            pairs[pair][0],
-            pairs[pair][1],
-            grad_mixed[:, columns],
-            mixed_parts[pair],
-            logs[pair],
-            back_lines[pair],
-        )
-        grad_queries.append(grad_query)
-        sums.append(line_sums)
-        terms = jnp.concatenate([key_grad, value_grad], 1).astype(low)
-        swapped = lax.all_to_all(
-            terms.reshape(n_ctx, rows, 2 * LANES), "ctx", split_axis=0, concat_axis=0, tiled=True
-        )
-        key_value_grads.append(jnp.sum(swapped.astype(jnp.float32), 0).astype(low))
+    grad_query, key_value_grad, sums, result_sum = attend_back(
+        query, jnp.stack(pairs), grad_mixed, mixed, jnp.concatenate(logs, 0), back_lines, result_part
+    )
+    result = (middle + result_sum.astype(jnp.float32)).astype(low)
     grad_projected = jnp.stack(
         [
-            jnp.concatenate(grad_queries, 1),
-            jnp.concatenate([terms[:, :LANES] for terms in key_value_grads], 1),
-            jnp.concatenate([terms[:, LANES:] for terms in key_value_grads], 1),
+            grad_query,
+            jnp.concatenate([key_value_grad[pair, :, :LANES] for pair in range(head_pairs)], 1),
+            jnp.concatenate([key_value_grad[pair, :, LANES:] for pair in range(head_pairs)], 1),
         ]
     )
     grad_exit = dot_tn(mixed, grad_attention).astype(low)
     grad_first_part = jnp.einsum(
         "kse,kde->sd", grad_projected, entry_full, preferred_element_type=jnp.float32
     )
-    grad_first_part, result = barrier(grad_first_part.astype(low), result)
-    grad_first = lax.psum(grad_first_part, "tp").astype(jnp.float32)
+    unused, pull = jax.vjp(normalize, inputs, gain_first)
+    grad_gain_first = pull(grad_first_part)[1]
     grad_entry = jnp.einsum(
         "sd,kse->dke", first, grad_projected, preferred_element_type=jnp.float32
     ).astype(low)
-    entry_terms = lax.all_to_all(
-        grad_entry.reshape(shards, depth, 3 * head_cols),
-        ("fsdp", "ctx"),
-        split_axis=0,
-        concat_axis=0,
-        tiled=True,
-    )
-    owned_in = (
-        jnp.sum(entry_terms.astype(jnp.float32), 0).reshape(depth, 3, head_cols).transpose(1, 0, 2)
-    )
-    exit_terms = lax.all_to_all(
-        grad_exit.reshape(head_cols, shards, depth).transpose(1, 0, 2),
-        ("fsdp", "ctx"),
-        split_axis=0,
-        concat_axis=0,
-        tiled=True,
-    )
-    owned_out = jnp.sum(exit_terms.astype(jnp.float32), 0)
-    unused, pull = jax.vjp(normalize, inputs, gain_first)
-    grad_inputs, grad_gain_first = pull(grad_first)
-    grad_tokens = grad_middle + grad_inputs
-
     table_grad = lax.dot_general(
-        hits.astype(jnp.float32),
-        jnp.concatenate(sums, 0).reshape(local_heads, span)[:, ::-1],
+        hits_back.astype(jnp.float32),
+        sums.reshape(local_heads, span),
         (((0,), (1,)), ((), ())),
         precision=highest,
         preferred_element_type=jnp.float32,
     )
-    own_tp = (jnp.arange(n_tp) == tp_here).astype(jnp.float32)
-    own_shard = (jnp.arange(shards) == here).astype(jnp.float32)
-    gain_sums = jnp.stack([grad_gain_first, grad_gain_second]) * own_tp[0]
+    gain_sums = jnp.stack([grad_gain_first, jnp.where(tp_here == 0, grad_gain_second, 0.0)])
     peak_own = jnp.concatenate(peak_parts)
     pieces = [
-        grad_router,
-        gain_sums,
-        own_tp[:, None, None] * table_grad[None],
-        own_shard[:, None, None] * own_tp[None, :, None] * peak_own[None, None, :],
+        grad_router.reshape(shards, -1),
+        gain_sums.reshape(2, shards, depth).transpose(1, 0, 2).reshape(shards, -1),
+        table_grad.reshape(shards, -1),
+        jnp.broadcast_to(peak_own[None], (shards, local_heads)),
     ]
-    packed = jnp.concatenate([piece.reshape(-1) for piece in pieces])
-    total = packed.shape[0]
-    packed = lax.psum(
-        jnp.pad(packed, (0, -total % 1024)).reshape(-1, LANES), ("fsdp", "ctx", "tp")
-    ).reshape(-1)
     spots = [0]
+    padded = []
     for piece in pieces:
-        spots.append(spots[-1] + piece.size)
-    router_sum = packed[spots[0] : spots[1]].reshape(shards, depth, experts)
-    owned_router = lax.dynamic_index_in_dim(router_sum, here, 0, keepdims=False)
-    gain_sum = packed[spots[1] : spots[2]].reshape(2, width)
-    owned_gains = lax.dynamic_slice_in_dim(gain_sum, here * depth, depth, 1)
-    table_sum = packed[spots[2] : spots[3]].reshape(n_tp, shards, table_size, local_heads)
-    owned_table = jnp.einsum("t,s,tsbh->bh", own_tp, own_shard, table_sum, precision=highest)
-    peak_sum = packed[spots[3] : spots[4]].reshape(shards, n_tp, local_heads)
-    peaks = jnp.max(jnp.einsum("t,sth->sh", own_tp, peak_sum, precision=highest), 0)
+        padded.append(jnp.pad(piece, ((0, 0), (0, -piece.shape[1] % LANES))))
+        spots.append(spots[-1] + padded[-1].shape[1] // LANES)
+    small = jnp.concatenate(padded, 1)
+    small = jnp.pad(small, ((0, 0), (0, -small.shape[1] % (8 * LANES)))).reshape(shards, -1, LANES)
+    columns = grad_expand_in.shape[0] * grad_expand_in.shape[1]
+    flat_master = expert_in[0].transpose(1, 2, 0).reshape(columns, width)
+    size = jnp.sqrt(jnp.mean(flat_master * flat_master) + step_epsilon)
+    first_part, small, entry_terms, exit_terms = barrier(
+        grad_first_part.astype(low), small, grad_entry, grad_exit
+    )
+    entry_terms = crossing(entry_terms.reshape(shards, depth, 3 * head_cols))
+    exit_terms = crossing(exit_terms.reshape(head_cols, shards, depth).transpose(1, 0, 2))
+    expand_right, expand_left, expand_new, grad_first, small_sum = tail(
+        first_part,
+        small,
+        spots[2],
+        grad_expand_in.reshape(columns, width).astype(low),
+        jnp.full((8, LANES), matrix_rate * size, jnp.float32),
+        expert_in_left,
+        expert_in_right,
+        flat_master,
+    )
+    grad_first, entry_terms, exit_terms = barrier(grad_first, entry_terms, exit_terms)
+    owned_in = (
+        jnp.sum(entry_terms.astype(jnp.float32), 0).reshape(depth, 3, head_cols).transpose(1, 0, 2)
+    )
+    owned_out = jnp.sum(exit_terms.astype(jnp.float32), 0)
+    grad_tokens = grad_middle + pull(grad_first.astype(jnp.float32))[0]
+
+    def small_piece(number, shape):
+        count = 1
+        for extent in shape:
+            count *= extent
+        return small_sum[spots[number] : spots[number + 1]].reshape(-1)[:count].reshape(shape)
+
+    owned_router = small_piece(0, (depth, experts))
+    owned_gains = small_piece(1, (2, depth))
+    owned_table = small_piece(2, (table_size, local_heads))
+    peaks = small_piece(3, (local_heads,))
     in_left, in_right, in_new = jax.vmap(precondition)(
         owned_in,
         attention_in,
@@ -572,8 +1098,8 @@
         out_new,
         out_left,
         out_right,
-        grad_expand_in[None],
-        expand_new.reshape(expert_in.shape),
+        grad_expand_in.transpose(2, 0, 1)[None],
+        expand_new.reshape(2, -1, width).transpose(2, 0, 1)[None],
         expand_left,
         expand_right,
         grad_expand_out[None],

time: 900 us -> 746 us (0.83)
  Pallas kernels: 69 us -> 249 us
  waiting for transfers between devices: 294 us -> 123 us
  matrix products: 210 us -> 160 us
  blocking collectives: 59.2 us -> 19.7 us
  local copies, waits for them, and re-layouts: 100 us -> 63.9 us
  other arithmetic: 92.8 us -> 65.9 us
    psum x3 -> x0, waiting for transfers between devices: 182 us -> none  [the longest x1 65.8 us: on_device(): lax.psum(dot_tn(picks, back_grads).astype(low), 'tp').astype(jnp.float32)]
    pallas_call x0 -> x2, Pallas kernels: none -> 142 us  [the longest x1 72.5 us: tail(): pl.pallas_call(functools.partial(tail_kernel, n_fsdp, n_ctx, n_tp, (right...]
    psum x1 -> x0, blocking collectives: 39.5 us -> none  [on_device(): lax.psum(jnp.pad(packed, (0, -total % 1024)).reshape(-1, LANES), ('fsdp',...]
    pallas_call x2 -> x1, Pallas kernels: 44.2 us -> 82.6 us  [attend_back(): pl.pallas_call(functools.partial(attend_back_kernel, length, rows, tile,...]
    all_to_all x5 -> x7, waiting for transfers between devices: 49.2 us -> 74.1 us  [crossing(): lax.all_to_all(values, ('fsdp', 'ctx'), split_axis=0, concat_axis=0, tile...]
    dot_general x9 -> x7, matrix products: 55.1 us -> 31.8 us  [dot_tn(): lax.dot_general(left, right, (((0,), (0,)), ((), ())), preferred_element_...]
    all_to_all x4 -> x0, waiting for transfers between devices: 16.4 us -> none  [the longest x2 8.45 us: on_device(): lax.all_to_all(terms.reshape(n_ctx, rows, 2 * LANES), 'ctx', split_axis=0...]
    all_to_all x4 -> x0, starting transfers between devices: 15.8 us -> none  [the longest x2 8.02 us: on_device(): lax.all_to_all(terms.reshape(n_ctx, rows, 2 * LANES), 'ctx', split_axis=0...]
  transfers between devices with their start and end apart: 20 -> 15, of which waited for: 11 -> 7; matrix products, arithmetic and copies ran while one was open for 30% -> 23% of each run, Pallas kernels for 5% -> 23%
where the time goes in v2:
time: 746 us; the launch traced here: 737 us
  Pallas kernels  249 us (33%)
  matrix products  160 us (21%)
  waiting for transfers between devices  123 us (16%)
  other arithmetic  65.9 us (9%)
  local copies, waits for them, and re-layouts  63.9 us (9%)
  starting transfers between devices  37.5 us (5%)
  blocking collectives  19.7 us (3%)
  between operations  18.8 us (3%)
    pallas_call x1, Pallas kernels, attend_back(): pl.pallas_call(functools.partial(attend_back_kernel, length, rows, tile,...  82.6 us
    all_to_all x7, waiting for transfers between devices, crossing(): lax.all_to_all(values, ('fsdp', 'ctx'), split_axis=0, concat_axis=0, tile...  74.1 us
    pallas_call x1, Pallas kernels, tail(): pl.pallas_call(functools.partial(tail_kernel, n_fsdp, n_ctx, n_tp, (right...  72.5 us
    pallas_call x1, Pallas kernels, combine_sum(): pl.pallas_call(functools.partial(combine_sum_kernel, lax.axis_size('tp'))...  69.4 us
    dot_general x9, matrix products, dot_nn(): lax.dot_general(left, right, (((1,), (0,)), ((), ())), preferred_element_...  54 us
    dot_general x7, matrix products, dot_tn(): lax.dot_general(left, right, (((0,), (0,)), ((), ())), preferred_element_...  31.8 us
    all_to_all x7, starting transfers between devices, crossing(): lax.all_to_all(values, ('fsdp', 'ctx'), split_axis=0, concat_axis=0, tile...  31.3 us
    unnamed x169, local copies, waits for them, and re-layouts  30.4 us
  transfers between devices with their start and end apart: 15, of which 7 were waited for; matrix products, arithmetic and copies ran while one was open for 23% of the time, Pallas kernels for 23%

profile of v2, /device:TPU:0, one launch (start us, length us, event | category | flops | bytes accessed | tf_op | source)
XLA Modules:
  0.0 737.5 jit_solution(90998662425216460)
XLA Ops:
  9.0 19.7 %all_gather.25 = bf16[256,1024]{1,0:T(8,128)(2,1)S(1)} all-gather(bf16[256,128]{1,0:T(8,128)(2,1)S(1)} %get-tuple-element.269), channel_id=1, replica_groups=mesh['fsdp'=4,'ctx'=2,'tp'=4] {'fsdp','ctx'}, dimensions={1}, use_global_device_ids=true | all-gather | bytes 589824 | tf_op jit(solution)/shard_map/all_gather | solution.py:924
  46.3 9.0 %fusion.28 = bf16[2560,1024]{1,0:T(8,128)(2,1)} fusion(bf16[1024,1024]{1,0:T(8,128)(2,1)} %param.23, s32[1024]{0:T(1024)S(1)} %get-tuple-element.241, s32[1024]{0:T(1024)S(1)} %get-tuple-element.240), kind=kOutput, calls=%fused_computation.50 | convolution fusion | flops 5379194880 | bytes 7348224 | tf_op jit(solution)/shard_map/dot_general | solution.py:35
  55.3 7.7 %all-gather.15.cloned.1.call-done = bf16[3200,256]{1,0:T(8,128)(2,1)} async-done(((bf16[400,256]{1,0:T(8,128)(2,1)}), bf16[3200,256]{1,0:T(8,128)(2,1)}) %all-gather.15.cloned.1.call-update) | async-done | bytes 1638416 | tf_op jit(solution)/shard_map/all_gather | solution.py:862
  85.0 17.6 %all-gather.7.cloned.1.call-done = bf16[2,2048,128]{2,1,0:T(8,128)(2,1)} async-done(((bf16[2,1024,128]{2,1,0:T(8,128)(2,1)}), bf16[2,2048,128]{2,1,0:T(8,128)(2,1)}) %all-gather.7.cloned.1.call-update) | async-done | bytes 1048592 | tf_op jit(solution)/shard_map/all_gather | solution.py:939
  104.9 12.4 %shard_map.421 = (bf16[1024,128]{1,0:T(8,128)(2,1)}, f32[1,2,1024]{2,1,0:T(2,128)}, f32[1,2,128]{2,1,0:T(2,128)}) custom-call(bf16[1024,128]{1,0:T(8,128)(2,1)} %get-tuple-element.265.q_ref, bf16[2048,128]{1,0:T(8,128)(2,1)} %get-tuple-element.263.k_ref, bf16[2048,128]{1,0:T(8,128)(2,1)} %get-tuple-element.262.v_ref, f32[1,2,3072]{2,1,0:T(2,128)} %get-tuple-element.271.line_ref), custom_call_target="tpu_custom_call" | custom-call | flops 4294967296 | bytes 2097152 | tf_op jit(solution)/shard_map/pallas_call | solution.py:91
  139.4 12.4 %shard_map.422 = (bf16[1024,128]{1,0:T(8,128)(2,1)}, f32[1,2,1024]{2,1,0:T(2,128)}, f32[1,2,128]{2,1,0:T(2,128)}) custom-call(bf16[1024,128]{1,0:T(8,128)(2,1)} %get-tuple-element.264.q_ref, bf16[2048,128]{1,0:T(8,128)(2,1)} %get-tuple-element.261.k_ref, bf16[2048,128]{1,0:T(8,128)(2,1)} %get-tuple-element.260.v_ref, f32[1,2,3072]{2,1,0:T(2,128)} %get-tuple-element.270.line_ref), custom_call_target="tpu_custom_call" | custom-call | flops 4294967296 | bytes 2097152 | tf_op jit(solution)/shard_map/pallas_call | solution.py:91
  166.6 23.0 %all-gather.13.cloned.1.call-done = bf16[1024,512]{1,0:T(8,128)(2,1)} async-done(((bf16[1024,128]{1,0:T(8,128)(2,1)}), bf16[1024,512]{1,0:T(8,128)(2,1)}) %all-gather.13.cloned.1.call-update) | async-done | bytes 1048592 | tf_op jit(solution)/shard_map/all_gather | solution.py:947
  195.7 7.9 %fusion.31 = bf16[2560,1024]{1,0:T(8,128)(2,1)} fusion(s32[1024]{0:T(1024)S(1)} %get-tuple-element.241, s32[1024]{0:T(1024)S(1)} %get-tuple-element.240, f32[1024,1024]{1,0:T(8,128)S(1)} %get-tuple-element.277, f32[1024]{0:T(1024)S(1)} %get-tuple-element.274, f32[1024]{0:T(1024)S(1)} %fusion.141), kind=kOutput, calls=%fused_computation.51 | convolution fusion | flops 5382340608 | bytes 9453568 | tf_op jit(solution)/shard_map/dot_general | solution.py:35
  211.1 8.5 %fusion.191 = f32[2560,704]{0,1:T(8,128)} fusion(bf16[2560,1024]{1,0:T(8,128)(2,1)} %bitcast.27, f32[1,704,1024]{2,1,0:T(8,128)S(1)} %copy-done.9), kind=kOutput, calls=%fused_computation.285 | convolution fusion | flops 3690987520 | bytes 15335424 | tf_op jit(solution)/shard_map/dot_general | solution.py:31
  219.5 48.6 %all-to-all-done.2 = bf16[8,320,1024]{2,1,0:T(8,128)(2,1)} async-done(((bf16[8,320,1024]{2,1,0:T(8,128)(2,1)}), bf16[8,320,1024]{2,1,0:T(8,128)(2,1)}, u32[]{:S(2)}, u32[]{:S(2)}) %all-to-all-start.2) | async-done | bytes 5242912 | tf_op jit(solution)/shard_map/all_to_all | solution.py:811
  268.1 11.3 %fusion.36 = f32[2560,2,704]{0,2,1:T(8,128)S(1)} fusion(bf16[2560,1024]{1,0:T(8,128)(2,1)} %bitcast.30, f32[1,1024,2,704]{1,3,2,0:T(8,128)} %param.31), kind=kOutput, calls=%fused_computation.56 | convolution fusion | flops 7381975040 | bytes 25427968 | tf_op jit(solution)/shard_map/sd,dgf->sgf/dot_general | solution.py:964
  279.4 8.0 %fusion.94 = f32[2560]{0:T(1024)S(1)} fusion(bf16[2560,1024]{1,0:T(8,128)(2,1)} %bitcast.30, bf16[1024,8]{1,0:T(8,128)(2,1)S(1)} %reshape.362, s32[2560]{0:T(1024)S(1)} %reshape.360, f32[8]{0:T(128)S(1)} %compare_convert_fusion), kind=kOutput, calls=%fused_computation.130 | convolution fusion | flops 42042880 | bytes 5279776 | tf_op jit(solution)/shard_map/dot_general | solution.py:35
  287.5 9.1 %fusion.57 = f32[704,1024]{1,0:T(8,128)} fusion(bf16[2560,1024]{1,0:T(8,128)(2,1)} %bitcast.27, f32[2560]{0:T(1024)S(1)} %add_divide_fusion, f32[2560,2,704]{0,2,1:T(8,128)S(1)} %fusion.36), kind=kOutput, calls=%fused_computation.84 | convolution fusion | flops 3710812160 | bytes 22554624 | tf_op jit(solution)/shard_map/dot_general | solution.py:39
  296.6 9.0 %multiply_bitcast_fusion = (f32[2560,1,704]{0,2,1:T(8,128)}, f32[2560,1,704]{0,2,1:T(8,128)}, f32[2560]{0:T(1024)S(1)}) fusion(f32[2560,704]{0,1:T(8,128)S(1)} %bitcast.332, f32[2560]{0:T(1024)S(1)} %add_divide_fusion, f32[2560,2,704]{0,2,1:T(8,128)S(1)} %fusion.36), kind=kLoop, calls=%fused_computation.40 | loop fusion | flops 46855680 | bytes 36065280 | tf_op jit(solution)/shard_map/transpose(jvp())/broadcast_in_dim | solution.py:785
  305.6 13.6 %fusion.85 = f32[2560,1024,1]{1,0,2:T(8,128)S(1)} fusion(f32[2560,1,704]{0,2,1:T(8,128)} %get-tuple-element.250, f32[2560,1,704]{0,2,1:T(8,128)} %get-tuple-element.249, f32[1,1024,2,704]{1,3,2,0:T(8,128)} %param.31), kind=kOutput, calls=%fused_computation.113 | convolution fusion | flops 7389184000 | bytes 30670848 | tf_op jit(solution)/shard_map/sgf,dgf->sd/dot_general | solution.py:971
  328.3 8.7 %multiply_reduce_fusion.2 = (f32[]{:T(128)}, f32[704,1024]{1,0:T(8,128)}) fusion(f32[2,1024,1024]{2,1,0:T(8,128)} %param.40, f32[2,704,704]{2,1,0:T(8,128)} %param.39, f32[704,1024]{1,0:T(8,128)} %fusion.57), kind=kOutput, calls=%fused_computation.93 | convolution fusion | flops 2494300160 | bytes 8945668 | tf_op jit(solution)/shard_map/dot_general | solution.py:35
  357.6 7.4 %convolution_convert_fusion = bf16[2560,1024]{1,0:T(8,128)(2,1)} fusion(f32[2560,2,704]{0,2,1:T(8,128)S(1)} %bitcast.321, f32[2560]{0:T(1024)S(1)} %add_divide_fusion, f32[1,704,1024]{2,1,0:T(8,128)S(1)} %copy-done.9), kind=kOutput, calls=%fused_computation.49 | convolution fusion | flops 3714154496 | bytes 22554624 | tf_op jit(solution)/shard_map/dot_general | solution.py:35
  365.1 13.3 %fusion.34 = f32[2,704,1024]{2,1,0:T(8,128)} fusion(bf16[2560,1024]{1,0:T(8,128)(2,1)} %bitcast.30, f32[2560,1,704]{0,2,1:T(8,128)} %get-tuple-element.250, f32[2560,1,704]{0,2,1:T(8,128)S(1)} %bitcast.330), kind=kOutput, calls=%fused_computation.54 | convolution fusion | flops 7389184000 | bytes 25427968 | tf_op jit(solution)/shard_map/sgf,sd->gfd/dot_general | solution.py:982
  378.3 9.5 %all-to-all-done.3 = bf16[8,320,1024]{2,1,0:T(8,128)(2,1)} async-done(((bf16[8,320,1024]{2,1,0:T(8,128)(2,1)}), bf16[8,320,1024]{2,1,0:T(8,128)(2,1)}, u32[]{:S(2)}, u32[]{:S(2)}) %all-to-all-start.3) | async-done | bytes 5242912 | tf_op jit(solution)/shard_map/all_to_all | solution.py:811
  408.6 69.4 %shard_map.423 = bf16[1024,1024]{1,0:T(8,128)(2,1)S(1)} custom-call(s32[1024,2]{1,0:T(8,128)S(1)} %copy-done.1, bf16[2560,1024]{1,0:T(8,128)(2,1)} %bitcast.40.back_ref), custom_call_target="tpu_custom_call" | custom-call | flops 5368709120 | bytes 209715200 | tf_op jit(solution)/shard_map/pallas_call | solution.py:332
  486.5 9.3 %fusion.72.part_ref = bf16[1024,1024]{1,0:T(8,128)(2,1)} fusion(bf16[2560,1024]{1,0:T(8,128)(2,1)} %bitcast.48, s32[1024]{0:T(1024)S(1)} %copy-done.51, s32[1024]{0:T(1024)S(1)} %copy-done.49), kind=kOutput, calls=%fused_computation.106 | convolution fusion | flops 5377622016 | bytes 7348224 | tf_op jit(solution)/shard_map/dot_general | solution.py:39
  495.8 82.6 %shard_map.424 = (bf16[1024,256]{1,0:T(8,128)(2,1)}, bf16[2,1024,256]{2,1,0:T(8,128)(2,1)}, f32[2,2,3072]{2,1,0:T(2,128)}, bf16[1024,1024]{1,0:T(8,128)(2,1)}) custom-call(bf16[1024,256]{1,0:T(8,128)(2,1)} %copy-done.18, bf16[2,2,2048,128]{3,2,1,0:T(8,128)(2,1)} %pad_maximum_fusion.k_ref.v_ref, bf16[2,2,2048,128]{3,2,1,0:T(8,128)(2,1)} %pad_maximum_fusion.k_ref.v_ref, ...), custom_call_target="tpu_custom_call" | custom-call | flops 21474836480 | bytes 12582912 | tf_op jit(solution)/shard_map/pallas_call | solution.py:508
  593.9 72.5 %shard_map.425 = (f32[1408,1408]{1,0:T(8,128)}, f32[1024,1024]{1,0:T(8,128)}, f32[1408,1024]{1,0:T(8,128)}, bf16[1024,1024]{1,0:T(8,128)(2,1)}, f32[16,128]{1,0:T(8,128)}) custom-call(bf16[1024,1024]{1,0:T(8,128)(2,1)} %get-tuple-element.86.part_ref, f32[8,16,128]{2,1,0:T(8,128)} %bitcast.360, bf16[1408,1024]{1,0:T(8,128)(2,1)} %bitcast.348, ...), custom_call_target="tpu_custom_call" | custom-call | flops 28051505152 | bytes 251658240 | tf_op jit(solution)/shard_map/pallas_call | solution.py:730
  684.0 12.9 %all-to-all-done.5 = bf16[8,128,768]{1,2,0:T(8,128)(2,1)} async-done(((bf16[8,128,768]{1,2,0:T(8,128)(2,1)}), bf16[8,128,768]{1,2,0:T(8,128)(2,1)}, u32[]{:S(2)}, u32[]{:S(2)}) %all-to-all-start.5) | async-done | bytes 1572896 | tf_op jit(solution)/shard_map/all_to_all | solution.py:811
  (330 shorter events, 215.3 us)
Async XLA Ops:
  7.2 35.7 %copy-start.27 = (s32[1024,2]{0,1:T(2,128)S(1)}, s32[1024,2]{0,1:T(2,128)}, u32[]{:S(2)}) copy-start(s32[1024,2]{0,1:T(2,128)} %param.24) | copy-start | bytes 24580
  7.2 38.0 %copy-start.42 = (s32[4095]{0:T(1024)S(1)}, s32[4095]{0:T(1024)}, u32[]{:S(2)}) copy-start(s32[4095]{0:T(1024)} %param.25) | copy-start | bytes 49144
  7.2 38.5 %copy-start.2 = (bf16[1024,1024]{1,0:T(8,128)(2,1)S(1)}, bf16[1024,1024]{1,0:T(8,128)(2,1)}, u32[]{:S(2)}) copy-start(bf16[1024,1024]{1,0:T(8,128)(2,1)} %param.22) | copy-start | bytes 6291460
  7.2 55.7 %all-gather.15.cloned.1.call-start = ((), (), s32[]{:S(2)}) async-start(), calls=%async_computation.11 | async-start | bytes 1843200 | tf_op jit(solution)/shard_map/all_gather | solution.py:862
  28.7 129.4 %copy-start.10 = (bf16[256,1024]{1,0:T(8,128)(2,1)}, bf16[256,1024]{1,0:T(8,128)(2,1)S(1)}, u32[]{:S(2)}) copy-start(bf16[256,1024]{1,0:T(8,128)(2,1)S(1)} %all_gather.25) | copy-start | bytes 1572868
  28.7 104.8 %collective-permute-start = (bf16[256,1024]{1,0:T(8,128)(2,1)S(1)}, bf16[256,1024]{1,0:T(8,128)(2,1)}, u32[]{:S(2)}, u32[]{:S(2)}) collective-permute-start(bf16[256,1024]{1,0:T(8,128)(2,1)S(1)} %all_gather.25), channel_id=1, source_target_pairs={{0,3},{1,0},{2,1},{3,2},{4,7},{5,4},{6,5},{7,6},{8,11},{9,8},{10,9... | collective-permute-start | bytes 1572872 | tf_op jit(solution)/shard_map/ppermute | solution.py:928
  32.3 103.0 %collective-permute-start.1 = (bf16[256,1024]{1,0:T(8,128)(2,1)S(1)}, bf16[256,1024]{1,0:T(8,128)(2,1)}, u32[]{:S(2)}, u32[]{:S(2)}) collective-permute-start(bf16[256,1024]{1,0:T(8,128)(2,1)S(1)} %all_gather.25), channel_id=1, source_target_pairs={{0,2},{1,3},{2,0},{3,1},{4,6},{5,7},{6,4},{7,5},{8,10},{9,11},{10,... | collective-permute-start | bytes 1572872 | tf_op jit(solution)/shard_map/ppermute | solution.py:928
  37.2 65.4 %all-gather.7.cloned.1.call-start = ((), (), s32[]{:S(2)}) async-start(), calls=%async_computation.7 | async-start | bytes 1572864 | tf_op jit(solution)/shard_map/all_gather | solution.py:939
  45.2 36.0 %copy-start.32 = (s32[3072]{0:T(1024)}, s32[3072]{0:T(1024)S(1)}, u32[]{:S(2)}) copy-start(s32[3072]{0:T(1024)S(1)} %pad_dynamic-slice_fusion) | copy-start | bytes 36868
  45.7 147.9 %copy-start.48 = (s32[1024]{0:T(1024)}, s32[1024]{0:T(1024)S(1)}, u32[]{:S(2)}) copy-start(s32[1024]{0:T(1024)S(1)} %get-tuple-element.240) | copy-start | bytes 12292
  45.7 147.9 %copy-start.50 = (s32[1024]{0:T(1024)}, s32[1024]{0:T(1024)S(1)}, u32[]{:S(2)}) copy-start(s32[1024]{0:T(1024)S(1)} %get-tuple-element.241) | copy-start | bytes 12292
  81.1 56.1 %all-gather.11.cloned.1.call-start = ((), (), s32[]{:S(2)}) async-start(), calls=%async_computation.9 | async-start | bytes 1572864 | tf_op jit(solution)/shard_map/all_gather | solution.py:939
  83.1 34.1 %copy-start.18 = (bf16[1024,256]{1,0:T(8,128)(2,1)}, bf16[1024,256]{1,0:T(8,128)(2,1)S(1)}, u32[]{:S(2)}) copy-start(bf16[1024,256]{1,0:T(8,128)(2,1)S(1)} %fusion.102.q_ref) | copy-start | bytes 1572868
  83.9 78.0 %all-gather.9.cloned.1.call-start = ((), (), s32[]{:S(2)}) async-start(), calls=%async_computation.8 | async-start | bytes 1310720 | tf_op jit(solution)/shard_map/all_gather | solution.py:947
  120.1 8.0 %all-to-all-start.1 = ((s32[8,1,320]{2,1,0:T(1,128)}), s32[8,1,320]{2,1,0:T(1,128)S(1)}, u32[]{:S(2)}, u32[]{:S(2)}) async-start(s32[8,1,320]{2,1,0:T(1,128)} %all_to_all.25), calls=%async_computation.1 | async-start | bytes 24576 | tf_op jit(solution)/shard_map/all_to_all | solution.py:811
  123.5 28.4 %collective-permute-start.2 = (bf16[256,1024]{1,0:T(8,128)(2,1)S(1)}, bf16[256,1024]{1,0:T(8,128)(2,1)S(1)}, u32[]{:S(2)}, u32[]{:S(2)}) collective-permute-start(bf16[256,1024]{1,0:T(8,128)(2,1)S(1)} %all_gather.25), channel_id=1, source_target_pairs={{0,1},{1,2},{2,3},{3,0},{4,5},{5,6},{6,7},{7,4},{8,9},{9,10},{10,1... | collective-permute-start | bytes 1572872 | tf_op jit(solution)/shard_map/ppermute | solution.py:928
  128.1 75.5 %all-to-all-start = ((bf16[8,320,1024]{2,1,0:T(8,128)(2,1)}), bf16[8,320,1024]{2,1,0:T(8,128)(2,1)}, u32[]{:S(2)}, u32[]{:S(2)}) async-start(bf16[8,320,1024]{2,1,0:T(8,128)(2,1)} %bitcast.341), calls=%async_computation | async-start | bytes 10485760 | tf_op jit(solution)/shard_map/all_to_all | solution.py:811
  132.8 56.9 %all-gather.13.cloned.1.call-start = ((), (), s32[]{:S(2)}) async-start(), calls=%async_computation.10 | async-start | bytes 1310720 | tf_op jit(solution)/shard_map/all_gather | solution.py:947
  203.5 64.6 %all-to-all-start.2 = ((bf16[8,320,1024]{2,1,0:T(8,128)(2,1)}), bf16[8,320,1024]{2,1,0:T(8,128)(2,1)}, u32[]{:S(2)}, u32[]{:S(2)}) async-start(bf16[8,320,1024]{2,1,0:T(8,128)(2,1)} %bitcast.343), calls=%async_computation.2 | async-start | bytes 10485760 | tf_op jit(solution)/shard_map/all_to_all | solution.py:811
  323.3 64.6 %all-to-all-start.3 = ((bf16[8,320,1024]{2,1,0:T(8,128)(2,1)}), bf16[8,320,1024]{2,1,0:T(8,128)(2,1)}, u32[]{:S(2)}, u32[]{:S(2)}) async-start(bf16[8,320,1024]{2,1,0:T(8,128)(2,1)} %bitcast.319), calls=%async_computation.3 | async-start | bytes 10485760 | tf_op jit(solution)/shard_map/all_to_all | solution.py:811
  387.8 90.2 %all-to-all-start.4 = ((bf16[8,320,1024]{2,1,0:T(8,128)(2,1)}), bf16[8,320,1024]{2,1,0:T(8,128)(2,1)}, u32[]{:S(2)}, u32[]{:S(2)}) async-start(bf16[8,320,1024]{2,1,0:T(8,128)(2,1)} %bitcast.342), calls=%async_computation.4 | async-start | bytes 10485760 | tf_op jit(solution)/shard_map/all_to_all | solution.py:811
  401.9 83.9 %copy-start.22 = (bf16[1024,256]{1,0:T(8,128)(2,1)}, bf16[1024,256]{1,0:T(8,128)(2,1)S(1)}, u32[]{:S(2)}) copy-start(bf16[1024,256]{1,0:T(8,128)(2,1)S(1)} %constant_dynamic-update-slice_fusion.8.m_ref) | copy-start | bytes 1572868
  589.4 83.0 %all-to-all-start.6 = ((bf16[8,256,128]{2,1,0:T(8,128)(2,1)}), bf16[8,256,128]{2,1,0:T(8,128)(2,1)S(1)}, u32[]{:S(2)}, u32[]{:S(2)}) async-start(bf16[8,256,128]{2,1,0:T(8,128)(2,1)} %bitcast_bitcast_fusion), calls=%async_computation.6 | async-start | bytes 1048576 | tf_op jit(solution)/shard_map/all_to_all | solution.py:811
  672.4 24.5 %all-to-all-start.5 = ((bf16[8,128,768]{1,2,0:T(8,128)(2,1)}), bf16[8,128,768]{1,2,0:T(8,128)(2,1)}, u32[]{:S(2)}, u32[]{:S(2)}) async-start(bf16[8,128,768]{1,2,0:T(8,128)(2,1)} %copy.159), calls=%async_computation.5 | async-start | bytes 3145728 | tf_op jit(solution)/shard_map/all_to_all | solution.py:811
  (66 other events, 485.7 us)
Sparse Core Ops, SparseCore 0:
  37.3 25.6 all-gather.14
  81.2 21.3 all-gather.6
  104.8 21.2 all-gather.10
  128.1 29.2 all-gather.8
  159.4 30.2 all-gather.12

commit v3 on v2

--- a/solution.py
+++ b/solution.py
@@ -44,18 +44,88 @@
     return (lane // DH) == half
 
 
-def attend_kernel(length, rows, tile, q_ref, k_ref, v_ref, line_ref, mixed_ref, log_ref, peak_ref, strip, wide):
+def attend_kernel(length, rows, tile, pairs, n_fsdp, n_ctx, n_tp, q_ref, own_ref, line_ref, cross_ref, mixed_ref, log_ref, peak_ref, kv_out, all_out, cross_out, strip, wide, kv_ref, all_ref, kv_send, kv_got, mix_send, mix_got, out_sem, cross_send, cross_got):
+    pair = pl.program_id(0)
     step = pl.program_id(1)
+    steps = rows // tile
     span = line_ref.shape[2]
+    here = lax.axis_index("ctx")
+    tp_here = lax.axis_index("tp")
+    own_rows = pl.ds(pl.multiple_of(here * rows, rows), rows)
+    ctx_peers = [(number, {"ctx": number}) for number in range(n_ctx)]
+    tp_peers = [(number, {"tp": number}) for number in range(n_tp)]
+    shard = lax.axis_index("fsdp") * n_ctx + here
+    plane = [(f * n_ctx + c, {"fsdp": f, "ctx": c}) for f in range(n_fsdp) for c in range(n_ctx)]
+    other = jnp.where(shard == 0, 1, 0)
+    other_plane = {"fsdp": other // n_ctx, "ctx": other % n_ctx}
+    other_ctx = {"ctx": jnp.where(here == 0, 1, 0)}
+    other_tp = {"tp": jnp.where(tp_here == 0, 1, 0)}
+
+    def kv_copy(slot, number, where):
+        return remote(
+            own_ref.at[slot], kv_ref.at[slot, :, own_rows, :], kv_send.at[slot, number], kv_got.at[slot, here], where
+        )
+
+    def kv_arrived(slot, number):
+        spot = kv_ref.at[slot, :, pl.ds(number * rows, rows), :]
+        remote(spot, spot, kv_got.at[slot, number], kv_got.at[slot, number], other_ctx).wait_recv()
+
+    def cross_copy(number, where):
+        return remote(
+            cross_ref.at[number], cross_out.at[shard], cross_send.at[number], cross_got.at[shard], where
+        )
+
+    def cross_own():
+        return pltpu.make_async_copy(cross_ref.at[shard], cross_out.at[shard], out_sem.at[2])
+
+    def mix_spot(slot, turn, number):
+        return (
+            pl.ds(pl.multiple_of(turn * tile, tile), tile),
+            pl.ds(pl.multiple_of((number * pairs + slot) * LANES, LANES), LANES),
+        )
+
+    def mix_copy(slot, turn, number, where):
+        spot = all_ref.at[mix_spot(slot, turn, tp_here)]
+        return remote(spot, spot, mix_send.at[slot, turn, number], mix_got.at[slot, turn, tp_here], where)
+
+    @pl.when((pair == 0) & (step == 0))
+    def _():
+        barrier = pltpu.get_barrier_semaphore()
+        greet(barrier, shard, plane)
+        greet(barrier, tp_here, tp_peers)
+        pl.semaphore_wait(barrier, n_fsdp * n_ctx - 1 + n_tp - 1)
+        for slot in range(pairs):
+            for number, where in ctx_peers:
+
+                @pl.when(number != here)
+                def _():
+                    kv_copy(slot, number, where).start()
+
+            kv_ref[slot, :, own_rows, :] = own_ref[slot]
 
     @pl.when(step == 0)
     def _():
         for half in range(2):
             line = jnp.broadcast_to(line_ref[0, half : half + 1, :], (LANES, span))
             strip[half] = pltpu.roll(line, span - (LANES - 1), 1, stride=1, stride_axis=0)
-        wide[:, :LANES] = v_ref[...]
         wide[:, LANES:] = jnp.ones((length, LANES), jnp.bfloat16)
         peak_ref[...] = jnp.full(peak_ref.shape, -jnp.inf, jnp.float32)
+        for number, where in ctx_peers:
+
+            @pl.when(number != here)
+            def _():
+                kv_arrived(pair, number)
+
+        wide[:, :LANES] = kv_ref[pair, 1]
+
+    @pl.when((pair == 0) & (step == 2))
+    def _():
+        cross_own().start()
+        for number, where in plane:
+
+            @pl.when(number != shard)
+            def _():
+                cross_copy(number, where).start()
 
     query = q_ref[...]
     groups = tile // LANES
@@ -64,7 +134,7 @@
     for half in range(2):
         mine = half_mask((tile, LANES), half)
         own = jnp.where(mine, query, jnp.zeros_like(query))
-        logit = dot_nt(own, k_ref[...])
+        logit = dot_nt(own, kv_ref[pair, 0])
         top = jnp.max(logit, 1, keepdims=True)
         bias = []
         for group in range(groups):
@@ -79,41 +149,105 @@
         log_ref[0, half : half + 1, :] = log_total.T[0:1, :]
         best = jnp.max(jnp.broadcast_to(top, (tile, LANES)), 0, keepdims=True)
         peak_ref[0, half : half + 1, :] = jnp.maximum(peak_ref[0, half : half + 1, :], best)
-    mixed_ref[...] = mixed.astype(jnp.bfloat16)
-
-
-def attend(query, keys, values, lines):
+    low = mixed.astype(jnp.bfloat16)
+    mixed_ref[...] = low
+    all_ref[mix_spot(pair, step, tp_here)] = low
+    for number, where in reversed(tp_peers):
+
+        @pl.when(number != tp_here)
+        def _():
+            mix_copy(pair, step, number, where).start()
+
+    @pl.when((pair == pairs - 1) & (step == steps - 1))
+    def _():
+        for slot in range(pairs):
+            for number, where in ctx_peers:
+
+                @pl.when(number != here)
+                def _():
+                    kv_copy(slot, number, where).wait_send()
+
+        def one(index, carry):
+            slot, turn = index // steps, index % steps
+            for number, where in tp_peers:
+
+                @pl.when(number != tp_here)
+                def _():
+                    spot = all_ref.at[mix_spot(slot, turn, number)]
+                    got = mix_got.at[slot, turn, number]
+                    remote(spot, spot, got, got, other_tp).wait_recv()
+                    mix_copy(slot, turn, number, where).wait_send()
+
+            return carry
+
+        kept = pltpu.make_async_copy(kv_ref, kv_out, out_sem.at[0])
+        kept.start()
+        lax.fori_loop(0, pairs * steps, one, 0)
+        gathered = pltpu.make_async_copy(all_ref, all_out, out_sem.at[1])
+        gathered.start()
+        kept.wait()
+        gathered.wait()
+        cross_own().wait()
+        for number, where in plane:
+
+            @pl.when(number != shard)
+            def _():
+                spot = cross_out.at[number]
+                remote(spot, spot, cross_got.at[number], cross_got.at[number], other_plane).wait_recv()
+                cross_copy(number, where).wait_send()
+
+
+def attend(query, own, lines, cross):
     rows, cols = query.shape
-    length = keys.shape[0]
+    n_fsdp, n_ctx, n_tp = lax.axis_size("fsdp"), lax.axis_size("ctx"), lax.axis_size("tp")
+    length = rows * n_ctx
     pairs = cols // LANES
     tile = 256 if length <= 4096 else 128
     span = lines.shape[2]
+    vmem = pl.BlockSpec(memory_space=pltpu.VMEM)
     return pl.pallas_call(
-        functools.partial(attend_kernel, length, rows, tile),
+        functools.partial(attend_kernel, length, rows, tile, pairs, n_fsdp, n_ctx, n_tp),
         grid=(pairs, rows // tile),
         in_specs=[
             pl.BlockSpec((tile, LANES), lambda p, t: (t, p)),
-            pl.BlockSpec((length, LANES), lambda p, t: (0, p)),
-            pl.BlockSpec((length, LANES), lambda p, t: (0, p)),
+            vmem,
             pl.BlockSpec((1, 2, span), lambda p, t: (p, 0, 0)),
+            pl.BlockSpec(memory_space=pl.ANY),
         ],
         out_specs=[
             pl.BlockSpec((tile, LANES), lambda p, t: (t, p)),
             pl.BlockSpec((1, 2, tile), lambda p, t: (p, 0, t)),
             pl.BlockSpec((1, 2, LANES), lambda p, t: (p, 0, 0)),
+            pl.BlockSpec(memory_space=pl.ANY),
+            pl.BlockSpec(memory_space=pl.ANY),
+            pl.BlockSpec(memory_space=pl.ANY),
         ],
         out_shape=[
             jax.ShapeDtypeStruct((rows, cols), jnp.bfloat16),
             jax.ShapeDtypeStruct((pairs, 2, rows), jnp.float32),
             jax.ShapeDtypeStruct((pairs, 2, LANES), jnp.float32),
+            jax.ShapeDtypeStruct((pairs, 2, length, LANES), jnp.bfloat16),
+            jax.ShapeDtypeStruct((rows, n_tp * cols), jnp.bfloat16),
+            jax.ShapeDtypeStruct(cross.shape, cross.dtype),
         ],
         scratch_shapes=[
             pltpu.VMEM((2, LANES, span), jnp.float32),
             pltpu.VMEM((length, 2 * LANES), jnp.bfloat16),
+            pltpu.VMEM((pairs, 2, length, LANES), jnp.bfloat16),
+            pltpu.VMEM((rows, n_tp * cols), jnp.bfloat16),
+            pltpu.SemaphoreType.DMA((pairs, n_ctx)),
+            pltpu.SemaphoreType.DMA((pairs, n_ctx)),
+            pltpu.SemaphoreType.DMA((pairs, rows // tile, n_tp)),
+            pltpu.SemaphoreType.DMA((pairs, rows // tile, n_tp)),
+            pltpu.SemaphoreType.DMA((3,)),
+            pltpu.SemaphoreType.DMA((n_fsdp * n_ctx,)),
+            pltpu.SemaphoreType.DMA((n_fsdp * n_ctx,)),
         ],
-        compiler_params=pltpu.CompilerParams(vmem_limit_bytes=56 * MIB),
-        cost_estimate=pl.CostEstimate(flops=16 * rows * length * cols, bytes_accessed=8 * length * cols, transcendentals=rows * length * cols // DH),
-    )(query, keys, values, lines)
+        compiler_params=pltpu.CompilerParams(
+            collective_id=3, has_side_effects=True, vmem_limit_bytes=60 * MIB
+        ),
+        cost_estimate=pl.CostEstimate(flops=100 * rows * length * cols, bytes_accessed=8 * length * cols, transcendentals=rows * length * cols // DH),
+    )(query, own, lines, cross)
 
 
 def remote(source, target, send, receive, where):
@@ -125,6 +259,16 @@
         device_id=where,
         device_id_type=pl.DeviceIdType.MESH,
     )
+
+
+def greet(barrier, me, peers):
+    for number, where in peers:
+
+        @pl.when(number != me)
+        def _():
+            pl.semaphore_signal(
+                barrier, inc=1, device_id=where, device_id_type=pl.DeviceIdType.MESH
+            )
 
 
 class LineSum:
@@ -548,16 +692,6 @@
     )(query, key_value, key_value, grad, mixed, logs, lines, part)
 
 
-def greet(barrier, me, peers):
-    for number, where in peers:
-
-        @pl.when(number != me)
-        def _():
-            pl.semaphore_signal(
-                barrier, inc=1, device_id=where, device_id_type=pl.DeviceIdType.MESH
-            )
-
-
 def tail_kernel(
     n_fsdp,
     n_ctx,
@@ -777,6 +911,74 @@
     )(part, small, grad, scale, right, right, left, left, weight)
 
 
+GELU_A = 0.7978845608028654
+GELU_B = 0.044715
+
+
+def expert_kernel(x_ref, plain_ref, other_ref, here_ref, w_ref, router_ref, sent_ref, hidden_ref, mixed_ref, choice_ref):
+    half = w_ref.shape[0] // 2
+    rows = x_ref[...]
+    first = dot_nt(rows, w_ref[:half, :])
+    second = dot_nt(rows, w_ref[half:, :])
+    logits = dot_nn(rows, router_ref[...])
+    lane = lax.broadcasted_iota(jnp.int32, logits.shape, 1)
+    contrast = (lane == here_ref[0:1, 0:1]).astype(jnp.float32) - (lane == other_ref[...]).astype(jnp.float32)
+    gate = jax.nn.sigmoid(jnp.sum(logits * contrast, 1, keepdims=True))
+    square = first * first
+    bent = jnp.tanh(GELU_A * first * (1.0 + GELU_B * square))
+    rise = 0.5 * (1.0 + bent)
+    gelu = first * rise
+    slope = rise + 0.5 * GELU_A * first * (1.0 - bent * bent) * (1.0 + 3.0 * GELU_B * square)
+    hidden = gelu * second
+    plain = plain_ref[...]
+    grad_gate = jnp.sum(plain * hidden, 1, keepdims=True)
+    choice = (gate * (1.0 - gate) * grad_gate * contrast).astype(jnp.bfloat16)
+    scaled = gate * plain
+    grad_first = (scaled * second * slope).astype(jnp.bfloat16)
+    grad_second = (scaled * gelu).astype(jnp.bfloat16)
+    hidden_ref[...] = (gate * hidden).astype(jnp.bfloat16)
+    mixed_ref[0] = grad_first
+    mixed_ref[1] = grad_second
+    choice_ref[...] = choice
+    sent = dot_nn(grad_first, w_ref[:half, :]) + dot_nn(grad_second, w_ref[half:, :])
+    sent_ref[...] = (sent + dot_nt(choice, router_ref[...])).astype(jnp.bfloat16)
+
+
+def expert_chain(rows, plain, other, here, weight, router):
+    count, width = rows.shape
+    half = weight.shape[0] // 2
+    tile = 320
+    vmem = pl.BlockSpec(memory_space=pltpu.VMEM)
+    return pl.pallas_call(
+        expert_kernel,
+        grid=(count // tile,),
+        in_specs=[
+            pl.BlockSpec((tile, width), lambda t: (t, 0)),
+            pl.BlockSpec((tile, half), lambda t: (t, 0)),
+            pl.BlockSpec((tile, 1), lambda t: (t, 0)),
+            vmem,
+            vmem,
+            vmem,
+        ],
+        out_specs=[
+            pl.BlockSpec((tile, width), lambda t: (t, 0)),
+            pl.BlockSpec((tile, half), lambda t: (t, 0)),
+            pl.BlockSpec((2, tile, half), lambda t: (0, t, 0)),
+            pl.BlockSpec((tile, LANES), lambda t: (t, 0)),
+        ],
+        out_shape=[
+            jax.ShapeDtypeStruct((count, width), jnp.bfloat16),
+            jax.ShapeDtypeStruct((count, half), jnp.bfloat16),
+            jax.ShapeDtypeStruct((2, count, half), jnp.bfloat16),
+            jax.ShapeDtypeStruct((count, LANES), jnp.bfloat16),
+        ],
+        compiler_params=pltpu.CompilerParams(vmem_limit_bytes=48 * MIB),
+        cost_estimate=pl.CostEstimate(
+            flops=8 * count * width * half, bytes_accessed=16 * count * width, transcendentals=count * half
+        ),
+    )(rows, plain, other, here, weight, router)
+
+
 def normalize(values, gain):
     return values * lax.rsqrt(jnp.mean(values * values, -1, keepdims=True) + norm_epsilon) * gain
 
@@ -860,7 +1062,14 @@
     )
     small = jnp.pad(small, (0, -small.shape[0] % (16 * head_cols))).reshape(-1, head_cols)
     gathered = lax.all_gather(
-        jnp.concatenate([attention_in.astype(low).reshape(3 * depth, head_cols), small], 0),
+        jnp.concatenate(
+            [
+                attention_in.astype(low).reshape(3 * depth, head_cols),
+                attention_out.astype(low).reshape(depth, head_cols),
+                small,
+            ],
+            0,
+        ),
         ("fsdp", "ctx"),
         axis=0,
         tiled=False,
@@ -871,7 +1080,13 @@
         .transpose(1, 0, 2, 3)
         .reshape(3, width, head_cols)
     )
-    small = gathered[:, 3 * depth :].reshape(shards, -1)
+    exit_own = (
+        gathered[:, 3 * depth : 4 * depth]
+        .reshape(shards, head_cols, depth)
+        .transpose(1, 0, 2)
+        .reshape(head_cols, width)
+    )
+    small = gathered[:, 4 * depth :].reshape(shards, -1)
     router_full = small[:, : sizes[0]].reshape(width, experts)
     gains_full = (
         small[:, sizes[0] : sizes[0] + sizes[1]]
@@ -882,7 +1097,6 @@
     table_full = small[:, sizes[0] + sizes[1] : sum(sizes)].reshape(shards * table_size, local_heads)
     gain_first = gains_full[0].astype(jnp.float32)
     gain_second = gains_full[1].astype(jnp.float32)
-    expand_in = expert_in[0].astype(low)
     expand_out = expert_out[0].astype(low)
 
     chosen = routes.reshape(-1)
@@ -901,86 +1115,68 @@
     )
     grad_buffer = dot_nn(picks, cotangent).astype(low).reshape(experts, capacity, width)
     other_arrived = crossing(other.reshape(experts, capacity)).reshape(-1)
-    grad_arrived = crossing(grad_buffer).reshape(slots_all, width)
 
     inputs = tokens.astype(jnp.float32)
     first = normalize(inputs, gain_first).astype(low)
-    first, unused = barrier(first, grad_buffer)
     projected = jnp.einsum(
         "sd,kde->kse", first, entry_full, preferred_element_type=jnp.float32
     )
     query = (projected[0].astype(low) * (DH**-0.5)).astype(low)
-    key_value = projected[1:].astype(low)
+    own_pairs = (
+        projected[1:].astype(low).reshape(2, rows, head_pairs, LANES).transpose(2, 0, 1, 3)
+    )
     low_end = length - rows - lax.axis_index("ctx") * rows
     near = lax.dynamic_slice_in_dim(jnp.pad(buckets, (0, 1)), low_end, span, 0)
     hits = (near[:, None] == jnp.arange(table_full.shape[0], dtype=jnp.int32)[None, :]).astype(low)
     lines = lax.dot_general(
         table_full, hits, (((0,), (1,)), ((), ())), preferred_element_type=jnp.float32
-    ).reshape(head_pairs, 1, 2, span)
+    ).reshape(head_pairs, 2, span)
     hits_back = (near[::-1][:, None] == jnp.arange(table_full.shape[0], dtype=jnp.int32)[None, :]).astype(low)
     back_lines = lax.dot_general(
         table_full, hits_back, (((0,), (1,)), ((), ())), preferred_element_type=jnp.float32
     ).reshape(head_pairs, 2, span)
-    exit_own = lax.all_gather(attention_out.astype(low), ("fsdp", "ctx"), axis=1, tiled=True)
-    exits = [exit_own]
+    exit_all = lax.dynamic_update_slice_in_dim(
+        jnp.zeros((n_tp * head_cols, width), low), exit_own, tp_here * head_cols, 0
+    )
     for shift in range(1, n_tp):
-        exits.append(
-            lax.ppermute(exit_own, "tp", [(i, (i + shift) % n_tp) for i in range(n_tp)])
+        piece = lax.ppermute(exit_own, "tp", [(i, (i + shift) % n_tp) for i in range(n_tp)])
+        exit_all = lax.dynamic_update_slice_in_dim(
+            exit_all, piece, (tp_here + n_tp - shift) % n_tp * head_cols, 0
         )
-    turned = jnp.concatenate(exits[::-1] + exits[::-1], 0)
-    exit_all = lax.dynamic_slice_in_dim(
-        turned, (n_tp - 1 - tp_here) * head_cols, n_tp * head_cols, 0
-    ).reshape(n_tp, head_pairs, LANES, width)
-    queries, pairs, mixed_parts, logs, peak_parts = [], [], [], [], []
-    value = jnp.zeros((), jnp.float32)
-    for pair in range(head_pairs):
-        columns = slice(pair * LANES, (pair + 1) * LANES)
-        queries.append(query[:, columns])
-        pairs.append(lax.all_gather(key_value[:, :, columns], "ctx", axis=1, tiled=True))
-    for pair in range(head_pairs):
-        mixed_part, log_part, peak_part = attend(
-            queries[pair], pairs[pair][0], pairs[pair][1], lines[pair]
-        )
-        mixed_parts.append(mixed_part)
-        logs.append(log_part)
-        peak_parts.append(peak_part[0, :, 0])
-        mixed_all = lax.all_gather(mixed_part, "tp", axis=1, tiled=True)
-        value = value + dot_nn(mixed_all, exit_all[:, pair].reshape(n_tp * LANES, width))
-    mixed = jnp.concatenate(mixed_parts, 1)
+    mixed, logs, peak_own, key_value, mixed_all, grad_arrived = attend(
+        query, own_pairs, lines, grad_buffer
+    )
+    grad_arrived = grad_arrived.reshape(slots_all, width)
+    value = dot_nn(mixed_all, exit_all)
     middle = inputs + value
     second = normalize(middle, gain_second).astype(low)
 
     buffer = dot_nn(picks, second).astype(low).reshape(experts, capacity, width)
-    buffer, grad_arrived, other_arrived = barrier(buffer, grad_arrived, other_arrived)
     arrived = crossing(buffer).reshape(slots_all, width)
+    columns = 2 * expert_in.shape[3]
+    flat_master = expert_in[0].transpose(1, 2, 0).reshape(columns, width)
+    flat_low = flat_master.astype(low)
+    wide_router = jnp.pad(router_full, ((0, 0), (0, LANES - experts)))
     plain_grad = dot_nt(grad_arrived, expand_out)
-    arrived, plain_grad = barrier(arrived, plain_grad)
-    logits = dot_nn(arrived, router_full)
-    names = jnp.arange(experts, dtype=jnp.int32)[None, :]
-    contrast = (names == here).astype(jnp.float32) - (names == other_arrived[:, None]).astype(
-        jnp.float32
-    )
-    gate = jax.nn.sigmoid(jnp.sum(logits * contrast, 1, keepdims=True))
-    mixed_up = jnp.einsum("sd,dgf->sgf", arrived, expand_in, preferred_element_type=jnp.float32)
-    hidden, pull = jax.vjp(gated_gelu, mixed_up)
-    gated_hidden = (gate * hidden).astype(low)
-    grad_gate = jnp.sum(plain_grad * hidden, 1, keepdims=True)
-    grad_choice = (gate * (1.0 - gate) * grad_gate * contrast).astype(low)
-    grad_mixed_up = pull(gate * plain_grad)[0].astype(low)
-    sent_grads = (
-        jnp.einsum("sgf,dgf->sd", grad_mixed_up, expand_in, preferred_element_type=jnp.float32)
-        + dot_nt(grad_choice, router_full)
-    ).astype(low)
+    arrived, plain_grad, flat_low, wide_router = barrier(arrived, plain_grad, flat_low, wide_router)
+    sent_grads, gated_hidden, grad_mixed_up, grad_choice = expert_chain(
+        arrived,
+        plain_grad,
+        other_arrived[:, None],
+        jnp.full((8, LANES), here, jnp.int32),
+        flat_low,
+        wide_router,
+    )
     back_grads = crossing(sent_grads.reshape(experts, capacity, width)).reshape(slots_all, width)
 
     sent_rows = dot_nn(gated_hidden, expand_out).astype(low)
-    grad_router = dot_tn(arrived, grad_choice)
+    grad_router = dot_tn(arrived, grad_choice)[:, :experts]
     grad_expand_out = dot_tn(gated_hidden, grad_arrived)
     shrink_left, shrink_right, shrink_new = precondition(
         grad_expand_out, expert_out[0], expert_out_left, expert_out_right
     )
     grad_expand_in = jnp.einsum(
-        "sgf,sd->gfd", grad_mixed_up, arrived, preferred_element_type=jnp.float32
+        "gsf,sd->gfd", grad_mixed_up, arrived, preferred_element_type=jnp.float32
     )
     back_grads, sent_rows, grad_router, grad_expand_out, grad_expand_in, shrink_left, shrink_right, shrink_new = barrier(
         back_grads, sent_rows, grad_router, grad_expand_out, grad_expand_in, shrink_left, shrink_right, shrink_new
@@ -997,7 +1193,7 @@
     grad_attention = grad_middle.astype(low)
     grad_mixed = dot_nt(grad_attention, exit_own).astype(low)
     grad_query, key_value_grad, sums, result_sum = attend_back(
-        query, jnp.stack(pairs), grad_mixed, mixed, jnp.concatenate(logs, 0), back_lines, result_part
+        query, key_value, grad_mixed, mixed, logs, back_lines, result_part
     )
     result = (middle + result_sum.astype(jnp.float32)).astype(low)
     grad_projected = jnp.stack(
@@ -1024,7 +1220,7 @@
         preferred_element_type=jnp.float32,
     )
     gain_sums = jnp.stack([grad_gain_first, jnp.where(tp_here == 0, grad_gain_second, 0.0)])
-    peak_own = jnp.concatenate(peak_parts)
+    peak_own = peak_own[:, :, 0].reshape(local_heads)
     pieces = [
         grad_router.reshape(shards, -1),
         gain_sums.reshape(2, shards, depth).transpose(1, 0, 2).reshape(shards, -1),
@@ -1038,14 +1234,18 @@
         spots.append(spots[-1] + padded[-1].shape[1] // LANES)
     small = jnp.concatenate(padded, 1)
     small = jnp.pad(small, ((0, 0), (0, -small.shape[1] % (8 * LANES)))).reshape(shards, -1, LANES)
-    columns = grad_expand_in.shape[0] * grad_expand_in.shape[1]
-    flat_master = expert_in[0].transpose(1, 2, 0).reshape(columns, width)
     size = jnp.sqrt(jnp.mean(flat_master * flat_master) + step_epsilon)
-    first_part, small, entry_terms, exit_terms = barrier(
-        grad_first_part.astype(low), small, grad_entry, grad_exit
-    )
-    entry_terms = crossing(entry_terms.reshape(shards, depth, 3 * head_cols))
-    exit_terms = crossing(exit_terms.reshape(head_cols, shards, depth).transpose(1, 0, 2))
+    weight_terms = jnp.concatenate(
+        [
+            grad_entry.reshape(shards, 3 * depth, head_cols),
+            grad_exit.reshape(head_cols, shards, depth)
+            .transpose(1, 0, 2)
+            .reshape(shards, depth, head_cols),
+        ],
+        1,
+    )
+    first_part, small, weight_terms = barrier(grad_first_part.astype(low), small, weight_terms)
+    weight_terms = crossing(weight_terms)
     expand_right, expand_left, expand_new, grad_first, small_sum = tail(
         first_part,
         small,
@@ -1056,11 +1256,10 @@
         expert_in_right,
         flat_master,
     )
-    grad_first, entry_terms, exit_terms = barrier(grad_first, entry_terms, exit_terms)
-    owned_in = (
-        jnp.sum(entry_terms.astype(jnp.float32), 0).reshape(depth, 3, head_cols).transpose(1, 0, 2)
-    )
-    owned_out = jnp.sum(exit_terms.astype(jnp.float32), 0)
+    grad_first, weight_terms = barrier(grad_first, weight_terms)
+    owned = jnp.sum(weight_terms.astype(jnp.float32), 0)
+    owned_in = owned[: 3 * depth].reshape(depth, 3, head_cols).transpose(1, 0, 2)
+    owned_out = owned[3 * depth :].reshape(head_cols, depth)
     grad_tokens = grad_middle + pull(grad_first.astype(jnp.float32))[0]
 
     def small_piece(number, shape):

time: 746 us -> 708 us (0.949)
  Pallas kernels: 249 us -> 352 us
  waiting for transfers between devices: 123 us -> 56 us
  matrix products: 160 us -> 113 us
  blocking collectives: 19.7 us -> 0 us
  other arithmetic: 65.9 us -> 57.7 us
    pallas_call x2, Pallas kernels: 24.8 us -> 128 us  [the longest x1 91 us: attend(): pl.pallas_call(functools.partial(attend_kernel, length, rows, tile, pairs...]
    all_gather x4 -> x0, waiting for transfers between devices: 40.6 us -> none  [the longest x2 23 us: on_device(): mixed_all = lax.all_gather(mixed_part, 'tp', axis=1, tiled=True)]
    dot_general x3 -> x1, matrix products: 38.1 us -> 11.8 us  [on_device(): jnp.einsum('gsf,sd->gfd', grad_mixed_up, arrived, preferred_element_type=...]
    all_to_all x7 -> x5, waiting for transfers between devices: 74.1 us -> 49.1 us  [crossing(): lax.all_to_all(values, ('fsdp', 'ctx'), split_axis=0, concat_axis=0, tile...]
    all_gather x1 -> x0, blocking collectives: 19.7 us -> none  [on_device(): lax.all_gather(attention_out.astype(low), ('fsdp', 'ctx'), axis=1, tiled=...]
    dot_general x9 -> x7, matrix products: 54 us -> 37.2 us  [dot_nn(): lax.dot_general(left, right, (((1,), (0,)), ((), ())), preferred_element_...]
    unnamed x169 -> x141, local copies, waits for them, and re-layouts: 30.4 us -> 21 us
    broadcast_in_dim x1 -> x0, other arithmetic: 8.96 us -> none  [gated_gelu(): return jax.nn.gelu(both[..., 0, :], approximate=True) * both[..., 1, :]]
  transfers between devices with their start and end apart: 15 -> 9, of which waited for: 7 -> 3; matrix products, arithmetic and copies ran while one was open for 23% -> 20% of each run, Pallas kernels for 23% -> 33%
where the time goes in v3:
time: 708 us; the launch traced here: 698 us
  Pallas kernels  352 us (50%)
  matrix products  113 us (16%)
  local copies, waits for them, and re-layouts  69.4 us (10%)
  other arithmetic  57.7 us (8%)
  waiting for transfers between devices  56 us (8%)
  starting transfers between devices  30.4 us (4%)
  between operations  18.7 us (3%)
    pallas_call x1, Pallas kernels, attend(): pl.pallas_call(functools.partial(attend_kernel, length, rows, tile, pairs...  91 us
    pallas_call x1, Pallas kernels, attend_back(): pl.pallas_call(functools.partial(attend_back_kernel, length, rows, tile,...  82.6 us
    pallas_call x1, Pallas kernels, tail(): pl.pallas_call(functools.partial(tail_kernel, n_fsdp, n_ctx, n_tp, (right...  72.5 us
    pallas_call x1, Pallas kernels, combine_sum(): pl.pallas_call(functools.partial(combine_sum_kernel, lax.axis_size('tp'))...  69.5 us
    all_to_all x5, waiting for transfers between devices, crossing(): lax.all_to_all(values, ('fsdp', 'ctx'), split_axis=0, concat_axis=0, tile...  49.1 us
    dot_general x7, matrix products, dot_nn(): lax.dot_general(left, right, (((1,), (0,)), ((), ())), preferred_element_...  37.2 us
    pallas_call x1, Pallas kernels, expert_chain(): pl.pallas_call(expert_kernel, grid=(count // tile,), in_specs=[pl.BlockSp...  36.9 us
    dot_general x7, matrix products, dot_tn(): lax.dot_general(left, right, (((0,), (0,)), ((), ())), preferred_element_...  30.4 us
  transfers between devices with their start and end apart: 9, of which 3 were waited for; matrix products, arithmetic and copies ran while one was open for 20% of the time, Pallas kernels for 33%

profile of v3, /device:TPU:0, one launch (start us, length us, event | category | flops | bytes accessed | tf_op | source)
XLA Modules:
  0.0 697.9 jit_solution(165929746718978126)
XLA Ops:
  23.3 5.2 all-to-all-start.1
  29.0 9.0 %fusion.8 = bf16[2560,1024]{1,0:T(8,128)(2,1)} fusion(bf16[1024,1024]{1,0:T(8,128)(2,1)} %param.23, s32[1024]{0:T(1024)S(1)} %get-tuple-element.241, s32[1024]{0:T(1024)S(1)} %get-tuple-element.240), kind=kOutput, calls=%fused_computation.17 | convolution fusion | flops 5379194880 | bytes 7348224 | tf_op jit(solution)/shard_map/dot_general | solution.py:35
  38.0 6.9 all-gather.3.cloned.1.call-done
  68.3 91.0 %shard_map.421 = (bf16[1024,256]{1,0:T(8,128)(2,1)}, f32[2,2,1024]{2,1,0:T(2,128)}, f32[2,2,128]{2,1,0:T(2,128)}, bf16[2,2,2048,128]{3,2,1,0:T(8,128)(2,1)}, bf1...) custom-call(bf16[1024,256]{1,0:T(8,128)(2,1)} %fusion.68.q_ref, ...), custom_call_target="tpu_custom_call" | custom-call | flops 53687091200 | bytes 4194304 | tf_op jit(solution)/shard_map/pallas_call | solution.py:208
  166.7 7.9 %fusion.11 = bf16[2560,1024]{1,0:T(8,128)(2,1)} fusion(s32[1024]{0:T(1024)S(1)} %get-tuple-element.241, s32[1024]{0:T(1024)S(1)} %get-tuple-element.240, f32[1024,1024]{1,0:T(8,128)S(1)} %get-tuple-element.262, f32[1024]{0:T(1024)S(1)} %get-tuple-element.259, f32[1024]{0:T(1024)S(1)} %fusion.101), kind=kOutput, calls=%fused_computation.18 | convolution fusion | flops 5382340608 | bytes 9453568 | tf_op jit(solution)/shard_map/dot_general | solution.py:35
  174.6 5.4 all-to-all-start
  189.1 10.2 %fusion.47 = f32[2560,704]{0,1:T(8,128)} fusion(bf16[2560,1024]{1,0:T(8,128)(2,1)} %bitcast.289, f32[1,704,1024]{2,1,0:T(8,128)} %param.32), kind=kOutput, calls=%fused_computation.70 | convolution fusion | flops 3691708416 | bytes 15335424 | tf_op jit(solution)/shard_map/dot_general | solution.py:31
  199.3 40.1 %all-to-all-done = bf16[8,320,1024]{2,1,0:T(8,128)(2,1)} async-done(((bf16[8,320,1024]{2,1,0:T(8,128)(2,1)}), bf16[8,320,1024]{2,1,0:T(8,128)(2,1)}, u32[]{:S(2)}, u32[]{:S(2)}) %all-to-all-start) | async-done | bytes 5242912 | tf_op jit(solution)/shard_map/all_to_all | solution.py:1013
  239.4 8.8 %copy.168.plain_ref = f32[2560,704]{1,0:T(8,128)} copy(f32[2560,704]{0,1:T(8,128)} %fusion.47) | data formatting | bytes 14417920 | tf_op jit(solution)/shard_map/optimization_barrier | solution.py:1009
  250.5 36.9 %shard_map.422 = (bf16[2560,1024]{1,0:T(8,128)(2,1)}, bf16[2560,704]{1,0:T(8,128)(2,1)}, bf16[2,2560,704]{2,1,0:T(8,128)(2,1)}, bf16[2560,128]{1,0:T(8,128)(2,1)S(1)}) custom-call(bf16[2560,1024]{1,0:T(8,128)(2,1)} %bitcast.23.x_ref, f32[2560,704]{1,0:T(8,128)} %copy.168.plain_ref, s32[2560,1]{1,0:T(8,128)S(1)} %copy-done.2, ...), custom_call_target="tpu_custom_call" | custom-call | flops 14763950080 | bytes 41943040 | tf_op jit(solution)/shard_map/pallas_call | solution.py:952
  287.4 4.8 all-to-all-start.2
  292.2 9.2 %fusion.128 = f32[704,1024]{1,0:T(8,128)} fusion(bf16[2560,704]{1,0:T(8,128)(2,1)} %get-tuple-element.73, bf16[2560,1024]{1,0:T(8,128)(2,1)} %bitcast.290), kind=kOutput, calls=%fused_computation.205 | convolution fusion | flops 3690987520 | bytes 11730944 | tf_op jit(solution)/shard_map/dot_general | solution.py:39
  301.4 7.3 %multiply_reduce_fusion.1 = (f32[]{:T(128)}, f32[704,1024]{1,0:T(8,128)S(1)}) fusion(f32[2,1024,1024]{2,1,0:T(8,128)} %param.40, f32[2,704,704]{2,1,0:T(8,128)} %param.39, f32[704,1024]{1,0:T(8,128)} %fusion.128), kind=kOutput, calls=%fused_computation.54 | convolution fusion | flops 2494300160 | bytes 8945668 | tf_op jit(solution)/shard_map/dot_general | solution.py:35
  315.8 5.0 fusion.36
  324.8 6.1 fusion.125
  330.9 11.8 %fusion.14 = f32[2,704,1024]{2,1,0:T(8,128)} fusion(bf16[2,2560,704]{2,1,0:T(8,128)(2,1)S(1)} %bitcast.296, bf16[2560,1024]{1,0:T(8,128)(2,1)} %bitcast.23.x_ref), kind=kOutput, calls=%fused_computation.21 | convolution fusion | flops 7381975040 | bytes 18219008 | tf_op jit(solution)/shard_map/gsf,sd->gfd/dot_general | solution.py:1178
  342.7 9.0 %all-to-all-done.2 = bf16[8,320,1024]{2,1,0:T(8,128)(2,1)} async-done(((bf16[8,320,1024]{2,1,0:T(8,128)(2,1)}), bf16[8,320,1024]{2,1,0:T(8,128)(2,1)}, u32[]{:S(2)}, u32[]{:S(2)}) %all-to-all-start.2) | async-done | bytes 5242912 | tf_op jit(solution)/shard_map/all_to_all | solution.py:1013
  369.1 69.5 %shard_map.423 = bf16[1024,1024]{1,0:T(8,128)(2,1)S(1)} custom-call(s32[1024,2]{1,0:T(8,128)S(1)} %copy-done.1, bf16[2560,1024]{1,0:T(8,128)(2,1)} %bitcast.32.back_ref), custom_call_target="tpu_custom_call" | custom-call | flops 5368709120 | bytes 209715200 | tf_op jit(solution)/shard_map/pallas_call | solution.py:476
  446.2 9.4 %fusion.43.part_ref = bf16[1024,1024]{1,0:T(8,128)(2,1)} fusion(bf16[2560,1024]{1,0:T(8,128)(2,1)} %bitcast.40, s32[1024]{0:T(1024)S(1)} %copy-done.47, s32[1024]{0:T(1024)S(1)} %copy-done.45), kind=kOutput, calls=%fused_computation.64 | convolution fusion | flops 5377622016 | bytes 7348224 | tf_op jit(solution)/shard_map/dot_general | solution.py:39
  456.3 82.6 %shard_map.424 = (bf16[1024,256]{1,0:T(8,128)(2,1)}, bf16[2,1024,256]{2,1,0:T(8,128)(2,1)}, f32[2,2,3072]{2,1,0:T(2,128)}, bf16[1024,1024]{1,0:T(8,128)(2,1)}) custom-call(bf16[1024,256]{1,0:T(8,128)(2,1)} %fusion.68.q_ref, bf16[2,2,2048,128]{3,2,1,0:T(8,128)(2,1)} %get-tuple-element.66.k_ref.v_ref, bf16[2,2,2048,128]{3,2,1,0:T(8,128)(2,1)} %get-tuple-element.66.k_ref.v_ref, ...), custom_call_target="tpu_custom_call" | custom-call | flops 21474836480 | bytes 12582912 | tf_op jit(solution)/shard_map/pallas_call | solution.py:652
  556.8 5.0 reshape.354
  569.9 72.5 %shard_map.425 = (f32[1408,1408]{1,0:T(8,128)}, f32[1024,1024]{1,0:T(8,128)}, f32[1408,1024]{1,0:T(8,128)}, bf16[1024,1024]{1,0:T(8,128)(2,1)}, f32[16,128]{1,0:T(8,128)}) custom-call(bf16[1024,1024]{1,0:T(8,128)(2,1)} %get-tuple-element.88.part_ref, f32[8,16,128]{2,1,0:T(8,128)} %bitcast.279, bf16[1408,1024]{1,0:T(8,128)(2,1)} %bitcast.265, ...), custom_call_target="tpu_custom_call" | custom-call | flops 28051505152 | bytes 251658240 | tf_op jit(solution)/shard_map/pallas_call | solution.py:864
  647.5 5.0 add_convert_fusion
  678.5 7.1 %copy.219 = f32[1,1024,2,704]{1,3,2,0:T(8,128)} copy(f32[1,1024,2,704]{1,3,2,0:T(8,128)} %bitcast.255) | data formatting | bytes 11534336
  (285 shorter events, 153.8 us)
Async XLA Ops:
  7.2 37.7 %all-gather.3.cloned.1.call-start = ((), (), s32[]{:S(2)}) async-start(), calls=%async_computation.5 | async-start | bytes 2433024 | tf_op jit(solution)/shard_map/all_gather | solution.py:1064
  13.8 14.7 %copy-start.38 = (s32[4095]{0:T(1024)S(1)}, s32[4095]{0:T(1024)}, u32[]{:S(2)}) copy-start(s32[4095]{0:T(1024)} %param.25) | copy-start | bytes 49144
  13.8 14.7 %copy-start.8 = (bf16[1024,1024]{1,0:T(8,128)(2,1)S(1)}, bf16[1024,1024]{1,0:T(8,128)(2,1)}, u32[]{:S(2)}) copy-start(bf16[1024,1024]{1,0:T(8,128)(2,1)} %param.22) | copy-start | bytes 6291460
  20.4 144.3 %copy-start.44 = (s32[1024]{0:T(1024)}, s32[1024]{0:T(1024)S(1)}, u32[]{:S(2)}) copy-start(s32[1024]{0:T(1024)S(1)} %get-tuple-element.240) | copy-start | bytes 12292
  20.4 144.3 %copy-start.46 = (s32[1024]{0:T(1024)}, s32[1024]{0:T(1024)S(1)}, u32[]{:S(2)}) copy-start(s32[1024]{0:T(1024)S(1)} %get-tuple-element.241) | copy-start | bytes 12292
  23.3 151.3 %all-to-all-start.1 = ((s32[8,1,320]{2,1,0:T(1,128)}), s32[8,1,320]{2,1,0:T(1,128)S(1)}, u32[]{:S(2)}, u32[]{:S(2)}) async-start(s32[8,1,320]{2,1,0:T(1,128)} %all_to_all.19), calls=%async_computation.1 | async-start | bytes 24576 | tf_op jit(solution)/shard_map/all_to_all | solution.py:1013
  28.5 39.0 %copy-start.26 = (s32[3072]{0:T(1024)}, s32[3072]{0:T(1024)S(1)}, u32[]{:S(2)}) copy-start(s32[3072]{0:T(1024)S(1)} %pad_dynamic-slice_fusion) | copy-start | bytes 36868
  29.0 25.9 %copy-start.29 = (f32[1024]{0:T(1024)}, f32[1024]{0:T(1024)S(1)}, u32[]{:S(2)}) copy-start(f32[1024]{0:T(1024)S(1)} %fusion.100) | copy-start | bytes 12292
  61.7 97.8 %copy-start.12 = (bf16[8,256,128]{1,2,0:T(8,128)(2,1)}, bf16[8,256,128]{1,2,0:T(8,128)(2,1)S(1)}, u32[]{:S(2)}) copy-start(bf16[8,256,128]{1,2,0:T(8,128)(2,1)S(1)} %copy.166) | copy-start | bytes 1572868
  61.7 97.9 %collective-permute-start = (bf16[256,1024]{0,1:T(8,128)(2,1)S(1)}, bf16[256,1024]{0,1:T(8,128)(2,1)}, u32[]{:S(2)}, u32[]{:S(2)}) collective-permute-start(bf16[256,1024]{0,1:T(8,128)(2,1)S(1)} %bitcast.259), channel_id=1, source_target_pairs={{0,1},{1,2},{2,3},{3,0},{4,5},{5,6},{6,7},{7,4},{8,9},{9,10},{10,1... | collective-permute-start | bytes 1572872 | tf_op jit(solution)/shard_map/ppermute | solution.py:1142
  63.2 97.7 %collective-permute-start.1 = (bf16[256,1024]{0,1:T(8,128)(2,1)S(1)}, bf16[256,1024]{0,1:T(8,128)(2,1)}, u32[]{:S(2)}, u32[]{:S(2)}) collective-permute-start(bf16[256,1024]{0,1:T(8,128)(2,1)S(1)} %bitcast.260), channel_id=1, source_target_pairs={{0,2},{1,3},{2,0},{3,1},{4,6},{5,7},{6,4},{7,5},{8,10},{9,11},{10,... | collective-permute-start | bytes 1572872 | tf_op jit(solution)/shard_map/ppermute | solution.py:1142
  65.6 96.4 %collective-permute-start.2 = (bf16[256,1024]{0,1:T(8,128)(2,1)S(1)}, bf16[256,1024]{0,1:T(8,128)(2,1)S(1)}, u32[]{:S(2)}, u32[]{:S(2)}) collective-permute-start(bf16[256,1024]{0,1:T(8,128)(2,1)S(1)} %bitcast.261), channel_id=1, source_target_pairs={{0,3},{1,0},{2,1},{3,2},{4,7},{5,4},{6,5},{7,6},{8,11},{9,8},{10,9... | collective-permute-start | bytes 1572872 | tf_op jit(solution)/shard_map/ppermute | solution.py:1142
  67.4 91.8 %copy-start.51 = (bf16[4,32]{1,0:T(4,128)(2,1)}, bf16[4,32]{1,0:T(4,128)(2,1)S(1)}, u32[]{:S(2)}) copy-start(bf16[4,32]{1,0:T(4,128)(2,1)S(1)} %copy.162) | copy-start | bytes 772
  174.6 64.8 %all-to-all-start = ((bf16[8,320,1024]{2,1,0:T(8,128)(2,1)}), bf16[8,320,1024]{2,1,0:T(8,128)(2,1)}, u32[]{:S(2)}, u32[]{:S(2)}) async-start(bf16[8,320,1024]{2,1,0:T(8,128)(2,1)} %bitcast.257), calls=%async_computation | async-start | bytes 10485760 | tf_op jit(solution)/shard_map/all_to_all | solution.py:1013
  287.4 64.3 %all-to-all-start.2 = ((bf16[8,320,1024]{2,1,0:T(8,128)(2,1)}), bf16[8,320,1024]{2,1,0:T(8,128)(2,1)}, u32[]{:S(2)}, u32[]{:S(2)}) async-start(bf16[8,320,1024]{2,1,0:T(8,128)(2,1)} %bitcast.258), calls=%async_computation.2 | async-start | bytes 10485760 | tf_op jit(solution)/shard_map/all_to_all | solution.py:1013
  351.7 86.8 %all-to-all-start.3 = ((bf16[8,320,1024]{2,1,0:T(8,128)(2,1)}), bf16[8,320,1024]{2,1,0:T(8,128)(2,1)}, u32[]{:S(2)}, u32[]{:S(2)}) async-start(bf16[8,320,1024]{2,1,0:T(8,128)(2,1)} %bitcast.256), calls=%async_computation.3 | async-start | bytes 10485760 | tf_op jit(solution)/shard_map/all_to_all | solution.py:1013
  369.1 69.5 %copy-start.32 = (f32[1024]{0:T(1024)S(1)}, f32[1024]{0:T(1024)}, u32[]{:S(2)}) copy-start(f32[1024]{0:T(1024)} %copy-done.31) | copy-start | bytes 12292
  564.7 87.8 %all-to-all-start.4 = ((bf16[8,512,256]{2,1,0:T(8,128)(2,1)}), bf16[8,512,256]{2,1,0:T(8,128)(2,1)}, u32[]{:S(2)}, u32[]{:S(2)}) async-start(bf16[8,512,256]{2,1,0:T(8,128)(2,1)} %pad_maximum_fusion), calls=%async_computation.4 | async-start | bytes 4194304 | tf_op jit(solution)/shard_map/all_to_all | solution.py:1013
  569.9 75.1 %copy-start.53 = (f32[2,128]{1,0:T(2,128)S(1)}, f32[2,128]{1,0:T(2,128)}, u32[]{:S(2)}) copy-start(f32[2,128]{1,0:T(2,128)} %param.29) | copy-start | bytes 3076
  569.9 75.1 %copy-start.54 = (f32[2,128]{1,0:T(2,128)S(1)}, f32[2,128]{1,0:T(2,128)}, u32[]{:S(2)}) copy-start(f32[2,128]{1,0:T(2,128)} %param.42) | copy-start | bytes 3076
  569.9 76.4 %copy-start.43 = (f32[4,4]{1,0:T(4,128)S(1)}, f32[4,4]{1,0:T(4,128)}, u32[]{:S(2)}) copy-start(f32[4,4]{1,0:T(4,128)} %param.30) | copy-start | bytes 196
  569.9 76.4 %copy-start.49 = (f32[4,4]{1,0:T(4,128)S(1)}, f32[4,4]{1,0:T(4,128)}, u32[]{:S(2)}) copy-start(f32[4,4]{1,0:T(4,128)} %param.43) | copy-start | bytes 196
  569.9 77.0 %copy-start.39 = (f32[128,8]{0,1:T(8,128)S(1)}, f32[128,8]{0,1:T(8,128)}, u32[]{:S(2)}) copy-start(f32[128,8]{0,1:T(8,128)} %param.28) | copy-start | bytes 12292
  569.9 77.0 %copy-start.48 = (f32[128,8]{0,1:T(8,128)S(1)}, f32[128,8]{0,1:T(8,128)}, u32[]{:S(2)}) copy-start(f32[128,8]{0,1:T(8,128)} %param.41) | copy-start | bytes 12292
  (52 other events, 283.5 us)
Sparse Core Ops, SparseCore 0:
  13.9 30.8 all-gather.2

commit v4 on v3

--- a/solution.py
+++ b/solution.py
@@ -272,9 +272,8 @@
 
 
 class LineSum:
-    lag = 3
-
-    def __init__(self, axis, count, size, pairs, own, left, right, stage, total, sems):
+    def __init__(self, axis, count, size, pairs, own, left, right, stage, total, sems, lag):
+        self.lag = lag
         self.axis, self.count, self.size, self.pairs = axis, count, size, pairs
         self.own, self.left, self.right, self.stage, self.total = own, left, right, stage, total
         self.part_send, self.left_got, self.right_got, self.total_got, self.down_send, self.up_send = (
@@ -435,12 +434,13 @@
 
 
 SUM_ROWS = 16
+BACK_ROWS = 32
 
 
 def combine_sum_kernel(count, slots_ref, back_ref, out_ref, own, left, right, stage, total, sems):
     rows, width = own.shape
     places = back_ref.shape[0]
-    line = LineSum("tp", count, SUM_ROWS, rows // SUM_ROWS // 2, own, left, right, stage, total, sems)
+    line = LineSum("tp", count, SUM_ROWS, rows // SUM_ROWS // 2, own, left, right, stage, total, sems, 3)
     barrier = pltpu.get_barrier_semaphore()
     line.signal_neighbours(barrier)
     size, depth = 256, 512
@@ -497,7 +497,7 @@
     last = length // LANES - 1
     here = lax.axis_index("ctx")
     turn = pair * steps + step
-    line_sum = LineSum("tp", n_tp, SUM_ROWS, part_ref.shape[0] // SUM_ROWS // 2, part_ref, left, right, stage, total, sems)
+    line_sum = LineSum("tp", n_tp, BACK_ROWS, part_ref.shape[0] // BACK_ROWS // 2, part_ref, left, right, stage, total, sems, 2)
     barrier = pltpu.get_barrier_semaphore()
 
     def swap(slot, peer):
@@ -684,7 +684,7 @@
             pltpu.SemaphoreType.DMA((pairs, n_ctx)),
             pltpu.SemaphoreType.DMA((pairs, n_ctx)),
         ]
-        + LineSum.scratch(rows, width, SUM_ROWS),
+        + LineSum.scratch(rows, width, BACK_ROWS),
         compiler_params=pltpu.CompilerParams(
             collective_id=1, has_side_effects=True, vmem_limit_bytes=60 * MIB
         ),
@@ -731,7 +731,7 @@
     turn = pl.program_id(0)
     turns = pl.num_programs(0)
     rights, lefts = blocks
-    line = LineSum("tp", n_tp, SUM_ROWS, part_ref.shape[0] // SUM_ROWS // 2, part_ref, left, right, stage, total, sems)
+    line = LineSum("tp", n_tp, BACK_ROWS, part_ref.shape[0] // BACK_ROWS // 2, part_ref, left, right, stage, total, sems, 2)
     here = lax.axis_index("fsdp") * n_ctx + lax.axis_index("ctx")
     tp_here = lax.axis_index("tp")
     shards = n_fsdp * n_ctx
@@ -901,7 +901,7 @@
             pltpu.SemaphoreType.DMA((n_tp,)),
             pltpu.SemaphoreType.DMA((n_tp,)),
         ]
-        + LineSum.scratch(rows, width, SUM_ROWS),
+        + LineSum.scratch(rows, width, BACK_ROWS),
         compiler_params=pltpu.CompilerParams(
             collective_id=2, has_side_effects=True, vmem_limit_bytes=56 * MIB
         ),
@@ -915,7 +915,7 @@
 GELU_B = 0.044715
 
 
-def expert_kernel(x_ref, plain_ref, other_ref, here_ref, w_ref, router_ref, sent_ref, hidden_ref, mixed_ref, choice_ref):
+def expert_kernel(x_ref, grad_ref, other_ref, here_ref, w_ref, out_ref, router_ref, sent_ref, hidden_ref, mixed_ref, choice_ref):
     half = w_ref.shape[0] // 2
     rows = x_ref[...]
     first = dot_nt(rows, w_ref[:half, :])
@@ -930,7 +930,7 @@
     gelu = first * rise
     slope = rise + 0.5 * GELU_A * first * (1.0 - bent * bent) * (1.0 + 3.0 * GELU_B * square)
     hidden = gelu * second
-    plain = plain_ref[...]
+    plain = dot_nt(grad_ref[...], out_ref[...])
     grad_gate = jnp.sum(plain * hidden, 1, keepdims=True)
     choice = (gate * (1.0 - gate) * grad_gate * contrast).astype(jnp.bfloat16)
     scaled = gate * plain
@@ -944,7 +944,7 @@
     sent_ref[...] = (sent + dot_nt(choice, router_ref[...])).astype(jnp.bfloat16)
 
 
-def expert_chain(rows, plain, other, here, weight, router):
+def expert_chain(rows, grads, other, here, weight, weight_out, router):
     count, width = rows.shape
     half = weight.shape[0] // 2
     tile = 320
@@ -954,8 +954,9 @@
         grid=(count // tile,),
         in_specs=[
             pl.BlockSpec((tile, width), lambda t: (t, 0)),
-            pl.BlockSpec((tile, half), lambda t: (t, 0)),
+            pl.BlockSpec((tile, width), lambda t: (t, 0)),
             pl.BlockSpec((tile, 1), lambda t: (t, 0)),
+            vmem,
             vmem,
             vmem,
             vmem,
@@ -976,7 +977,7 @@
         cost_estimate=pl.CostEstimate(
             flops=8 * count * width * half, bytes_accessed=16 * count * width, transcendentals=count * half
         ),
-    )(rows, plain, other, here, weight, router)
+    )(rows, grads, other, here, weight, weight_out, router)
 
 
 def normalize(values, gain):
@@ -1065,7 +1066,6 @@
         jnp.concatenate(
             [
                 attention_in.astype(low).reshape(3 * depth, head_cols),
-                attention_out.astype(low).reshape(depth, head_cols),
                 small,
             ],
             0,
@@ -1080,13 +1080,7 @@
         .transpose(1, 0, 2, 3)
         .reshape(3, width, head_cols)
     )
-    exit_own = (
-        gathered[:, 3 * depth : 4 * depth]
-        .reshape(shards, head_cols, depth)
-        .transpose(1, 0, 2)
-        .reshape(head_cols, width)
-    )
-    small = gathered[:, 4 * depth :].reshape(shards, -1)
+    small = gathered[:, 3 * depth :].reshape(shards, -1)
     router_full = small[:, : sizes[0]].reshape(width, experts)
     gains_full = (
         small[:, sizes[0] : sizes[0] + sizes[1]]
@@ -1135,14 +1129,17 @@
     back_lines = lax.dot_general(
         table_full, hits_back, (((0,), (1,)), ((), ())), preferred_element_type=jnp.float32
     ).reshape(head_pairs, 2, span)
-    exit_all = lax.dynamic_update_slice_in_dim(
-        jnp.zeros((n_tp * head_cols, width), low), exit_own, tp_here * head_cols, 0
+    exit_piece = attention_out.astype(low)
+    exit_rows = lax.dynamic_update_slice_in_dim(
+        jnp.zeros((n_tp * head_cols, depth), low), exit_piece, tp_here * head_cols, 0
     )
     for shift in range(1, n_tp):
-        piece = lax.ppermute(exit_own, "tp", [(i, (i + shift) % n_tp) for i in range(n_tp)])
-        exit_all = lax.dynamic_update_slice_in_dim(
-            exit_all, piece, (tp_here + n_tp - shift) % n_tp * head_cols, 0
+        piece = lax.ppermute(exit_piece, "tp", [(i, (i + shift) % n_tp) for i in range(n_tp)])
+        exit_rows = lax.dynamic_update_slice_in_dim(
+            exit_rows, piece, (tp_here + n_tp - shift) % n_tp * head_cols, 0
         )
+    exit_all = lax.all_gather(exit_rows, ("fsdp", "ctx"), axis=1, tiled=True)
+    exit_own = lax.dynamic_slice_in_dim(exit_all, tp_here * head_cols, head_cols, 0)
     mixed, logs, peak_own, key_value, mixed_all, grad_arrived = attend(
         query, own_pairs, lines, grad_buffer
     )
@@ -1157,14 +1154,14 @@
     flat_master = expert_in[0].transpose(1, 2, 0).reshape(columns, width)
     flat_low = flat_master.astype(low)
     wide_router = jnp.pad(router_full, ((0, 0), (0, LANES - experts)))
-    plain_grad = dot_nt(grad_arrived, expand_out)
-    arrived, plain_grad, flat_low, wide_router = barrier(arrived, plain_grad, flat_low, wide_router)
+    arrived, low_out, flat_low, wide_router = barrier(arrived, expand_out, flat_low, wide_router)
     sent_grads, gated_hidden, grad_mixed_up, grad_choice = expert_chain(
         arrived,
-        plain_grad,
+        grad_arrived,
         other_arrived[:, None],
         jnp.full((8, LANES), here, jnp.int32),
         flat_low,
+        low_out,
         wide_router,
     )
     back_grads = crossing(sent_grads.reshape(experts, capacity, width)).reshape(slots_all, width)

time: 708 us -> 684 us (0.966)
  local copies, waits for them, and re-layouts: 69.4 us -> 55.4 us
    dot_general x5 -> x4, matrix products: 21 us -> 11.4 us  [dot_nt(): lax.dot_general(left, right, (((1,), (1,)), ((), ())), preferred_element_...]
    optimization_barrier x2 -> x1, local copies, waits for them, and re-layouts: 8.99 us -> 0.19 us  [barrier(): return lax.optimization_barrier(values)]
    all_to_all x5, waiting for transfers between devices: 49.1 us -> 57 us  [crossing(): lax.all_to_all(values, ('fsdp', 'ctx'), split_axis=0, concat_axis=0, tile...]
    unnamed x141 -> x115, local copies, waits for them, and re-layouts: 21 us -> 21 us
  transfers between devices with their start and end apart: 9 -> 10, of which waited for: 3 -> 2; matrix products, arithmetic and copies ran while one was open for 20% -> 20% of each run, Pallas kernels for 33% -> 34%
where the time goes in v4:
time: 684 us; the launch traced here: 678 us
  Pallas kernels  345 us (50%)
  matrix products  109 us (16%)
  other arithmetic  62.6 us (9%)
  waiting for transfers between devices  57.1 us (8%)
  local copies, waits for them, and re-layouts  55.4 us (8%)
  starting transfers between devices  30.1 us (4%)
  between operations  18.7 us (3%)
    pallas_call x1, Pallas kernels, attend(): pl.pallas_call(functools.partial(attend_kernel, length, rows, tile, pairs...  89.7 us
    pallas_call x1, Pallas kernels, attend_back(): pl.pallas_call(functools.partial(attend_back_kernel, length, rows, tile,...  81.6 us
    pallas_call x1, Pallas kernels, tail(): pl.pallas_call(functools.partial(tail_kernel, n_fsdp, n_ctx, n_tp, (right...  73.8 us
    pallas_call x1, Pallas kernels, combine_sum(): pl.pallas_call(functools.partial(combine_sum_kernel, lax.axis_size('tp'))...  69.4 us
    all_to_all x5, waiting for transfers between devices, crossing(): lax.all_to_all(values, ('fsdp', 'ctx'), split_axis=0, concat_axis=0, tile...  57 us
    dot_general x7, matrix products, dot_nn(): lax.dot_general(left, right, (((1,), (0,)), ((), ())), preferred_element_...  41.5 us
    dot_general x7, matrix products, dot_tn(): lax.dot_general(left, right, (((0,), (0,)), ((), ())), preferred_element_...  31.2 us
    pallas_call x1, Pallas kernels, expert_chain(): pl.pallas_call(expert_kernel, grid=(count // tile,), in_specs=[pl.BlockSp...  30.6 us
  transfers between devices with their start and end apart: 10, of which 2 were waited for; matrix products, arithmetic and copies ran while one was open for 20% of the time, Pallas kernels for 34%

profile of v4, /device:TPU:0, one launch (start us, length us, event | category | flops | bytes accessed | tf_op | source)
XLA Modules:
  0.0 677.8 jit_solution(16413507140691345273)
XLA Ops:
  35.5 9.0 %fusion.8 = bf16[2560,1024]{1,0:T(8,128)(2,1)} fusion(bf16[1024,1024]{1,0:T(8,128)(2,1)} %param.23, s32[1024]{0:T(1024)S(1)} %get-tuple-element.241, s32[1024]{0:T(1024)S(1)} %get-tuple-element.240), kind=kOutput, calls=%fused_computation.17 | convolution fusion | flops 5379194880 | bytes 7348224 | tf_op jit(solution)/shard_map/dot_general | solution.py:35
  62.4 89.7 %shard_map.421 = (bf16[1024,256]{1,0:T(8,128)(2,1)}, f32[2,2,1024]{2,1,0:T(2,128)}, f32[2,2,128]{2,1,0:T(2,128)}, bf16[2,2,2048,128]{3,2,1,0:T(8,128)(2,1)}, bf1...) custom-call(bf16[1024,256]{1,0:T(8,128)(2,1)} %fusion.65.q_ref, ...), custom_call_target="tpu_custom_call" | custom-call | flops 53687091200 | bytes 4194304 | tf_op jit(solution)/shard_map/pallas_call | solution.py:208
  152.1 4.7 multiply_reduce_fusion
  158.8 8.3 %fusion.11 = bf16[2560,1024]{1,0:T(8,128)(2,1)} fusion(s32[1024]{0:T(1024)S(1)} %get-tuple-element.241, s32[1024]{0:T(1024)S(1)} %get-tuple-element.240, f32[1024,1024]{1,0:T(8,128)S(1)} %get-tuple-element.262, f32[1024]{0:T(1024)S(1)} %get-tuple-element.259, f32[1024]{0:T(1024)S(1)} %fusion.99), kind=kOutput, calls=%fused_computation.18 | convolution fusion | flops 5382340608 | bytes 9453568 | tf_op jit(solution)/shard_map/dot_general | solution.py:35
  167.1 4.9 all-to-all-start
  183.1 48.9 %all-to-all-done = bf16[8,320,1024]{2,1,0:T(8,128)(2,1)} async-done(((bf16[8,320,1024]{2,1,0:T(8,128)(2,1)}), bf16[8,320,1024]{2,1,0:T(8,128)(2,1)}, u32[]{:S(2)}, u32[]{:S(2)}) %all-to-all-start) | async-done | bytes 5242912 | tf_op jit(solution)/shard_map/all_to_all | solution.py:1014
  233.0 30.6 %shard_map.422 = (bf16[2560,1024]{1,0:T(8,128)(2,1)}, bf16[2560,704]{1,0:T(8,128)(2,1)}, bf16[2,2560,704]{2,1,0:T(8,128)(2,1)}, bf16[2560,128]{1,0:T(8,128)(2,1)S(1)}) custom-call(bf16[2560,1024]{1,0:T(8,128)(2,1)} %bitcast.20.x_ref, bf16[2560,1024]{1,0:T(8,128)(2,1)} %bitcast.266, s32[2560,1]{1,0:T(8,128)S(1)} %broadcast_in_dim_reshape.5.other_ref, ...), custom_call_target="tpu_custom_call" | custom-call | flops 14763950080 | bytes 41943040 | tf_op jit(solution)/shard_map/pallas_call | solution.py:952
  263.6 4.9 all-to-all-start.2
  268.5 9.2 %fusion.123 = f32[704,1024]{1,0:T(8,128)} fusion(bf16[2560,704]{1,0:T(8,128)(2,1)} %get-tuple-element.73, bf16[2560,1024]{1,0:T(8,128)(2,1)} %bitcast.267), kind=kOutput, calls=%fused_computation.202 | convolution fusion | flops 3690987520 | bytes 11730944 | tf_op jit(solution)/shard_map/dot_general | solution.py:39
  277.7 8.7 %multiply_reduce_fusion.1 = (f32[]{:T(128)}, f32[704,1024]{1,0:T(8,128)}) fusion(f32[2,1024,1024]{2,1,0:T(8,128)} %param.40, f32[2,704,704]{2,1,0:T(8,128)} %param.39, f32[704,1024]{1,0:T(8,128)} %fusion.123), kind=kOutput, calls=%fused_computation.54 | convolution fusion | flops 2494300160 | bytes 8945668 | tf_op jit(solution)/shard_map/dot_general | solution.py:35
  293.6 5.0 fusion.36
  302.5 5.9 convolution_convert_fusion
  308.4 11.6 %fusion.14 = f32[2,704,1024]{2,1,0:T(8,128)} fusion(bf16[2,2560,704]{2,1,0:T(8,128)(2,1)S(1)} %bitcast.273, bf16[2560,1024]{1,0:T(8,128)(2,1)} %bitcast.20.x_ref), kind=kOutput, calls=%fused_computation.21 | convolution fusion | flops 7381975040 | bytes 18219008 | tf_op jit(solution)/shard_map/gsf,sd->gfd/dot_general | solution.py:1175
  320.0 8.0 %all-to-all-done.2 = bf16[8,320,1024]{2,1,0:T(8,128)(2,1)} async-done(((bf16[8,320,1024]{2,1,0:T(8,128)(2,1)}), bf16[8,320,1024]{2,1,0:T(8,128)(2,1)}, u32[]{:S(2)}, u32[]{:S(2)}) %all-to-all-start.2) | async-done | bytes 5242912 | tf_op jit(solution)/shard_map/all_to_all | solution.py:1014
  328.0 4.8 all-to-all-start.3
  332.9 4.7 fusion.7
  341.2 4.7 convert_element_type.206
  346.0 69.4 %shard_map.423 = bf16[1024,1024]{1,0:T(8,128)(2,1)S(1)} custom-call(s32[1024,2]{1,0:T(8,128)S(1)} %copy-done.1, bf16[2560,1024]{1,0:T(8,128)(2,1)} %bitcast.29.back_ref), custom_call_target="tpu_custom_call" | custom-call | flops 5368709120 | bytes 209715200 | tf_op jit(solution)/shard_map/pallas_call | solution.py:476
  420.9 10.9 %fusion.43.part_ref = bf16[1024,1024]{1,0:T(8,128)(2,1)} fusion(bf16[2560,1024]{1,0:T(8,128)(2,1)} %bitcast.36, s32[1024]{0:T(1024)S(1)} %get-tuple-element.241, s32[1024]{0:T(1024)S(1)} %get-tuple-element.240), kind=kOutput, calls=%fused_computation.64 | convolution fusion | flops 5377622016 | bytes 7348224 | tf_op jit(solution)/shard_map/dot_general | solution.py:39
  435.1 81.6 %shard_map.424 = (bf16[1024,256]{1,0:T(8,128)(2,1)}, bf16[2,1024,256]{2,1,0:T(8,128)(2,1)}, f32[2,2,3072]{2,1,0:T(2,128)}, bf16[1024,1024]{1,0:T(8,128)(2,1)}) custom-call(bf16[1024,256]{1,0:T(8,128)(2,1)} %fusion.65.q_ref, bf16[2,2,2048,128]{3,2,1,0:T(8,128)(2,1)} %get-tuple-element.66.k_ref.v_ref, bf16[2,2,2048,128]{3,2,1,0:T(8,128)(2,1)} %get-tuple-element.66.k_ref.v_ref, ...), custom_call_target="tpu_custom_call" | custom-call | flops 21474836480 | bytes 12582912 | tf_op jit(solution)/shard_map/pallas_call | solution.py:652
  534.7 5.0 reshape.341
  547.8 73.8 %shard_map.425 = (f32[1408,1408]{1,0:T(8,128)}, f32[1024,1024]{1,0:T(8,128)}, f32[1408,1024]{1,0:T(8,128)}, bf16[1024,1024]{1,0:T(8,128)(2,1)}, f32[16,128]{1,0:T(8,128)}) custom-call(bf16[1024,1024]{1,0:T(8,128)(2,1)} %get-tuple-element.88.part_ref, f32[8,16,128]{2,1,0:T(8,128)} %bitcast.256, bf16[1408,1024]{1,0:T(8,128)(2,1)} %bitcast.243, ...), custom_call_target="tpu_custom_call" | custom-call | flops 28051505152 | bytes 251658240 | tf_op jit(solution)/shard_map/pallas_call | solution.py:864
  626.7 5.0 add_convert_fusion
  658.4 7.1 %copy.210 = f32[1,1024,2,704]{1,3,2,0:T(8,128)} copy(f32[1,1024,2,704]{1,3,2,0:T(8,128)} %bitcast.238) | data formatting | bytes 11534336
  (257 shorter events, 142.7 us)
Async XLA Ops:
  7.2 20.8 %copy-start.23 = (s32[1024,2]{0,1:T(2,128)S(1)}, s32[1024,2]{0,1:T(2,128)}, u32[]{:S(2)}) copy-start(s32[1024,2]{0,1:T(2,128)} %param.24) | copy-start | bytes 24580
  7.2 38.9 %all-gather.6.cloned.1.call-start = ((), (), s32[]{:S(2)}) async-start(), calls=%async_computation.6 | async-start | bytes 1843200 | tf_op jit(solution)/shard_map/all_gather | solution.py:1065
  7.3 27.7 %copy-start.7 = (bf16[1024,1024]{1,0:T(8,128)(2,1)S(1)}, bf16[1024,1024]{1,0:T(8,128)(2,1)}, u32[]{:S(2)}) copy-start(bf16[1024,1024]{1,0:T(8,128)(2,1)} %param.22) | copy-start | bytes 6291460
  9.0 35.4 %collective-permute-start = (bf16[256,128]{1,0:T(8,128)(2,1)}, bf16[256,128]{1,0:T(8,128)(2,1)}, u32[]{:S(2)}, u32[]{:S(2)}) collective-permute-start(bf16[256,128]{1,0:T(8,128)(2,1)} %get-tuple-element.250), channel_id=1, source_target_pairs={{0,1},{1,2},{2,3},{3,0},{4,5},{5,6},{6,7},{7,4},{8,9},{9,10},{10,1... | collective-permute-start | bytes 196616 | tf_op jit(solution)/shard_map/ppermute | solution.py:1137
  12.1 33.3 %collective-permute-start.1 = (bf16[256,128]{1,0:T(8,128)(2,1)}, bf16[256,128]{1,0:T(8,128)(2,1)S(1)}, u32[]{:S(2)}, u32[]{:S(2)}) collective-permute-start(bf16[256,128]{1,0:T(8,128)(2,1)} %get-tuple-element.250), channel_id=1, source_target_pairs={{0,2},{1,3},{2,0},{3,1},{4,6},{5,7},{6,4},{7,5},{8,10},{9,11},{10,... | collective-permute-start | bytes 196616 | tf_op jit(solution)/shard_map/ppermute | solution.py:1137
  14.6 30.7 %collective-permute-start.2 = (bf16[256,128]{1,0:T(8,128)(2,1)}, bf16[256,128]{1,0:T(8,128)(2,1)S(1)}, u32[]{:S(2)}, u32[]{:S(2)}) collective-permute-start(bf16[256,128]{1,0:T(8,128)(2,1)} %get-tuple-element.250), channel_id=1, source_target_pairs={{0,3},{1,0},{2,1},{3,2},{4,7},{5,4},{6,5},{7,6},{8,11},{9,8},{10,9... | collective-permute-start | bytes 196616 | tf_op jit(solution)/shard_map/ppermute | solution.py:1137
  30.9 136.2 %all-to-all-start.1 = ((s32[8,1,320]{2,1,0:T(1,128)}), s32[8,1,320]{2,1,0:T(1,128)S(1)}, u32[]{:S(2)}, u32[]{:S(2)}) async-start(s32[8,1,320]{2,1,0:T(1,128)} %all_to_all.19), calls=%async_computation.1 | async-start | bytes 24576 | tf_op jit(solution)/shard_map/all_to_all | solution.py:1014
  34.6 117.5 %all-gather.4.cloned.1.call-start = ((), (), s32[]{:S(2)}) async-start(), calls=%async_computation.5 | async-start | bytes 2359296 | tf_op jit(solution)/shard_map/all_gather | solution.py:1141
  35.4 20.8 %copy-start.27 = (f32[1024]{0:T(1024)}, f32[1024]{0:T(1024)S(1)}, u32[]{:S(2)}) copy-start(f32[1024]{0:T(1024)S(1)} %fusion.98) | copy-start | bytes 12292
  44.4 17.2 %copy-start.24 = (s32[3072]{0:T(1024)}, s32[3072]{0:T(1024)S(1)}, u32[]{:S(2)}) copy-start(s32[3072]{0:T(1024)S(1)} %pad_dynamic-slice_fusion) | copy-start | bytes 36868
  167.1 64.9 %all-to-all-start = ((bf16[8,320,1024]{2,1,0:T(8,128)(2,1)}), bf16[8,320,1024]{2,1,0:T(8,128)(2,1)}, u32[]{:S(2)}, u32[]{:S(2)}) async-start(bf16[8,320,1024]{2,1,0:T(8,128)(2,1)} %bitcast.240), calls=%async_computation | async-start | bytes 10485760 | tf_op jit(solution)/shard_map/all_to_all | solution.py:1014
  263.6 64.4 %all-to-all-start.2 = ((bf16[8,320,1024]{2,1,0:T(8,128)(2,1)}), bf16[8,320,1024]{2,1,0:T(8,128)(2,1)}, u32[]{:S(2)}, u32[]{:S(2)}) async-start(bf16[8,320,1024]{2,1,0:T(8,128)(2,1)} %bitcast.241), calls=%async_computation.2 | async-start | bytes 10485760 | tf_op jit(solution)/shard_map/all_to_all | solution.py:1014
  287.1 11.5 %slice-start.3 = ((s8[8388608]{0:T(1024)(128)(4,1)}), s8[4194304]{0:T(1024)(128)(4,1)S(1)}, s32[]{:S(2)}) async-start(s8[8388608]{0:T(1024)(128)(4,1)} %bitcast.264), calls=%async_computation.10 | async-start | bytes 8388608
  328.0 87.4 %all-to-all-start.3 = ((bf16[8,320,1024]{2,1,0:T(8,128)(2,1)}), bf16[8,320,1024]{2,1,0:T(8,128)(2,1)}, u32[]{:S(2)}, u32[]{:S(2)}) async-start(bf16[8,320,1024]{2,1,0:T(8,128)(2,1)} %bitcast.239), calls=%async_computation.3 | async-start | bytes 10485760 | tf_op jit(solution)/shard_map/all_to_all | solution.py:1014
  420.9 11.6 %copy-start.3 = (f32[1024,1024]{1,0:T(8,128)}, f32[1024,1024]{1,0:T(8,128)S(1)}, u32[]{:S(2)}) copy-start(f32[1024,1024]{1,0:T(8,128)S(1)} %fusion.30) | copy-start | bytes 12582916
  420.9 10.9 %copy-start.20 = (bf16[1024,256]{1,0:T(8,128)(2,1)S(1)}, bf16[1024,256]{1,0:T(8,128)(2,1)}, u32[]{:S(2)}) copy-start(bf16[1024,256]{1,0:T(8,128)(2,1)} %get-tuple-element.79.m_ref) | copy-start | bytes 1572868
  542.6 89.0 %all-to-all-start.4 = ((bf16[8,512,256]{2,1,0:T(8,128)(2,1)}), bf16[8,512,256]{2,1,0:T(8,128)(2,1)}, u32[]{:S(2)}, u32[]{:S(2)}) async-start(bf16[8,512,256]{2,1,0:T(8,128)(2,1)} %pad_maximum_fusion), calls=%async_computation.4 | async-start | bytes 4194304 | tf_op jit(solution)/shard_map/all_to_all | solution.py:1014
  547.8 76.4 %copy-start.41 = (f32[2,128]{1,0:T(2,128)S(1)}, f32[2,128]{1,0:T(2,128)}, u32[]{:S(2)}) copy-start(f32[2,128]{1,0:T(2,128)} %param.29) | copy-start | bytes 3076
  547.8 76.4 %copy-start.42 = (f32[2,128]{1,0:T(2,128)S(1)}, f32[2,128]{1,0:T(2,128)}, u32[]{:S(2)}) copy-start(f32[2,128]{1,0:T(2,128)} %param.42) | copy-start | bytes 3076
  547.8 77.7 %copy-start.37 = (f32[4,4]{1,0:T(4,128)S(1)}, f32[4,4]{1,0:T(4,128)}, u32[]{:S(2)}) copy-start(f32[4,4]{1,0:T(4,128)} %param.30) | copy-start | bytes 196
  547.8 77.7 %copy-start.39 = (f32[4,4]{1,0:T(4,128)S(1)}, f32[4,4]{1,0:T(4,128)}, u32[]{:S(2)}) copy-start(f32[4,4]{1,0:T(4,128)} %param.43) | copy-start | bytes 196
  547.8 78.2 %copy-start.35 = (f32[128,8]{0,1:T(8,128)S(1)}, f32[128,8]{0,1:T(8,128)}, u32[]{:S(2)}) copy-start(f32[128,8]{0,1:T(8,128)} %param.28) | copy-start | bytes 12292
  547.8 78.2 %copy-start.38 = (f32[128,8]{0,1:T(8,128)S(1)}, f32[128,8]{0,1:T(8,128)}, u32[]{:S(2)}) copy-start(f32[128,8]{0,1:T(8,128)} %param.41) | copy-start | bytes 12292
  633.6 11.6 %copy-start.13 = (f32[512,256]{1,0:T(8,128)}, f32[512,256]{1,0:T(8,128)S(1)}, u32[]{:S(2)}) copy-start(f32[512,256]{1,0:T(8,128)S(1)} %convert_reduce_fusion) | copy-start | bytes 1572868
  (40 other events, 214.8 us)
Sparse Core Ops, SparseCore 0:
  21.0 24.3 all-gather.5
  47.8 33.7 all-gather.3

commit v5 on v4

--- a/solution.py
+++ b/solution.py
@@ -702,12 +702,10 @@
     small_ref,
     grad_ref,
     scale_ref,
-    s_right,
     p_right,
     s_left,
     p_left,
     w_ref,
-    new_right,
     new_left,
     new_w,
     total_ref,
@@ -795,9 +793,7 @@
     @pl.when(turn < rights)
     def _():
         spot = pl.ds(pl.multiple_of(turn * LANES, LANES), LANES)
-        grad = grad_ref[...]
-        new_right[...] = decay * s_right[...] + (1.0 - decay) * dot_nt(grad_ref[spot, :], grad)
-        turned[spot, :] = dot_nn(p_right[...].astype(jnp.bfloat16), grad).astype(jnp.bfloat16)
+        turned[spot, :] = dot_nn(p_right[...].astype(jnp.bfloat16), grad_ref[...]).astype(jnp.bfloat16)
 
     @pl.when((turn >= rights) & (turn < rights + lefts))
     def _():
@@ -869,21 +865,18 @@
             vmem,
             vmem,
             vmem,
-            pl.BlockSpec((None, LANES, deep), lambda t: (0, at_right(t), 0)),
             pl.BlockSpec((None, LANES, deep), lambda t: (1, at_right(t), 0)),
             pl.BlockSpec((None, LANES, wide), lambda t: (0, at_left(t), 0)),
             pl.BlockSpec((None, wide, LANES), lambda t: (1, 0, at_left(t))),
             pl.BlockSpec((LANES, wide), lambda t: (at_weight(t), 0)),
         ],
         out_specs=[
-            pl.BlockSpec((LANES, deep), lambda t: (at_right(t), 0)),
             pl.BlockSpec((LANES, wide), lambda t: (at_left(t), 0)),
             pl.BlockSpec((LANES, wide), lambda t: (at_weight(t), 0)),
             vmem,
             vmem,
         ],
         out_shape=[
-            jax.ShapeDtypeStruct((deep, deep), jnp.float32),
             jax.ShapeDtypeStruct((wide, wide), jnp.float32),
             jax.ShapeDtypeStruct((deep, wide), jnp.float32),
             jax.ShapeDtypeStruct((rows, width), jnp.bfloat16),
@@ -908,76 +901,122 @@
         cost_estimate=pl.CostEstimate(
             flops=8 * deep * wide * (deep + wide), bytes_accessed=240 * rows * width, transcendentals=0
         ),
-    )(part, small, grad, scale, right, right, left, left, weight)
+    )(part, small, grad, scale, right, left, left, weight)
 
 
 GELU_A = 0.7978845608028654
 GELU_B = 0.044715
 
 
-def expert_kernel(x_ref, grad_ref, other_ref, here_ref, w_ref, out_ref, router_ref, sent_ref, hidden_ref, mixed_ref, choice_ref):
+def expert_kernel(n_fsdp, n_ctx, slots_ref, second_ref, grad_ref, other_ref, w_ref, out_ref, router_ref, sent_ref, hidden_ref, mixed_ref, choice_ref, rows_out, stage, land, send, got, own_sem):
+    experts, capacity, width = stage.shape
     half = w_ref.shape[0] // 2
-    rows = x_ref[...]
-    first = dot_nt(rows, w_ref[:half, :])
-    second = dot_nt(rows, w_ref[half:, :])
-    logits = dot_nn(rows, router_ref[...])
-    lane = lax.broadcasted_iota(jnp.int32, logits.shape, 1)
-    contrast = (lane == here_ref[0:1, 0:1]).astype(jnp.float32) - (lane == other_ref[...]).astype(jnp.float32)
-    gate = jax.nn.sigmoid(jnp.sum(logits * contrast, 1, keepdims=True))
-    square = first * first
-    bent = jnp.tanh(GELU_A * first * (1.0 + GELU_B * square))
-    rise = 0.5 * (1.0 + bent)
-    gelu = first * rise
-    slope = rise + 0.5 * GELU_A * first * (1.0 - bent * bent) * (1.0 + 3.0 * GELU_B * square)
-    hidden = gelu * second
-    plain = dot_nt(grad_ref[...], out_ref[...])
-    grad_gate = jnp.sum(plain * hidden, 1, keepdims=True)
-    choice = (gate * (1.0 - gate) * grad_gate * contrast).astype(jnp.bfloat16)
-    scaled = gate * plain
-    grad_first = (scaled * second * slope).astype(jnp.bfloat16)
-    grad_second = (scaled * gelu).astype(jnp.bfloat16)
-    hidden_ref[...] = (gate * hidden).astype(jnp.bfloat16)
-    mixed_ref[0] = grad_first
-    mixed_ref[1] = grad_second
-    choice_ref[...] = choice
-    sent = dot_nn(grad_first, w_ref[:half, :]) + dot_nn(grad_second, w_ref[half:, :])
-    sent_ref[...] = (sent + dot_nt(choice, router_ref[...])).astype(jnp.bfloat16)
-
-
-def expert_chain(rows, grads, other, here, weight, weight_out, router):
-    count, width = rows.shape
+    rows_all = second_ref.shape[0]
+    here = lax.axis_index("fsdp") * n_ctx + lax.axis_index("ctx")
+    plane = [(f * n_ctx + c, {"fsdp": f, "ctx": c}) for f in range(n_fsdp) for c in range(n_ctx)]
+    other = jnp.where(here == 0, 1, 0)
+    barrier = pltpu.get_barrier_semaphore()
+    greet(barrier, here, plane)
+
+    def build(expert):
+        place = lax.broadcasted_iota(jnp.int32, (capacity, rows_all), 0) + expert * capacity
+        hit = (place == slots_ref[0:1, :]) | (place == slots_ref[1:2, :])
+        picks = jnp.where(hit, 1.0, 0.0).astype(jnp.bfloat16)
+        return dot_nn(picks, second_ref[...]).astype(jnp.bfloat16)
+
+    def copy_to(expert):
+        where = {"fsdp": expert // n_ctx, "ctx": expert % n_ctx}
+        return remote(stage.at[expert], land.at[here], send.at[expert], got.at[here], where)
+
+    land[here] = build(here)
+    pl.semaphore_wait(barrier, experts - 1)
+
+    def post(turn, carry):
+        expert = (here + turn) % experts
+        stage[expert] = build(expert)
+        copy_to(expert).start()
+        return carry
+
+    lax.fori_loop(1, experts, post, 0)
+
+    def compute(turn, carry):
+        source = (here + experts - turn) % experts
+
+        @pl.when(turn > 0)
+        def _():
+            where = {"fsdp": other // n_ctx, "ctx": other % n_ctx}
+            remote(land.at[source], land.at[source], got.at[source], got.at[source], where).wait_recv()
+
+        rows = land[source]
+        first = dot_nt(rows, w_ref[:half, :])
+        second = dot_nt(rows, w_ref[half:, :])
+        logits = dot_nn(rows, router_ref[...])
+        lane = lax.broadcasted_iota(jnp.int32, logits.shape, 1)
+        contrast = (lane == here).astype(jnp.float32) - (lane == other_ref[source]).astype(jnp.float32)
+        gate = jax.nn.sigmoid(jnp.sum(logits * contrast, 1, keepdims=True))
+        square = first * first
+        bent = jnp.tanh(GELU_A * first * (1.0 + GELU_B * square))
+        rise = 0.5 * (1.0 + bent)
+        gelu = first * rise
+        slope = rise + 0.5 * GELU_A * first * (1.0 - bent * bent) * (1.0 + 3.0 * GELU_B * square)
+        hidden = gelu * second
+        plain = dot_nt(grad_ref[source], out_ref[...])
+        grad_gate = jnp.sum(plain * hidden, 1, keepdims=True)
+        choice = (gate * (1.0 - gate) * grad_gate * contrast).astype(jnp.bfloat16)
+        scaled = gate * plain
+        grad_first = (scaled * second * slope).astype(jnp.bfloat16)
+        grad_second = (scaled * gelu).astype(jnp.bfloat16)
+        hidden_ref[source] = (gate * hidden).astype(jnp.bfloat16)
+        mixed_ref[0, source] = grad_first
+        mixed_ref[1, source] = grad_second
+        choice_ref[source] = choice
+        sent = dot_nn(grad_first, w_ref[:half, :]) + dot_nn(grad_second, w_ref[half:, :])
+        sent_ref[source] = (sent + dot_nt(choice, router_ref[...])).astype(jnp.bfloat16)
+        return carry
+
+    lax.fori_loop(0, experts, compute, 0)
+    keep = pltpu.make_async_copy(land, rows_out, own_sem)
+    keep.start()
+
+    def settle(turn, carry):
+        copy_to((here + turn) % experts).wait_send()
+        return carry
+
+    lax.fori_loop(1, experts, settle, 0)
+    keep.wait()
+
+
+def expert_chain(slots, second, grads, other, weight, weight_out, router):
+    experts, capacity, width = grads.shape
     half = weight.shape[0] // 2
-    tile = 320
+    n_fsdp, n_ctx = lax.axis_size("fsdp"), lax.axis_size("ctx")
     vmem = pl.BlockSpec(memory_space=pltpu.VMEM)
+    count = experts * capacity
     return pl.pallas_call(
-        expert_kernel,
-        grid=(count // tile,),
-        in_specs=[
-            pl.BlockSpec((tile, width), lambda t: (t, 0)),
-            pl.BlockSpec((tile, width), lambda t: (t, 0)),
-            pl.BlockSpec((tile, 1), lambda t: (t, 0)),
-            vmem,
-            vmem,
-            vmem,
-            vmem,
+        functools.partial(expert_kernel, n_fsdp, n_ctx),
+        in_specs=[vmem] * 7,
+        out_specs=[vmem] * 4 + [pl.BlockSpec(memory_space=pl.ANY)],
+        out_shape=[
+            jax.ShapeDtypeStruct((experts, capacity, width), jnp.bfloat16),
+            jax.ShapeDtypeStruct((experts, capacity, half), jnp.bfloat16),
+            jax.ShapeDtypeStruct((2, experts, capacity, half), jnp.bfloat16),
+            jax.ShapeDtypeStruct((experts, capacity, LANES), jnp.bfloat16),
+            jax.ShapeDtypeStruct((experts, capacity, width), jnp.bfloat16),
         ],
-        out_specs=[
-            pl.BlockSpec((tile, width), lambda t: (t, 0)),
-            pl.BlockSpec((tile, half), lambda t: (t, 0)),
-            pl.BlockSpec((2, tile, half), lambda t: (0, t, 0)),
-            pl.BlockSpec((tile, LANES), lambda t: (t, 0)),
+        scratch_shapes=[
+            pltpu.VMEM((experts, capacity, width), jnp.bfloat16),
+            pltpu.VMEM((experts, capacity, width), jnp.bfloat16),
+            pltpu.SemaphoreType.DMA((experts,)),
+            pltpu.SemaphoreType.DMA((experts,)),
+            pltpu.SemaphoreType.DMA,
         ],
-        out_shape=[
-            jax.ShapeDtypeStruct((count, width), jnp.bfloat16),
-            jax.ShapeDtypeStruct((count, half), jnp.bfloat16),
-            jax.ShapeDtypeStruct((2, count, half), jnp.bfloat16),
-            jax.ShapeDtypeStruct((count, LANES), jnp.bfloat16),
-        ],
-        compiler_params=pltpu.CompilerParams(vmem_limit_bytes=48 * MIB),
+        compiler_params=pltpu.CompilerParams(
+            collective_id=4, has_side_effects=True, vmem_limit_bytes=60 * MIB
+        ),
         cost_estimate=pl.CostEstimate(
-            flops=8 * count * width * half, bytes_accessed=16 * count * width, transcendentals=count * half
+            flops=20 * count * width * half, bytes_accessed=80 * count * width, transcendentals=count * half
         ),
-    )(rows, grads, other, here, weight, weight_out, router)
+    )(slots, second, grads, other, weight, weight_out, router)
 
 
 def normalize(values, gain):
@@ -1143,27 +1182,29 @@
     mixed, logs, peak_own, key_value, mixed_all, grad_arrived = attend(
         query, own_pairs, lines, grad_buffer
     )
-    grad_arrived = grad_arrived.reshape(slots_all, width)
     value = dot_nn(mixed_all, exit_all)
     middle = inputs + value
     second = normalize(middle, gain_second).astype(low)
 
-    buffer = dot_nn(picks, second).astype(low).reshape(experts, capacity, width)
-    arrived = crossing(buffer).reshape(slots_all, width)
     columns = 2 * expert_in.shape[3]
     flat_master = expert_in[0].transpose(1, 2, 0).reshape(columns, width)
     flat_low = flat_master.astype(low)
     wide_router = jnp.pad(router_full, ((0, 0), (0, LANES - experts)))
-    arrived, low_out, flat_low, wide_router = barrier(arrived, expand_out, flat_low, wide_router)
-    sent_grads, gated_hidden, grad_mixed_up, grad_choice = expert_chain(
-        arrived,
+    half = columns // 2
+    sent_grads, gated_hidden, grad_mixed_up, grad_choice, arrived = expert_chain(
+        slot_rows.T,
+        second,
         grad_arrived,
-        other_arrived[:, None],
-        jnp.full((8, LANES), here, jnp.int32),
+        other_arrived.reshape(experts, capacity, 1),
         flat_low,
-        low_out,
+        expand_out,
         wide_router,
     )
+    gated_hidden = gated_hidden.reshape(slots_all, half)
+    grad_mixed_up = grad_mixed_up.reshape(2, slots_all, half)
+    grad_choice = grad_choice.reshape(slots_all, LANES)
+    arrived = arrived.reshape(slots_all, width)
+    grad_arrived = grad_arrived.reshape(slots_all, width)
     back_grads = crossing(sent_grads.reshape(experts, capacity, width)).reshape(slots_all, width)
 
     sent_rows = dot_nn(gated_hidden, expand_out).astype(low)
@@ -1175,8 +1216,10 @@
     grad_expand_in = jnp.einsum(
         "gsf,sd->gfd", grad_mixed_up, arrived, preferred_element_type=jnp.float32
     )
-    back_grads, sent_rows, grad_router, grad_expand_out, grad_expand_in, shrink_left, shrink_right, shrink_new = barrier(
-        back_grads, sent_rows, grad_router, grad_expand_out, grad_expand_in, shrink_left, shrink_right, shrink_new
+    flat_grad = grad_expand_in.reshape(columns, width).astype(low)
+    expand_right = decay * expert_in_right[0] + (1.0 - decay) * dot_nt(flat_grad, flat_grad)
+    back_grads, sent_rows, grad_router, grad_expand_out, grad_expand_in, shrink_left, shrink_right, shrink_new, expand_right, flat_grad = barrier(
+        back_grads, sent_rows, grad_router, grad_expand_out, grad_expand_in, shrink_left, shrink_right, shrink_new, expand_right, flat_grad
     )
     grad_second = combine_sum(slot_rows, back_grads, rows)
 
@@ -1243,11 +1286,11 @@
     )
     first_part, small, weight_terms = barrier(grad_first_part.astype(low), small, weight_terms)
     weight_terms = crossing(weight_terms)
-    expand_right, expand_left, expand_new, grad_first, small_sum = tail(
+    expand_left, expand_new, grad_first, small_sum = tail(
         first_part,
         small,
         spots[2],
-        grad_expand_in.reshape(columns, width).astype(low),
+        flat_grad,
         jnp.full((8, LANES), matrix_rate * size, jnp.float32),
         expert_in_left,
         expert_in_right,

time: 684 us -> 670 us (0.980)
  waiting for transfers between devices: 57.1 us -> 0.09 us
  Pallas kernels: 345 us -> 387 us
    all_to_all x5 -> x4, waiting for transfers between devices: 57 us -> 0.01 us  [crossing(): lax.all_to_all(values, ('fsdp', 'ctx'), split_axis=0, concat_axis=0, tile...]
    pallas_call x1, Pallas kernels: 30.6 us -> 76.8 us  [expert_chain(): pl.pallas_call(functools.partial(expert_kernel, n_fsdp, n_ctx), in_specs=...]
    dot_general x7 -> x6, matrix products: 41.5 us -> 31.6 us  [dot_nn(): lax.dot_general(left, right, (((1,), (0,)), ((), ())), preferred_element_...]
    dot_general x4 -> x5, matrix products: 11.4 us -> 17.7 us  [dot_nt(): lax.dot_general(left, right, (((1,), (1,)), ((), ())), preferred_element_...]
    unnamed x115 -> x130, local copies, waits for them, and re-layouts: 21 us -> 16.4 us
    all_to_all x5 -> x4, starting transfers between devices: 22.9 us -> 23.2 us  [crossing(): lax.all_to_all(values, ('fsdp', 'ctx'), split_axis=0, concat_axis=0, tile...]
  transfers between devices with their start and end apart: 10 -> 9, of which waited for: 2 -> 0; matrix products, arithmetic and copies ran while one was open for 20% -> 20% of each run, Pallas kernels for 34% -> 34%
where the time goes in v5:
time: 670 us; the launch traced here: 662 us
  Pallas kernels  387 us (58%)
  matrix products  106 us (16%)
  other arithmetic  66.6 us (10%)
  local copies, waits for them, and re-layouts  53.9 us (8%)
  starting transfers between devices  30.3 us (5%)
  between operations  19 us (3%)
    pallas_call x1, Pallas kernels, attend(): pl.pallas_call(functools.partial(attend_kernel, length, rows, tile, pairs...  85.7 us
    pallas_call x1, Pallas kernels, attend_back(): pl.pallas_call(functools.partial(attend_back_kernel, length, rows, tile,...  83.1 us
    pallas_call x1, Pallas kernels, expert_chain(): pl.pallas_call(functools.partial(expert_kernel, n_fsdp, n_ctx), in_specs=...  76.8 us
    pallas_call x1, Pallas kernels, tail(): pl.pallas_call(functools.partial(tail_kernel, n_fsdp, n_ctx, n_tp, (right...  71.5 us
    pallas_call x1, Pallas kernels, combine_sum(): pl.pallas_call(functools.partial(combine_sum_kernel, lax.axis_size('tp'))...  69.8 us
    dot_general x6, matrix products, dot_nn(): lax.dot_general(left, right, (((1,), (0,)), ((), ())), preferred_element_...  31.6 us
    dot_general x7, matrix products, dot_tn(): lax.dot_general(left, right, (((0,), (0,)), ((), ())), preferred_element_...  31.4 us
    all_to_all x4, starting transfers between devices, crossing(): lax.all_to_all(values, ('fsdp', 'ctx'), split_axis=0, concat_axis=0, tile...  23.2 us
  transfers between devices with their start and end apart: 9, of which 0 were waited for; matrix products, arithmetic and copies ran while one was open for 20% of the time, Pallas kernels for 34%

profile of v5, /device:TPU:0, one launch (start us, length us, event | category | flops | bytes accessed | tf_op | source)
XLA Modules:
  0.0 662.5 jit_solution(9944500843162732898)
XLA Ops:
  44.5 4.8 bitcast_convert_fusion.7.w_ref
  49.3 7.6 %fusion.7 = bf16[2560,1024]{1,0:T(8,128)(2,1)} fusion(bf16[1024,1024]{1,0:T(8,128)(2,1)S(1)} %copy-done.11, s32[1024]{0:T(1024)S(1)} %get-tuple-element.237, s32[1024]{0:T(1024)S(1)} %get-tuple-element.236), kind=kOutput, calls=%fused_computation.18 | convolution fusion | flops 5379194880 | bytes 7348224 | tf_op jit(solution)/shard_map/dot_general | solution.py:35
  79.0 85.7 %shard_map.421 = (bf16[1024,256]{1,0:T(8,128)(2,1)}, f32[2,2,1024]{2,1,0:T(2,128)}, f32[2,2,128]{2,1,0:T(2,128)}, bf16[2,2,2048,128]{3,2,1,0:T(8,128)(2,1)}, bf1...) custom-call(bf16[1024,256]{1,0:T(8,128)(2,1)} %fusion.60.q_ref, ...), custom_call_target="tpu_custom_call" | custom-call | flops 53687091200 | bytes 4194304 | tf_op jit(solution)/shard_map/pallas_call | solution.py:208
  164.8 4.7 multiply_reduce_fusion
  172.1 76.8 %shard_map.422 = (bf16[8,320,1024]{2,1,0:T(8,128)(2,1)}, bf16[8,320,704]{2,1,0:T(8,128)(2,1)}, bf16[2,8,320,704]{3,2,1,0:T(8,128)(2,1)}, bf16[8,320,128]{2,1,0:T(8,128)(2,1)}, bf16[8,320,1024]{2,1,0:T(8,128)(2,1)}) custom-call(s32[2,1024]{1,0:T(2,128)} %copy.160.slots_ref, bf16[1024,1024]{1,0:T(8,128)(2,1)} %multiply_convert_fusion.second_ref, ...), custom_call_target="tpu_custom_call" | custom-call | flops 36909875200 | bytes 209715200 | tf_op jit(solution)/shard_map/pallas_call | solution.py:995
  248.9 10.1 %all-to-all-start.1 = ((bf16[8,320,1024]{2,1,0:T(8,128)(2,1)}), bf16[8,320,1024]{2,1,0:T(8,128)(2,1)}, u32[]{:S(2)}, u32[]{:S(2)}) async-start(bf16[8,320,1024]{2,1,0:T(8,128)(2,1)} %get-tuple-element.66), calls=%async_computation.1 | async-start | bytes 10485760 | tf_op jit(solution)/shard_map/all_to_all | solution.py:1053
  259.0 7.1 %convolution_bitcast_fusion = f32[704,1024]{1,0:T(8,128)S(1)} fusion(bf16[8,320,704]{2,1,0:T(8,128)(2,1)} %get-tuple-element.67, bf16[8,320,1024]{2,1,0:T(8,128)(2,1)} %get-tuple-element.65.grad_ref), kind=kOutput, calls=%fused_computation.62 | convolution fusion | flops 3690987520 | bytes 11730944 | tf_op jit(solution)/shard_map/dot_general | solution.py:39
  267.7 6.0 fusion.28
  273.7 8.8 %multiply_reduce_fusion.1 = (f32[]{:T(128)}, f32[704,1024]{1,0:T(8,128)}) fusion(f32[2,1024,1024]{2,1,0:T(8,128)} %param.40, f32[2,704,704]{2,1,0:T(8,128)} %param.39, f32[704,1024]{1,0:T(8,128)} %copy-done.50), kind=kOutput, calls=%fused_computation.52 | convolution fusion | flops 2494300160 | bytes 8945668 | tf_op jit(solution)/shard_map/dot_general | solution.py:35
  291.0 4.4 fusion.33
  295.4 6.1 convolution_convert_fusion
  301.5 12.0 %fusion.114 = (bf16[2,704,1024]{2,1,0:T(8,128)(2,1)S(1)}, f32[2,704,1024]{2,1,0:T(8,128)}) fusion(bf16[2,8,320,704]{3,2,1,0:T(8,128)(2,1)} %get-tuple-element.70, bf16[8,320,1024]{2,1,0:T(8,128)(2,1)S(1)} %bitcast.286), kind=kOutput, calls=%fused_computation.201 | convolution fusion | flops 7383416832 | bytes 21102592 | tf_op jit(solution)/shard_map/gsf,sd->gfd/dot_general | solution.py:1216
  315.2 6.9 %fusion.1 = f32[1408,1408]{1,0:T(8,128)} fusion(bf16[1408,1024]{1,0:T(8,128)(2,1)S(1)} %bitcast.281, f32[2,1408,1408]{2,1,0:T(8,128)S(1)} %bitcast.276), kind=kOutput, calls=%fused_computation.5 | convolution fusion | flops 4064051200 | bytes 21626880 | tf_op jit(solution)/shard_map/dot_general | solution.py:31
  322.1 4.8 all-to-all-start.2
  327.1 4.8 fusion.6
  335.4 69.8 %shard_map.423 = bf16[1024,1024]{1,0:T(8,128)(2,1)S(1)} custom-call(s32[1024,2]{1,0:T(8,128)S(1)} %copy-done.1, bf16[2560,1024]{1,0:T(8,128)(2,1)} %bitcast.26.back_ref), custom_call_target="tpu_custom_call" | custom-call | flops 5368709120 | bytes 209715200 | tf_op jit(solution)/shard_map/pallas_call | solution.py:476
  410.8 10.8 %fusion.38.part_ref = bf16[1024,1024]{1,0:T(8,128)(2,1)} fusion(bf16[2560,1024]{1,0:T(8,128)(2,1)} %bitcast.41, s32[1024]{0:T(1024)S(1)} %copy-done.38, s32[1024]{0:T(1024)S(1)} %copy-done.36), kind=kOutput, calls=%fused_computation.61 | convolution fusion | flops 5377622016 | bytes 7348224 | tf_op jit(solution)/shard_map/dot_general | solution.py:39
  425.0 83.1 %shard_map.424 = (bf16[1024,256]{1,0:T(8,128)(2,1)}, bf16[2,1024,256]{2,1,0:T(8,128)(2,1)}, f32[2,2,3072]{2,1,0:T(2,128)}, bf16[1024,1024]{1,0:T(8,128)(2,1)}) custom-call(bf16[1024,256]{1,0:T(8,128)(2,1)} %fusion.60.q_ref, bf16[2,2,2048,128]{3,2,1,0:T(8,128)(2,1)} %get-tuple-element.64.k_ref.v_ref, bf16[2,2,2048,128]{3,2,1,0:T(8,128)(2,1)} %get-tuple-element.64.k_ref.v_ref, ...), custom_call_target="tpu_custom_call" | custom-call | flops 21474836480 | bytes 12582912 | tf_op jit(solution)/shard_map/pallas_call | solution.py:652
  510.0 4.5 bitcast_convert_fusion
  526.1 5.0 reshape.336
  534.0 4.7 all-to-all-start.3
  539.3 71.5 %shard_map.425 = (f32[1024,1024]{1,0:T(8,128)}, f32[1408,1024]{1,0:T(8,128)}, bf16[1024,1024]{1,0:T(8,128)(2,1)}, f32[16,128]{1,0:T(8,128)}) custom-call(bf16[1024,1024]{1,0:T(8,128)(2,1)} %get-tuple-element.83.part_ref, f32[8,16,128]{2,1,0:T(8,128)} %bitcast.267, bf16[1408,1024]{1,0:T(8,128)(2,1)} %bitcast.282, f32[8,128]{1,0:T(8,128)} %broadcast_in_dim.85.scale_ref, ...), custom_call_target="tpu_custom_call" | custom-call | flops 28051505152 | bytes 251658240 | tf_op jit(solution)/shard_map/pallas_call | solution.py:860
  615.8 5.0 add_convert_fusion
  646.8 6.3 copy.209
  (270 shorter events, 132.1 us)
Async XLA Ops:
  7.2 54.4 %all-gather.6.cloned.1.call-start = ((), (), s32[]{:S(2)}) async-start(), calls=%async_computation.5 | async-start | bytes 1843200 | tf_op jit(solution)/shard_map/all_gather | solution.py:1104
  8.9 51.0 %collective-permute-start = (bf16[256,128]{1,0:T(8,128)(2,1)}, bf16[256,128]{1,0:T(8,128)(2,1)}, u32[]{:S(2)}, u32[]{:S(2)}) collective-permute-start(bf16[256,128]{1,0:T(8,128)(2,1)} %get-tuple-element.246), channel_id=1, source_target_pairs={{0,1},{1,2},{2,3},{3,0},{4,5},{5,6},{6,7},{7,4},{8,9},{9,10},{10,1... | collective-permute-start | bytes 196616 | tf_op jit(solution)/shard_map/ppermute | solution.py:1176
  11.9 48.9 %collective-permute-start.1 = (bf16[256,128]{1,0:T(8,128)(2,1)}, bf16[256,128]{1,0:T(8,128)(2,1)S(1)}, u32[]{:S(2)}, u32[]{:S(2)}) collective-permute-start(bf16[256,128]{1,0:T(8,128)(2,1)} %get-tuple-element.246), channel_id=1, source_target_pairs={{0,2},{1,3},{2,0},{3,1},{4,6},{5,7},{6,4},{7,5},{8,10},{9,11},{10,... | collective-permute-start | bytes 196616 | tf_op jit(solution)/shard_map/ppermute | solution.py:1176
  14.5 46.3 %collective-permute-start.2 = (bf16[256,128]{1,0:T(8,128)(2,1)}, bf16[256,128]{1,0:T(8,128)(2,1)S(1)}, u32[]{:S(2)}, u32[]{:S(2)}) collective-permute-start(bf16[256,128]{1,0:T(8,128)(2,1)} %get-tuple-element.246), channel_id=1, source_target_pairs={{0,3},{1,0},{2,1},{3,2},{4,7},{5,4},{6,5},{7,6},{8,11},{9,8},{10,9... | collective-permute-start | bytes 196616 | tf_op jit(solution)/shard_map/ppermute | solution.py:1176
  20.7 16.9 %copy-start.6 = (bf16[1024,1024]{1,0:T(8,128)(2,1)S(1)}, bf16[1024,1024]{1,0:T(8,128)(2,1)}, u32[]{:S(2)}) copy-start(bf16[1024,1024]{1,0:T(8,128)(2,1)} %param.22) | copy-start | bytes 6291460
  30.5 26.6 %copy-start = (s32[1024,2]{1,0:T(8,128)}, s32[1024,2]{1,0:T(8,128)S(1)}, u32[]{:S(2)}) copy-start(s32[1024,2]{1,0:T(8,128)S(1)} %add.178.slots_ref) | copy-start | bytes 24580
  31.0 18.3 %copy-start.35 = (s32[1024]{0:T(1024)}, s32[1024]{0:T(1024)S(1)}, u32[]{:S(2)}) copy-start(s32[1024]{0:T(1024)S(1)} %get-tuple-element.236) | copy-start | bytes 12292
  31.0 18.3 %copy-start.37 = (s32[1024]{0:T(1024)}, s32[1024]{0:T(1024)S(1)}, u32[]{:S(2)}) copy-start(s32[1024]{0:T(1024)S(1)} %get-tuple-element.237) | copy-start | bytes 12292
  33.9 24.7 %all-to-all-start = ((s32[8,1,320]{2,1,0:T(1,128)}), s32[8,1,320]{2,1,0:T(1,128)S(1)}, u32[]{:S(2)}, u32[]{:S(2)}) async-start(s32[8,1,320]{2,1,0:T(1,128)} %all_to_all.15), calls=%async_computation | async-start | bytes 24576 | tf_op jit(solution)/shard_map/all_to_all | solution.py:1053
  37.6 127.2 %all-gather.4.cloned.1.call-start = ((), (), s32[]{:S(2)}) async-start(), calls=%async_computation.4 | async-start | bytes 2359296 | tf_op jit(solution)/shard_map/all_gather | solution.py:1180
  41.3 30.3 %copy-start.24 = (f32[1024]{0:T(1024)}, f32[1024]{0:T(1024)S(1)}, u32[]{:S(2)}) copy-start(f32[1024]{0:T(1024)S(1)} %fusion.93) | copy-start | bytes 12292
  57.0 21.2 %copy-start.21 = (s32[3072]{0:T(1024)}, s32[3072]{0:T(1024)S(1)}, u32[]{:S(2)}) copy-start(s32[3072]{0:T(1024)S(1)} %pad_dynamic-slice_fusion) | copy-start | bytes 36868
  77.1 87.7 %copy-start.44 = (bf16[4,32]{1,0:T(4,128)(2,1)}, bf16[4,32]{1,0:T(4,128)(2,1)S(1)}, u32[]{:S(2)}) copy-start(bf16[4,32]{1,0:T(4,128)(2,1)S(1)} %copy.155) | copy-start | bytes 772
  248.9 73.2 %all-to-all-start.1 = ((bf16[8,320,1024]{2,1,0:T(8,128)(2,1)}), bf16[8,320,1024]{2,1,0:T(8,128)(2,1)}, u32[]{:S(2)}, u32[]{:S(2)}) async-start(bf16[8,320,1024]{2,1,0:T(8,128)(2,1)} %get-tuple-element.66), calls=%async_computation.1 | async-start | bytes 10485760 | tf_op jit(solution)/shard_map/all_to_all | solution.py:1053
  295.4 19.8 %slice-start.1 = ((s8[15859712]{0:T(1024)(128)(4,1)}), s8[4194304]{0:T(1024)(128)(4,1)S(1)}, s32[]{:S(2)}) async-start(s8[15859712]{0:T(1024)(128)(4,1)} %bitcast.275), calls=%async_computation.7 | async-start | bytes 8388608
  295.4 19.8 %slice-start.2 = ((s8[15859712]{0:T(1024)(128)(4,1)}), s8[4194304]{0:T(1024)(128)(4,1)S(1)}, s32[]{:S(2)}) async-start(s8[15859712]{0:T(1024)(128)(4,1)} %bitcast.275), calls=%async_computation.8 | async-start | bytes 8388608
  322.1 83.1 %all-to-all-start.2 = ((bf16[8,320,1024]{2,1,0:T(8,128)(2,1)}), bf16[8,320,1024]{2,1,0:T(8,128)(2,1)}, u32[]{:S(2)}, u32[]{:S(2)}) async-start(bf16[8,320,1024]{2,1,0:T(8,128)(2,1)} %bitcast.253), calls=%async_computation.2 | async-start | bytes 10485760 | tf_op jit(solution)/shard_map/all_to_all | solution.py:1053
  534.0 86.8 %all-to-all-start.3 = ((bf16[8,512,256]{2,1,0:T(8,128)(2,1)}), bf16[8,512,256]{2,1,0:T(8,128)(2,1)}, u32[]{:S(2)}, u32[]{:S(2)}) async-start(bf16[8,512,256]{2,1,0:T(8,128)(2,1)} %pad_maximum_fusion), calls=%async_computation.3 | async-start | bytes 4194304 | tf_op jit(solution)/shard_map/all_to_all | solution.py:1053
  539.2 74.1 %copy-start.46 = (f32[2,128]{1,0:T(2,128)S(1)}, f32[2,128]{1,0:T(2,128)}, u32[]{:S(2)}) copy-start(f32[2,128]{1,0:T(2,128)} %param.29) | copy-start | bytes 3076
  539.2 74.1 %copy-start.47 = (f32[2,128]{1,0:T(2,128)S(1)}, f32[2,128]{1,0:T(2,128)}, u32[]{:S(2)}) copy-start(f32[2,128]{1,0:T(2,128)} %param.42) | copy-start | bytes 3076
  539.3 75.3 %copy-start.34 = (f32[4,4]{1,0:T(4,128)S(1)}, f32[4,4]{1,0:T(4,128)}, u32[]{:S(2)}) copy-start(f32[4,4]{1,0:T(4,128)} %param.30) | copy-start | bytes 196
  539.3 75.3 %copy-start.42 = (f32[4,4]{1,0:T(4,128)S(1)}, f32[4,4]{1,0:T(4,128)}, u32[]{:S(2)}) copy-start(f32[4,4]{1,0:T(4,128)} %param.43) | copy-start | bytes 196
  539.3 75.9 %copy-start.32 = (f32[128,8]{0,1:T(8,128)S(1)}, f32[128,8]{0,1:T(8,128)}, u32[]{:S(2)}) copy-start(f32[128,8]{0,1:T(8,128)} %param.28) | copy-start | bytes 12292
  539.3 75.9 %copy-start.39 = (f32[128,8]{0,1:T(8,128)S(1)}, f32[128,8]{0,1:T(8,128)}, u32[]{:S(2)}) copy-start(f32[128,8]{0,1:T(8,128)} %param.41) | copy-start | bytes 12292
  (47 other events, 283.4 us)
Sparse Core Ops, SparseCore 0:
  20.8 24.4 all-gather.5
  61.7 28.9 all-gather.3

commit v6 on v5

--- a/solution.py
+++ b/solution.py
@@ -908,7 +908,7 @@
 GELU_B = 0.044715
 
 
-def expert_kernel(n_fsdp, n_ctx, slots_ref, second_ref, grad_ref, other_ref, w_ref, out_ref, router_ref, sent_ref, hidden_ref, mixed_ref, choice_ref, rows_out, stage, land, send, got, own_sem):
+def expert_kernel(n_fsdp, n_ctx, slots_ref, second_ref, grad_ref, other_ref, w_ref, out_ref, router_ref, sent_ref, hidden_ref, mixed_ref, choice_ref, rows_out, stage, land, w_low, out_low, send, got, own_sem):
     experts, capacity, width = stage.shape
     half = w_ref.shape[0] // 2
     rows_all = second_ref.shape[0]
@@ -939,6 +939,15 @@
 
     lax.fori_loop(1, experts, post, 0)
 
+    def narrow(part, carry):
+        spot = pl.ds(pl.multiple_of(part * 64, 64), 64)
+        both = pl.ds(pl.multiple_of(part * 128, 128), 128)
+        w_low[both, :] = w_ref[both, :].astype(jnp.bfloat16)
+        out_low[spot, :] = out_ref[spot, :].astype(jnp.bfloat16)
+        return carry
+
+    lax.fori_loop(0, half // 64, narrow, 0)
+
     def compute(turn, carry):
         source = (here + experts - turn) % experts
 
@@ -948,8 +957,8 @@
             remote(land.at[source], land.at[source], got.at[source], got.at[source], where).wait_recv()
 
         rows = land[source]
-        first = dot_nt(rows, w_ref[:half, :])
-        second = dot_nt(rows, w_ref[half:, :])
+        first = dot_nt(rows, w_low[:half, :])
+        second = dot_nt(rows, w_low[half:, :])
         logits = dot_nn(rows, router_ref[...])
         lane = lax.broadcasted_iota(jnp.int32, logits.shape, 1)
         contrast = (lane == here).astype(jnp.float32) - (lane == other_ref[source]).astype(jnp.float32)
@@ -960,7 +969,7 @@
         gelu = first * rise
         slope = rise + 0.5 * GELU_A * first * (1.0 - bent * bent) * (1.0 + 3.0 * GELU_B * square)
         hidden = gelu * second
-        plain = dot_nt(grad_ref[source], out_ref[...])
+        plain = dot_nt(grad_ref[source], out_low[...])
         grad_gate = jnp.sum(plain * hidden, 1, keepdims=True)
         choice = (gate * (1.0 - gate) * grad_gate * contrast).astype(jnp.bfloat16)
         scaled = gate * plain
@@ -970,7 +979,7 @@
         mixed_ref[0, source] = grad_first
         mixed_ref[1, source] = grad_second
         choice_ref[source] = choice
-        sent = dot_nn(grad_first, w_ref[:half, :]) + dot_nn(grad_second, w_ref[half:, :])
+        sent = dot_nn(grad_first, w_low[:half, :]) + dot_nn(grad_second, w_low[half:, :])
         sent_ref[source] = (sent + dot_nt(choice, router_ref[...])).astype(jnp.bfloat16)
         return carry
 
@@ -1006,6 +1015,8 @@
         scratch_shapes=[
             pltpu.VMEM((experts, capacity, width), jnp.bfloat16),
             pltpu.VMEM((experts, capacity, width), jnp.bfloat16),
+            pltpu.VMEM((2 * half, width), jnp.bfloat16),
+            pltpu.VMEM((half, width), jnp.bfloat16),
             pltpu.SemaphoreType.DMA((experts,)),
             pltpu.SemaphoreType.DMA((experts,)),
             pltpu.SemaphoreType.DMA,
@@ -1188,7 +1199,6 @@
 
     columns = 2 * expert_in.shape[3]
     flat_master = expert_in[0].transpose(1, 2, 0).reshape(columns, width)
-    flat_low = flat_master.astype(low)
     wide_router = jnp.pad(router_full, ((0, 0), (0, LANES - experts)))
     half = columns // 2
     sent_grads, gated_hidden, grad_mixed_up, grad_choice, arrived = expert_chain(
@@ -1196,8 +1206,8 @@
         second,
         grad_arrived,
         other_arrived.reshape(experts, capacity, 1),
-        flat_low,
-        expand_out,
+        flat_master,
+        expert_out[0],
         wide_router,
     )
     gated_hidden = gated_hidden.reshape(slots_all, half)

time: 670 us -> 665 us (level)
  other arithmetic: 66.6 us -> 59.2 us
    convert_element_type x2 -> x0, other arithmetic: 7.99 us -> none  [the longest x1 4.82 us: on_device(): flat_low = flat_master.astype(low)]
  transfers between devices with their start and end apart: 9 -> 9, of which waited for: 0 -> 0; matrix products, arithmetic and copies ran while one was open for 20% -> 19% of each run, Pallas kernels for 34% -> 34%
where the time goes in v6:
time: 665 us; the launch traced here: 658 us
  Pallas kernels  389 us (58%)
  matrix products  104 us (16%)
  other arithmetic  59.2 us (9%)
  local copies, waits for them, and re-layouts  56.7 us (9%)
  starting transfers between devices  30.3 us (5%)
  between operations  19.1 us (3%)
    pallas_call x1, Pallas kernels, attend(): pl.pallas_call(functools.partial(attend_kernel, length, rows, tile, pairs...  85.7 us
    pallas_call x1, Pallas kernels, attend_back(): pl.pallas_call(functools.partial(attend_back_kernel, length, rows, tile,...  83.4 us
    pallas_call x1, Pallas kernels, expert_chain(): pl.pallas_call(functools.partial(expert_kernel, n_fsdp, n_ctx), in_specs=...  78.1 us
    pallas_call x1, Pallas kernels, tail(): pl.pallas_call(functools.partial(tail_kernel, n_fsdp, n_ctx, n_tp, (right...  71.5 us
    pallas_call x1, Pallas kernels, combine_sum(): pl.pallas_call(functools.partial(combine_sum_kernel, lax.axis_size('tp'))...  69.8 us
    dot_general x6, matrix products, dot_nn(): lax.dot_general(left, right, (((1,), (0,)), ((), ())), preferred_element_...  32.2 us
    dot_general x7, matrix products, dot_tn(): lax.dot_general(left, right, (((0,), (0,)), ((), ())), preferred_element_...  31.4 us
    all_to_all x4, starting transfers between devices, crossing(): lax.all_to_all(values, ('fsdp', 'ctx'), split_axis=0, concat_axis=0, tile...  23.3 us
  transfers between devices with their start and end apart: 9, of which 0 were waited for; matrix products, arithmetic and copies ran while one was open for 19% of the time, Pallas kernels for 34%

profile of v6, /device:TPU:0, one launch (start us, length us, event | category | flops | bytes accessed | tf_op | source)
XLA Modules:
  0.0 658.5 jit_solution(8607465225468800269)
XLA Ops:
  43.4 7.6 %fusion.7 = bf16[2560,1024]{1,0:T(8,128)(2,1)} fusion(bf16[1024,1024]{1,0:T(8,128)(2,1)S(1)} %copy-done.11, s32[1024]{0:T(1024)S(1)} %get-tuple-element.237, s32[1024]{0:T(1024)S(1)} %get-tuple-element.236), kind=kOutput, calls=%fused_computation.18 | convolution fusion | flops 5379194880 | bytes 7348224 | tf_op jit(solution)/shard_map/dot_general | solution.py:35
  73.1 85.7 %shard_map.421 = (bf16[1024,256]{1,0:T(8,128)(2,1)}, f32[2,2,1024]{2,1,0:T(2,128)}, f32[2,2,128]{2,1,0:T(2,128)}, bf16[2,2,2048,128]{3,2,1,0:T(8,128)(2,1)}, bf1...) custom-call(bf16[1024,256]{1,0:T(8,128)(2,1)} %fusion.59.q_ref, ...), custom_call_target="tpu_custom_call" | custom-call | flops 53687091200 | bytes 4194304 | tf_op jit(solution)/shard_map/pallas_call | solution.py:208
  158.8 4.7 multiply_reduce_fusion
  167.3 78.1 %shard_map.422 = (bf16[8,320,1024]{2,1,0:T(8,128)(2,1)}, bf16[8,320,704]{2,1,0:T(8,128)(2,1)}, bf16[2,8,320,704]{3,2,1,0:T(8,128)(2,1)}, bf16[8,320,128]{2,1,0:T(8,128)(2,1)}, bf16[8,320,1024]{2,1,0:T(8,128)(2,1)}) custom-call(s32[2,1024]{1,0:T(2,128)} %copy.160.slots_ref, bf16[1024,1024]{1,0:T(8,128)(2,1)} %multiply_convert_fusion.second_ref, ...), custom_call_target="tpu_custom_call" | custom-call | flops 36909875200 | bytes 209715200 | tf_op jit(solution)/shard_map/pallas_call | solution.py:1004
  245.4 10.1 %all-to-all-start.1 = ((bf16[8,320,1024]{2,1,0:T(8,128)(2,1)}), bf16[8,320,1024]{2,1,0:T(8,128)(2,1)}, u32[]{:S(2)}, u32[]{:S(2)}) async-start(bf16[8,320,1024]{2,1,0:T(8,128)(2,1)} %get-tuple-element.66), calls=%async_computation.1 | async-start | bytes 10485760 | tf_op jit(solution)/shard_map/all_to_all | solution.py:1064
  255.5 7.1 %convolution_bitcast_fusion = f32[704,1024]{1,0:T(8,128)S(1)} fusion(bf16[8,320,704]{2,1,0:T(8,128)(2,1)} %get-tuple-element.67, bf16[8,320,1024]{2,1,0:T(8,128)(2,1)} %get-tuple-element.65.grad_ref), kind=kOutput, calls=%fused_computation.60 | convolution fusion | flops 3690987520 | bytes 11730944 | tf_op jit(solution)/shard_map/dot_general | solution.py:39
  264.2 6.0 fusion.28
  270.2 8.8 %multiply_reduce_fusion.1 = (f32[]{:T(128)}, f32[704,1024]{1,0:T(8,128)}) fusion(f32[2,1024,1024]{2,1,0:T(8,128)} %param.40, f32[2,704,704]{2,1,0:T(8,128)} %param.39, f32[704,1024]{1,0:T(8,128)} %copy-done.48), kind=kOutput, calls=%fused_computation.49 | convolution fusion | flops 2494300160 | bytes 8945668 | tf_op jit(solution)/shard_map/dot_general | solution.py:35
  279.7 4.2 multiply_subtract_fusion
  290.3 6.1 convolution_convert_fusion
  296.4 12.0 %fusion.113 = (bf16[2,704,1024]{2,1,0:T(8,128)(2,1)S(1)}, f32[2,704,1024]{2,1,0:T(8,128)}) fusion(bf16[2,8,320,704]{3,2,1,0:T(8,128)(2,1)} %get-tuple-element.70, bf16[8,320,1024]{2,1,0:T(8,128)(2,1)S(1)} %bitcast.286), kind=kOutput, calls=%fused_computation.198 | convolution fusion | flops 7383416832 | bytes 21102592 | tf_op jit(solution)/shard_map/gsf,sd->gfd/dot_general | solution.py:1226
  310.2 6.9 %fusion.1 = f32[1408,1408]{1,0:T(8,128)} fusion(bf16[1408,1024]{1,0:T(8,128)(2,1)S(1)} %bitcast.281, f32[2,1408,1408]{2,1,0:T(8,128)S(1)} %bitcast.274), kind=kOutput, calls=%fused_computation.5 | convolution fusion | flops 4064051200 | bytes 21626880 | tf_op jit(solution)/shard_map/dot_general | solution.py:31
  317.0 4.8 all-to-all-start.2
  322.0 4.8 fusion.6
  330.4 69.8 %shard_map.423 = bf16[1024,1024]{1,0:T(8,128)(2,1)S(1)} custom-call(s32[1024,2]{1,0:T(8,128)S(1)} %copy-done.1, bf16[2560,1024]{1,0:T(8,128)(2,1)} %bitcast.26.back_ref), custom_call_target="tpu_custom_call" | custom-call | flops 5368709120 | bytes 209715200 | tf_op jit(solution)/shard_map/pallas_call | solution.py:476
  405.8 10.9 %fusion.37.part_ref = bf16[1024,1024]{1,0:T(8,128)(2,1)} fusion(bf16[2560,1024]{1,0:T(8,128)(2,1)} %bitcast.41, s32[1024]{0:T(1024)S(1)} %copy-done.38, s32[1024]{0:T(1024)S(1)} %copy-done.36), kind=kOutput, calls=%fused_computation.59 | convolution fusion | flops 5377622016 | bytes 7348224 | tf_op jit(solution)/shard_map/dot_general | solution.py:39
  420.0 83.4 %shard_map.424 = (bf16[1024,256]{1,0:T(8,128)(2,1)}, bf16[2,1024,256]{2,1,0:T(8,128)(2,1)}, f32[2,2,3072]{2,1,0:T(2,128)}, bf16[1024,1024]{1,0:T(8,128)(2,1)}) custom-call(bf16[1024,256]{1,0:T(8,128)(2,1)} %fusion.59.q_ref, bf16[2,2,2048,128]{3,2,1,0:T(8,128)(2,1)} %get-tuple-element.64.k_ref.v_ref, bf16[2,2,2048,128]{3,2,1,0:T(8,128)(2,1)} %get-tuple-element.64.k_ref.v_ref, ...), custom_call_target="tpu_custom_call" | custom-call | flops 21474836480 | bytes 12582912 | tf_op jit(solution)/shard_map/pallas_call | solution.py:652
  505.2 4.5 bitcast_convert_fusion
  517.3 4.1 copy.166
  521.4 5.0 reshape.336
  529.3 4.7 all-to-all-start.3
  534.6 71.5 %shard_map.425 = (f32[1024,1024]{1,0:T(8,128)}, f32[1408,1024]{1,0:T(8,128)}, bf16[1024,1024]{1,0:T(8,128)(2,1)}, f32[16,128]{1,0:T(8,128)}) custom-call(bf16[1024,1024]{1,0:T(8,128)(2,1)} %get-tuple-element.83.part_ref, f32[8,16,128]{2,1,0:T(8,128)} %bitcast.265, bf16[1408,1024]{1,0:T(8,128)(2,1)} %bitcast.282, f32[8,128]{1,0:T(8,128)} %broadcast_in_dim.85.scale_ref, ...), custom_call_target="tpu_custom_call" | custom-call | flops 28051505152 | bytes 251658240 | tf_op jit(solution)/shard_map/pallas_call | solution.py:860
  611.1 5.0 add_convert_fusion
  642.8 6.3 copy.209
  (269 shorter events, 127.3 us)
Async XLA Ops:
  7.2 48.4 %all-gather.6.cloned.1.call-start = ((), (), s32[]{:S(2)}) async-start(), calls=%async_computation.5 | async-start | bytes 1843200 | tf_op jit(solution)/shard_map/all_gather | solution.py:1115
  8.9 45.1 %collective-permute-start = (bf16[256,128]{1,0:T(8,128)(2,1)}, bf16[256,128]{1,0:T(8,128)(2,1)}, u32[]{:S(2)}, u32[]{:S(2)}) collective-permute-start(bf16[256,128]{1,0:T(8,128)(2,1)} %get-tuple-element.246), channel_id=1, source_target_pairs={{0,1},{1,2},{2,3},{3,0},{4,5},{5,6},{6,7},{7,4},{8,9},{9,10},{10,1... | collective-permute-start | bytes 196616 | tf_op jit(solution)/shard_map/ppermute | solution.py:1187
  11.9 42.9 %collective-permute-start.1 = (bf16[256,128]{1,0:T(8,128)(2,1)}, bf16[256,128]{1,0:T(8,128)(2,1)S(1)}, u32[]{:S(2)}, u32[]{:S(2)}) collective-permute-start(bf16[256,128]{1,0:T(8,128)(2,1)} %get-tuple-element.246), channel_id=1, source_target_pairs={{0,2},{1,3},{2,0},{3,1},{4,6},{5,7},{6,4},{7,5},{8,10},{9,11},{10,... | collective-permute-start | bytes 196616 | tf_op jit(solution)/shard_map/ppermute | solution.py:1187
  14.5 40.4 %collective-permute-start.2 = (bf16[256,128]{1,0:T(8,128)(2,1)}, bf16[256,128]{1,0:T(8,128)(2,1)S(1)}, u32[]{:S(2)}, u32[]{:S(2)}) collective-permute-start(bf16[256,128]{1,0:T(8,128)(2,1)} %get-tuple-element.246), channel_id=1, source_target_pairs={{0,3},{1,0},{2,1},{3,2},{4,7},{5,4},{6,5},{7,6},{8,11},{9,8},{10,9... | collective-permute-start | bytes 196616 | tf_op jit(solution)/shard_map/ppermute | solution.py:1187
  23.2 19.1 %copy-start.6 = (bf16[1024,1024]{1,0:T(8,128)(2,1)S(1)}, bf16[1024,1024]{1,0:T(8,128)(2,1)}, u32[]{:S(2)}) copy-start(bf16[1024,1024]{1,0:T(8,128)(2,1)} %param.22) | copy-start | bytes 6291460
  31.1 19.9 %copy-start = (s32[1024,2]{1,0:T(8,128)}, s32[1024,2]{1,0:T(8,128)S(1)}, u32[]{:S(2)}) copy-start(s32[1024,2]{1,0:T(8,128)S(1)} %add.178.slots_ref) | copy-start | bytes 24580
  31.6 19.3 %copy-start.35 = (s32[1024]{0:T(1024)}, s32[1024]{0:T(1024)S(1)}, u32[]{:S(2)}) copy-start(s32[1024]{0:T(1024)S(1)} %get-tuple-element.236) | copy-start | bytes 12292
  31.7 19.3 %copy-start.37 = (s32[1024]{0:T(1024)}, s32[1024]{0:T(1024)S(1)}, u32[]{:S(2)}) copy-start(s32[1024]{0:T(1024)S(1)} %get-tuple-element.237) | copy-start | bytes 12292
  35.2 17.4 %all-to-all-start = ((s32[8,1,320]{2,1,0:T(1,128)}), s32[8,1,320]{2,1,0:T(1,128)S(1)}, u32[]{:S(2)}, u32[]{:S(2)}) async-start(s32[8,1,320]{2,1,0:T(1,128)} %all_to_all.15), calls=%async_computation | async-start | bytes 24576 | tf_op jit(solution)/shard_map/all_to_all | solution.py:1064
  38.9 119.9 %all-gather.4.cloned.1.call-start = ((), (), s32[]{:S(2)}) async-start(), calls=%async_computation.4 | async-start | bytes 2359296 | tf_op jit(solution)/shard_map/all_gather | solution.py:1191
  43.4 22.3 %copy-start.24 = (f32[1024]{0:T(1024)}, f32[1024]{0:T(1024)S(1)}, u32[]{:S(2)}) copy-start(f32[1024]{0:T(1024)S(1)} %fusion.92) | copy-start | bytes 12292
  51.0 21.2 %copy-start.21 = (s32[3072]{0:T(1024)}, s32[3072]{0:T(1024)S(1)}, u32[]{:S(2)}) copy-start(s32[3072]{0:T(1024)S(1)} %pad_dynamic-slice_fusion) | copy-start | bytes 36868
  71.1 87.7 %copy-start.42 = (bf16[4,32]{1,0:T(4,128)(2,1)}, bf16[4,32]{1,0:T(4,128)(2,1)S(1)}, u32[]{:S(2)}) copy-start(bf16[4,32]{1,0:T(4,128)(2,1)S(1)} %copy.155) | copy-start | bytes 772
  245.4 71.7 %all-to-all-start.1 = ((bf16[8,320,1024]{2,1,0:T(8,128)(2,1)}), bf16[8,320,1024]{2,1,0:T(8,128)(2,1)}, u32[]{:S(2)}, u32[]{:S(2)}) async-start(bf16[8,320,1024]{2,1,0:T(8,128)(2,1)} %get-tuple-element.66), calls=%async_computation.1 | async-start | bytes 10485760 | tf_op jit(solution)/shard_map/all_to_all | solution.py:1064
  290.3 19.8 %slice-start.1 = ((s8[15859712]{0:T(1024)(128)(4,1)}), s8[4194304]{0:T(1024)(128)(4,1)S(1)}, s32[]{:S(2)}) async-start(s8[15859712]{0:T(1024)(128)(4,1)} %bitcast.273), calls=%async_computation.7 | async-start | bytes 8388608
  290.3 19.8 %slice-start.2 = ((s8[15859712]{0:T(1024)(128)(4,1)}), s8[4194304]{0:T(1024)(128)(4,1)S(1)}, s32[]{:S(2)}) async-start(s8[15859712]{0:T(1024)(128)(4,1)} %bitcast.273), calls=%async_computation.8 | async-start | bytes 8388608
  317.0 83.2 %all-to-all-start.2 = ((bf16[8,320,1024]{2,1,0:T(8,128)(2,1)}), bf16[8,320,1024]{2,1,0:T(8,128)(2,1)}, u32[]{:S(2)}, u32[]{:S(2)}) async-start(bf16[8,320,1024]{2,1,0:T(8,128)(2,1)} %bitcast.251), calls=%async_computation.2 | async-start | bytes 10485760 | tf_op jit(solution)/shard_map/all_to_all | solution.py:1064
  529.3 86.8 %all-to-all-start.3 = ((bf16[8,512,256]{2,1,0:T(8,128)(2,1)}), bf16[8,512,256]{2,1,0:T(8,128)(2,1)}, u32[]{:S(2)}, u32[]{:S(2)}) async-start(bf16[8,512,256]{2,1,0:T(8,128)(2,1)} %pad_maximum_fusion), calls=%async_computation.3 | async-start | bytes 4194304 | tf_op jit(solution)/shard_map/all_to_all | solution.py:1064
  534.5 74.1 %copy-start.44 = (f32[2,128]{1,0:T(2,128)S(1)}, f32[2,128]{1,0:T(2,128)}, u32[]{:S(2)}) copy-start(f32[2,128]{1,0:T(2,128)} %param.29) | copy-start | bytes 3076
  534.5 74.1 %copy-start.45 = (f32[2,128]{1,0:T(2,128)S(1)}, f32[2,128]{1,0:T(2,128)}, u32[]{:S(2)}) copy-start(f32[2,128]{1,0:T(2,128)} %param.42) | copy-start | bytes 3076
  534.5 75.4 %copy-start.34 = (f32[4,4]{1,0:T(4,128)S(1)}, f32[4,4]{1,0:T(4,128)}, u32[]{:S(2)}) copy-start(f32[4,4]{1,0:T(4,128)} %param.30) | copy-start | bytes 196
  534.5 75.4 %copy-start.40 = (f32[4,4]{1,0:T(4,128)S(1)}, f32[4,4]{1,0:T(4,128)}, u32[]{:S(2)}) copy-start(f32[4,4]{1,0:T(4,128)} %param.43) | copy-start | bytes 196
  534.5 76.0 %copy-start.32 = (f32[128,8]{0,1:T(8,128)S(1)}, f32[128,8]{0,1:T(8,128)}, u32[]{:S(2)}) copy-start(f32[128,8]{0,1:T(8,128)} %param.28) | copy-start | bytes 12292
  534.6 76.0 %copy-start.39 = (f32[128,8]{0,1:T(8,128)S(1)}, f32[128,8]{0,1:T(8,128)}, u32[]{:S(2)}) copy-start(f32[128,8]{0,1:T(8,128)} %param.41) | copy-start | bytes 12292
  (47 other events, 271.6 us)
Sparse Core Ops, SparseCore 0:
  20.8 24.4 all-gather.5
  55.7 28.9 all-gather.3
